TPU v7x, 128 devices: a whole 4x4x4 slice. The times are simulated.
128 devices in a mesh: lon: 16 (over x_lo, y, core), lat: 8 (over z, x_hi).
Axes of the slice: x: 4 (x_hi: 2, x_lo: 2; x = x_hi * 2 + x_lo), y: 4, z: 4, core: 2. Of those that a mesh axis runs over, the one named last changes fastest.
Arguments:
- tokens: bfloat16 [8, 192, 576, 192], P(None, 'lat', 'lon'), may hold values from -64 to 64
- cotangent: bfloat16 [8, 192, 576, 192], P(None, 'lat', 'lon'), may hold values from -6 to 6
- ln_gain: float32 [192], replicated, may hold values from 0.5 to 1.5
- qkv_weight: bfloat16 [192, 576], replicated, may hold values from -0.4375 to 0.4375
- out_weight: bfloat16 [192, 192], replicated, may hold values from -0.4375 to 0.4375
- pair_bias: float32 [6, 144, 144], replicated, may hold values from -4 to 250
Outputs:
- grad_x: bfloat16 [8, 192, 576, 192], P(None, 'lat', 'lon')
- grad_qkv: float32 [192, 576], replicated
- grad_out: float32 [192, 192], replicated
- grad_bias: float32 [6, 144, 144], replicated
- grad_gain: float32 [192], replicated
All inputs are finite; a program needn't handle non-finite values.
Results may differ from a plain program's by a relative error of at most 0.0095.
Values may be sent and summed in bfloat16 or wider, within the bound.
No kernel may reach another device: no remote copies, remote signals or barrier semaphores. Data moves between devices by JAX's collectives and lax.ppermute only.
A program may use at most 128 MiB of HBM per device.

v0:
```python
import jax
import jax.numpy as jnp
from jax import lax
from jax.sharding import PartitionSpec as P

WIN_LEV = 2
WIN_LAT = 6
WIN_LON = 12
W = 144
HALF_LAT = 3
HALF_LON = 6


def from_behind(value, axis, steps):
    count = lax.axis_size(axis)
    pairs = [(source, (source + steps) % count) for source in range(count)]
    return lax.ppermute(value, axis, pairs)


def window_grads(xwin, dywin, ln_gain, qkv_weight, out_weight, pair_bias, region):
    win_count, win_span, feature_width = xwin.shape
    head_count = pair_bias.shape[0]
    head_dim = feature_width // head_count
    score_scale = head_dim ** (-0.5)
    inputs = xwin.astype(jnp.float32)
    average = jnp.mean(inputs, axis=-1, keepdims=True)
    centred = inputs - average
    inv_std = lax.rsqrt(jnp.mean(centred * centred, axis=-1, keepdims=True) + 1e-05)
    unit_rows = centred * inv_std
    normed = (unit_rows * ln_gain).astype(jnp.bfloat16)
    flat_normed = normed.reshape(win_count * win_span, feature_width)
    packed = jnp.dot(flat_normed, qkv_weight, preferred_element_type=jnp.float32).astype(
        jnp.bfloat16
    )
    packed = packed.reshape(win_count, win_span, 3, head_count, head_dim)
    queries = packed[:, :, 0]
    key_rows = packed[:, :, 1]
    values = packed[:, :, 2]
    scores = (
        jnp.einsum("bihd,bjhd->bhij", queries, key_rows, preferred_element_type=jnp.float32)
        * score_scale
        + pair_bias[None]
    )
    same_region = region[:, None, :, None] == region[:, None, None, :]
    scores = jnp.where(same_region, scores, jnp.float32(-1e30))
    row_peak = jnp.max(scores, axis=-1, keepdims=True)
    exp_scores = jnp.exp(scores - row_peak)
    probs = exp_scores / jnp.sum(exp_scores, axis=-1, keepdims=True)
    probs_low = probs.astype(jnp.bfloat16)
    attended = jnp.einsum(
        "bhij,bjhd->bihd", probs_low, values, preferred_element_type=jnp.float32
    ).astype(jnp.bfloat16)
    flat_dy = dywin.reshape(win_count * win_span, feature_width)
    d_attended = jnp.dot(flat_dy, out_weight.T, preferred_element_type=jnp.float32).astype(
        jnp.bfloat16
    )
    d_attended = d_attended.reshape(win_count, win_span, head_count, head_dim)
    grad_out = jnp.dot(
        attended.reshape(win_count * win_span, feature_width).T,
        flat_dy,
        preferred_element_type=jnp.float32,
    )
    d_probs = jnp.einsum("bihd,bjhd->bhij", d_attended, values, preferred_element_type=jnp.float32)
    d_scores = probs * (d_probs - jnp.sum(probs * d_probs, axis=-1, keepdims=True))
    grad_bias = jnp.sum(d_scores, axis=0)
    d_scores_low = d_scores.astype(jnp.bfloat16)
    d_queries = (
        jnp.einsum("bhij,bjhd->bihd", d_scores_low, key_rows, preferred_element_type=jnp.float32)
        * score_scale
    )
    d_keys = (
        jnp.einsum("bhij,bihd->bjhd", d_scores_low, queries, preferred_element_type=jnp.float32)
        * score_scale
    )
    d_values = jnp.einsum(
        "bhij,bihd->bjhd", probs_low, d_attended, preferred_element_type=jnp.float32
    )
    d_packed = jnp.stack([d_queries, d_keys, d_values], axis=2).astype(jnp.bfloat16)
    d_packed = d_packed.reshape(win_count * win_span, 3 * feature_width)
    grad_qkv = jnp.dot(flat_normed.T, d_packed, preferred_element_type=jnp.float32)
    d_normed = jnp.dot(d_packed, qkv_weight.T, preferred_element_type=jnp.float32)
    d_normed = d_normed.reshape(win_count, win_span, feature_width)
    grad_gain = jnp.sum(d_normed * unit_rows, axis=(0, 1))
    d_unit = d_normed * ln_gain
    d_inputs = inv_std * (
        d_unit
        - jnp.mean(d_unit, axis=-1, keepdims=True)
        - unit_rows * jnp.mean(d_unit * unit_rows, axis=-1, keepdims=True)
    )
    d_tokens = (dywin.astype(jnp.float32) + d_inputs).astype(jnp.bfloat16)
    return (d_tokens, (grad_qkv, grad_out, grad_bias, grad_gain))


def to_windows(field):
    levels, lat_rows, lon_cols, channels = field.shape
    shaped = field.reshape(
        levels // WIN_LEV,
        WIN_LEV,
        lat_rows // WIN_LAT,
        WIN_LAT,
        lon_cols // WIN_LON,
        WIN_LON,
        channels,
    )
    shaped = shaped.transpose(0, 2, 4, 1, 3, 5, 6)
    return shaped.reshape(
        levels // WIN_LEV * (lat_rows // WIN_LAT), lon_cols // WIN_LON, W, channels
    )


def from_windows(blocks, levels, lat_rows, lon_cols):
    channels = blocks.shape[-1]
    shaped = blocks.reshape(
        levels // WIN_LEV,
        lat_rows // WIN_LAT,
        lon_cols // WIN_LON,
        WIN_LEV,
        WIN_LAT,
        WIN_LON,
        channels,
    )
    shaped = shaped.transpose(0, 3, 1, 4, 2, 5, 6)
    return shaped.reshape(levels, lat_rows, lon_cols, channels)


def local(tokens, cotangent, ln_gain, qkv_weight, out_weight, pair_bias):
    levels, lat_rows, lon_cols, feature_width = tokens.shape
    lon_recv = from_behind((tokens[:, :, :HALF_LON], cotangent[:, :, :HALF_LON]), "lon", -1)
    lon_tokens = jnp.concatenate([tokens[:, :, HALF_LON:], lon_recv[0]], axis=2)
    lon_cot = jnp.concatenate([cotangent[:, :, HALF_LON:], lon_recv[1]], axis=2)
    lat_recv = from_behind((lon_tokens[:, :HALF_LAT], lon_cot[:, :HALF_LAT]), "lat", -1)
    rolled = jnp.concatenate([lon_tokens[:, HALF_LAT:], lat_recv[0]], axis=1)
    rolled_cot = jnp.concatenate([lon_cot[:, HALF_LAT:], lat_recv[1]], axis=1)
    lat_total = lat_rows * lax.axis_size("lat")
    global_rows = lax.axis_index("lat") * lat_rows + jnp.arange(lat_rows, dtype=jnp.int32)
    region_rows = (global_rows >= lat_total - HALF_LAT).astype(jnp.int32)
    region = jnp.broadcast_to(region_rows[None, :, None, None], (levels, lat_rows, lon_cols, 1))
    x_blocks = to_windows(rolled)
    dy_blocks = to_windows(rolled_cot)
    region_blocks = to_windows(region)[..., 0]

    def window_step(carries, pieces):
        d_tokens, grads = window_grads(
            pieces[0], pieces[1], ln_gain, qkv_weight, out_weight, pair_bias, pieces[2]
        )
        return (tuple((c + g for c, g in zip(carries, grads))), d_tokens)

    zeros_init = (
        jnp.zeros((feature_width, 3 * feature_width), jnp.float32),
        jnp.zeros((feature_width, feature_width), jnp.float32),
        jnp.zeros(pair_bias.shape, jnp.float32),
        jnp.zeros((feature_width,), jnp.float32),
    )
    partial_grads, d_blocks = lax.scan(
        window_step, zeros_init, (x_blocks, dy_blocks, region_blocks)
    )
    d_rolled = from_windows(d_blocks, levels, lat_rows, lon_cols)
    lat_back = from_behind(d_rolled[:, lat_rows - HALF_LAT :], "lat", 1)
    lat_fixed = jnp.concatenate([lat_back, d_rolled[:, : lat_rows - HALF_LAT]], axis=1)
    lon_back = from_behind(lat_fixed[:, :, lon_cols - HALF_LON :], "lon", 1)
    grad_x = jnp.concatenate([lon_back, lat_fixed[:, :, : lon_cols - HALF_LON]], axis=2)
    totals = lax.psum(
        (partial_grads[0], partial_grads[1], partial_grads[2], partial_grads[3]), ("lon", "lat")
    )
    factor = float(levels * lat_total * lon_cols * lax.axis_size("lon")) ** (-0.5)
    return (grad_x, totals[0] * factor, totals[1] * factor, totals[2], totals[3] * factor)


def solution(mesh):
    placed = (P(None, "lat", "lon", None), P(None, "lat", "lon", None), P(), P(), P(), P())
    return jax.shard_map(
        local,
        mesh=mesh,
        in_specs=placed,
        out_specs=(P(None, "lat", "lon", None), P(), P(), P(), P()),
        check_vma=False,
    )
```

profile of v0, /device:TPU:0, one launch (start us, length us, event | category | flops | bytes accessed | tf_op | source)
XLA Modules:
  0.0 762.0 jit_solution(4362381603460581107)
XLA Ops:
  8.6 3.5 collective-permute-start
  15.8 3.7 collective-permute-done
  20.4 6.2 collective-permute-start.1
  30.2 10.3 %collective-permute-start.3 = (bf16[8,3,36,192]{3,0,2,1:T(8,128)(2,1)}, bf16[8,3,36,192]{3,0,2,1:T(8,128)(2,1)}, u32[]{:S(2)}, u32[]{:S(2)}) collective-permute-start(bf16[8,3,36,192]{3,0,2,1:T(8,128)(2,1)} %slice.66), channel_id=1, source_target_pairs={{0,7},{1,0},{2,1},{3,2},{4,3},{5,4},{6,5},{7,6},{8,15},{9,8},{10,9... | collective-permute-start | bytes 995336 | tf_op jit(solution)/shard_map/ppermute | solution.py:17
  50.3 3.7 reshape.141
  54.0 5.3 copy.80
  59.3 7.3 reshape.156
  69.2 3.7 reshape.143
  72.9 5.3 copy.81
  78.2 7.3 reshape.157
  86.2 505.2 %while.19 = (s32[]{:T(128)}, f32[192,576]{1,0:T(8,128)}, f32[192,192]{1,0:T(8,128)}, f32[6,144,144]{1,2,0:T(8,128)}, f32[192]{0:T(256)S(1)}, /*index=5*/bf16[16,...) while((s32[]{:T(128)}, f32[192,576]{1,0:T(8,128)}, ...), condition=%wide.region_10.11_spmd.clone, body=%wide.region_0.10_spmd.clone.sunk | while | flops 504737760 | bytes 43340216 | solution.py:154
  110.8 2.6 multiply_reduce_fusion.10
  142.3 2.6 multiply_reduce_fusion.10
  173.9 2.6 multiply_reduce_fusion.10
  205.5 2.6 multiply_reduce_fusion.10
  237.1 2.6 multiply_reduce_fusion.10
  268.7 2.6 multiply_reduce_fusion.10
  300.3 2.6 multiply_reduce_fusion.10
  331.8 2.6 multiply_reduce_fusion.10
  363.4 2.6 multiply_reduce_fusion.10
  395.0 2.6 multiply_reduce_fusion.10
  426.6 2.6 multiply_reduce_fusion.10
  458.2 2.6 multiply_reduce_fusion.10
  489.7 2.6 multiply_reduce_fusion.10
  521.3 2.6 multiply_reduce_fusion.10
  594.0 3.3 copy.71
  597.3 3.2 reshape.145
  600.5 7.4 copy.72
  607.9 7.1 reshape.146
  619.1 67.9 %psum.31 = f32[192]{0:T(256)S(1)} all-reduce(f32[192]{0:T(256)S(1)} %copy-done.16), channel_id=1, replica_groups=mesh['lon'=16,'lat'=8] {'lon','lat'}, use_global_device_ids=true, to_apply=%region_14.15 | all-reduce | flops 192 | bytes 1536 | tf_op jit(solution)/shard_map/psum | solution.py:162
  689.4 55.4 %all-reduce.3.cloned.1.call-done = (f32[192,576]{1,0:T(8,128)}, f32[192,192]{1,0:T(8,128)}, f32[6,144,144]{2,1,0:T(8,128)}) async-done(((f32[192,576]{1,0:T(8,128)}, f32[192,192]{1,0:T(8,128)}, f32[6,144,144]{2,1,0:T(8,128)}), (f32[192,576]{1,0:T(8,128)}, f32[192,192]{1,0:T(8,128)}, f32[6,144,144]{2,1,0:T(8,128)})) %all-reduce.3.cloned.1.call-update) | async-done | bytes 1087504 | tf_op jit(solution)/shard_map/psum | solution.py:162
  750.4 3.8 copy.74
  (930 shorter events, 502.2 us)
Async XLA Ops:
  7.2 4.9 slice-start
  7.2 737.6 %all-reduce.3.cloned.1.call-start = ((), (), s32[]{:S(2)}) async-start(), calls=%async_computation | async-start | bytes 3145728 | tf_op jit(solution)/shard_map/psum | solution.py:162
  8.6 10.9 %collective-permute-start = (bf16[8,24,6,192]{3,0,2,1:T(8,128)(2,1)S(1)}, bf16[8,24,6,192]{3,0,2,1:T(8,128)(2,1)S(1)}, u32[]{:S(2)}, u32[]{:S(2)}) collective-permute-start(bf16[8,24,6,192]{3,0,2,1:T(8,128)(2,1)S(1)} %copy.88), channel_id=1, source_target_pairs={{0,120},{8,0},{16,8},{24,16},{32,24},{40,32},{48,40},{56,48},{64,5... | collective-permute-start | bytes 1327112 | tf_op jit(solution)/shard_map/ppermute | solution.py:17
  12.3 15.3 %collective-permute-start.2 = (bf16[8,24,6,192]{3,0,2,1:T(8,128)(2,1)S(1)}, bf16[8,24,6,192]{3,0,2,1:T(8,128)(2,1)S(1)}, u32[]{:S(2)}, u32[]{:S(2)}) collective-permute-start(bf16[8,24,6,192]{3,0,2,1:T(8,128)(2,1)S(1)} %copy.90), channel_id=1, source_target_pairs={{0,120},{8,0},{16,8},{24,16},{32,24},{40,32},{48,40},{56,48},{64,5... | collective-permute-start | bytes 1327112 | tf_op jit(solution)/shard_map/ppermute | solution.py:17
  14.9 11.7 %slice-start.1 = ((bf16[8,24,36,192]{3,1,2,0:T(8,128)(2,1)}), bf16[8,24,30,192]{3,1,2,0:T(8,128)(2,1)S(1)}, s32[]{:S(2)}) async-start(bf16[8,24,36,192]{3,1,2,0:T(8,128)(2,1)} %param.9), calls=%async_computation.2 | async-start | bytes 5898240 | tf_op jit(solution)/shard_map/slice | solution.py:130
  20.4 28.3 %collective-permute-start.1 = (bf16[8,3,36,192]{3,0,2,1:T(8,128)(2,1)}, bf16[8,3,36,192]{3,0,2,1:T(8,128)(2,1)}, u32[]{:S(2)}, u32[]{:S(2)}) collective-permute-start(bf16[8,3,36,192]{3,0,2,1:T(8,128)(2,1)} %slice.64), channel_id=1, source_target_pairs={{0,7},{1,0},{2,1},{3,2},{4,3},{5,4},{6,5},{7,6},{8,15},{9,8},{10,9... | collective-permute-start | bytes 995336 | tf_op jit(solution)/shard_map/ppermute | solution.py:17
  30.2 36.4 %collective-permute-start.3 = (bf16[8,3,36,192]{3,0,2,1:T(8,128)(2,1)}, bf16[8,3,36,192]{3,0,2,1:T(8,128)(2,1)}, u32[]{:S(2)}, u32[]{:S(2)}) collective-permute-start(bf16[8,3,36,192]{3,0,2,1:T(8,128)(2,1)} %slice.66), channel_id=1, source_target_pairs={{0,7},{1,0},{2,1},{3,2},{4,3},{5,4},{6,5},{7,6},{8,15},{9,8},{10,9... | collective-permute-start | bytes 995336 | tf_op jit(solution)/shard_map/ppermute | solution.py:17
  78.2 7.9 %copy-start.13 = (f32[192]{0:T(256)S(1)}, f32[192]{0:T(256)}, u32[]{:S(2)}) copy-start(f32[192]{0:T(256)} %param.10) | copy-start | bytes 2308
  78.2 7.9 %copy-start.14 = (f32[192]{0:T(256)S(1)}, f32[192]{0:T(256)}, u32[]{:S(2)}) copy-start(f32[192]{0:T(256)} %custom-call.3) | copy-start | bytes 2308
  110.7 4.2 copy-start.1
  110.7 4.1 copy-start.5
  142.3 4.2 copy-start.1
  142.3 4.1 copy-start.5
  173.8 4.2 copy-start.1
  173.9 4.1 copy-start.5
  205.4 4.2 copy-start.1
  205.5 4.1 copy-start.5
  237.0 4.2 copy-start.1
  237.1 4.1 copy-start.5
  268.6 4.2 copy-start.1
  300.2 4.2 copy-start.1
  331.7 4.2 copy-start.1
  363.3 4.2 copy-start.1
  394.9 4.2 copy-start.1
  426.5 4.2 copy-start.1
  458.1 4.2 copy-start.1
  489.6 4.2 copy-start.1
  521.2 4.2 copy-start.1
  552.8 4.2 copy-start.1
  584.4 4.2 copy-start.1
  617.0 70.6 %collective-permute-start.4 = (bf16[8,3,36,192]{3,0,2,1:T(8,128)(2,1)}, bf16[8,3,36,192]{3,0,2,1:T(8,128)(2,1)}, u32[]{:S(2)}, u32[]{:S(2)}) collective-permute-start(bf16[8,3,36,192]{3,0,2,1:T(8,128)(2,1)} %slice.67), channel_id=1, source_target_pairs={{0,1},{1,2},{2,3},{3,4},{4,5},{5,6},{6,7},{7,0},{8,9},{9,10},{10,1... | collective-permute-start | bytes 995336 | tf_op jit(solution)/shard_map/ppermute | solution.py:17
  689.4 58.9 %collective-permute-start.5 = (bf16[8,24,6,192]{3,0,2,1:T(8,128)(2,1)}, bf16[8,24,6,192]{3,0,2,1:T(8,128)(2,1)}, u32[]{:S(2)}, u32[]{:S(2)}) collective-permute-start(bf16[8,24,6,192]{3,0,2,1:T(8,128)(2,1)} %pad_maximum_fusion.3), channel_id=1, source_target_pairs={{0,8},{8,16},{16,24},{24,32},{32,40},{40,48},{48,56},{56,64},{64,7... | collective-permute-start | bytes 1327112 | tf_op jit(solution)/shard_map/ppermute | solution.py:17
  (130 other events, 251.4 us)
Sparse Core Ops, SparseCore 0:
  594.1 150.6 all-reduce.2
where the time goes:
time: 770 us; the launch traced here: 762 us
  matrix products  230 us (30%)
  local copies, waits for them, and re-layouts  211 us (27%)
  other arithmetic  156 us (20%)
  blocking collectives  67.9 us (9%)
  waiting for transfers between devices  59.1 us (8%)
  starting transfers between devices  20.8 us (3%)
  between operations  14.2 us (2%)
    psum x1, blocking collectives, local(): lax.psum((partial_grads[0], partial_grads[1], partial_grads[2], partial_g...  67.9 us
    psum x1, waiting for transfers between devices, local(): lax.psum((partial_grads[0], partial_grads[1], partial_grads[2], partial_g...  55.4 us
    dot_general x16, matrix products, window_grads(): jnp.dot(d_packed, qkv_weight.T, preferred_element_type=jnp.float32)  42.3 us
    sub x16, matrix products, window_grads(): exp_scores = jnp.exp(scores - row_peak)  42.1 us
    unnamed x27, local copies, waits for them, and re-layouts  39.4 us
    dynamic_update_slice x16, other arithmetic, local(): lax.scan(window_step, zeros_init, (x_blocks, dy_blocks, region_blocks))  37.6 us
    convert_element_type x32, other arithmetic, window_grads(): normed = (unit_rows * ln_gain).astype(jnp.bfloat16)  35.8 us
    dot_general x16, matrix products, window_grads(): jnp.dot(attended.reshape(win_count * win_span, feature_width).T, flat_dy,...  30.5 us
  transfers between devices with their start and end apart: 7, of which 2 were waited for; matrix products, arithmetic and copies ran while one was open for 8% of the time, Pallas kernels for 0%

commit v1 on v0

v1 whole, which is shorter than its diff:
```python
import jax
import jax.numpy as jnp
from jax import lax
from jax.experimental import pallas as pl
from jax.experimental.pallas import tpu as pltpu
from jax.sharding import PartitionSpec as P

WIN_LEV = 2
WIN_LAT = 6
WIN_LON = 12
W = 144
HEADS = 6
HEAD = 32
D = 192
HALF_LAT = 3
HALF_LON = 6
LANES = 896
LOG2E = 1.4426950408889634
SCALE = HEAD**-0.5
F32 = jnp.float32
BF16 = jnp.bfloat16
WROWS = 6 * D
BROWS = 7 * W
ROWS = 2176

NN = (((1,), (0,)), ((), ()))
NT = (((1,), (1,)), ((), ()))
TN = (((0,), (0,)), ((), ()))


def mm(a, b, dims):
    return lax.dot_general(a, b, dims, preferred_element_type=F32)


def spread(rows16):
    head_of = lax.broadcasted_iota(jnp.int32, (1, D), 1) // HEAD
    main = rows16[:128]
    rest = rows16[128:]
    zero_main = jnp.zeros_like(main)
    zero_rest = jnp.zeros_like(rest)
    parts = []
    for pair in range(3):
        parts.append(
            jnp.concatenate(
                [jnp.where(head_of == 2 * pair + n, main, zero_main) for n in range(2)], axis=0
            )
        )
    parts.append(
        jnp.concatenate(
            [jnp.where(head_of == h, rest, zero_rest) for h in range(HEADS)]
            + [zero_rest, zero_rest],
            axis=0,
        )
    )
    return parts


def fold_rest(rest):
    head_of = lax.broadcasted_iota(jnp.int32, (1, D), 1) // HEAD
    total = rest[:16]
    for h in range(1, HEADS):
        total = jnp.where(head_of == h, rest[16 * h : 16 * h + 16], total)
    return total


def attention_window(q, k, v, da, bias_ref, gb_ref):
    qm = spread(q)
    dam = spread(da)
    kt = k.T
    vt = v.T
    dk = None
    dv = None
    a_rows = []
    dq_rows = []
    for c in range(4):
        lo = 256 * c
        width = 256 if c < 3 else 128
        s = mm(k, qm[c], NT) * (SCALE * LOG2E) + bias_ref[:, lo : lo + width]
        dp = mm(v, dam[c], NT)
        e = jnp.exp2(s - jnp.max(s, axis=0, keepdims=True))
        p = e * (1.0 / jnp.sum(e, axis=0, keepdims=True))
        ds = p * (dp - jnp.sum(p * dp, axis=0, keepdims=True))
        gb_ref[:, lo : lo + width] += ds
        pb = p.astype(BF16)
        dsb = ds.astype(BF16)
        dvc = mm(pb, dam[c], NN)
        dkc = mm(dsb, qm[c], NN)
        dv = dvc if dv is None else dv + dvc
        dk = dkc if dk is None else dk + dkc
        if c < 3:
            at = mm(vt[64 * c : 64 * c + 64], pb, NN)
            dqt = mm(kt[64 * c : 64 * c + 64], dsb, NN)
            a_rows += [at[:32, :128], at[32:, 128:]]
            dq_rows += [dqt[:32, :128], dqt[32:, 128:]]
        else:
            a_rest = fold_rest(mm(pb, v, TN))
            dq_rest = fold_rest(mm(dsb, k, TN))
    a = jnp.concatenate([jnp.concatenate(a_rows, axis=0).T, a_rest], axis=0).astype(BF16)
    dq = jnp.concatenate([jnp.concatenate(dq_rows, axis=0).T, dq_rest], axis=0)
    return a, (dq * SCALE).astype(BF16), (dk * SCALE).astype(BF16), dv.astype(BF16)


def windows_backward(x, dy, gain, wqkv_ref, wout_ref, bias_ref, gw_ref, gb_ref):
    count = x.shape[0] // W
    mean = jnp.mean(x, axis=-1, keepdims=True)
    centred = x - mean
    inv_std = lax.rsqrt(jnp.mean(centred * centred, axis=-1, keepdims=True) + 1e-05)
    unit = centred * inv_std
    normed = (unit * gain).astype(BF16)
    dyb = dy.astype(BF16)
    packed = mm(normed, wqkv_ref[...], NN).astype(BF16)
    datt = mm(dyb, wout_ref[...], NT).astype(BF16)
    grads = None
    parts = []
    for w in range(count):
        rows = slice(W * w, W * w + W)
        a, dq, dk, dv = attention_window(
            packed[rows, 0:192],
            packed[rows, 256:448],
            packed[rows, 512:704],
            datt[rows],
            bias_ref,
            gb_ref,
        )
        parts.append((a, dq, dk, dv))
    a, dq, dk, dv = (jnp.concatenate([p[n] for p in parts], axis=0) for n in range(4))
    gw_ref[0] += mm(normed, dq, TN)
    gw_ref[1] += mm(normed, dk, TN)
    gw_ref[2] += mm(normed, dv, TN)
    gw_ref[3] += mm(a, dyb, TN)
    dn = (
        mm(dq, wqkv_ref[:, 0:192], NT)
        + mm(dk, wqkv_ref[:, 256:448], NT)
        + mm(dv, wqkv_ref[:, 512:704], NT)
    )
    du = dn * gain
    dx = inv_std * (
        du
        - jnp.mean(du, axis=-1, keepdims=True)
        - unit * jnp.mean(du * unit, axis=-1, keepdims=True)
    )
    return dy + dx


def start_sums(first, gw_ref, gb_ref, gw_in, gb_in):
    @pl.when(first)
    def _():
        if gw_in is None:
            gw_ref[...] = jnp.zeros_like(gw_ref)
            gb_ref[...] = jnp.zeros_like(gb_ref)
        else:
            gw_ref[...] = gw_in[...]
            gb_ref[...] = gb_in[...]


def lat_rows(refs, levels):
    return [(refs[n // 3], lv, n % 3) for lv in levels for n in range(WIN_LAT)]


def inner_kernel(xt, xu, yt, yu, gain, wqkv, wout, bias, dx_ref, gw_ref, gb_ref):
    first = (pl.program_id(0) == 0) & (pl.program_id(1) == 0)
    start_sums(first, gw_ref, gb_ref, None, None)

    def load(refs):
        rows = [r[lv, la].astype(F32) for r, lv, la in lat_rows(refs, (0, 1))]
        return jnp.concatenate(
            [row[6 + 12 * n : 18 + 12 * n] for n in range(2) for row in rows], axis=0
        )

    out = windows_backward(
        load((xt, xu)), load((yt, yu)), gain[...], wqkv, wout, bias, gw_ref, gb_ref
    )
    for n in range(12):
        row = jnp.concatenate([out[12 * n : 12 * n + 12], out[W + 12 * n : W + 12 * n + 12]], axis=0)
        dx_ref[n // 6, n % 6] = row.astype(BF16)


def east_kernel(
    xt, xu, yt, yu, ext, exu, eyt, eyu, gain, wqkv, wout, bias, gw_in, gb_in, dx_ref, gw_ref, gb_ref
):
    first = (pl.program_id(0) == 0) & (pl.program_id(1) == 0)
    start_sums(first, gw_ref, gb_ref, gw_in, gb_in)

    def load(refs, east):
        pieces = []
        for (r, lv, la), (e, _, _) in zip(
            lat_rows(refs, range(4)), lat_rows(east, range(4))
        ):
            pieces += [r[lv, la].astype(F32)[30:36], e[lv, la].astype(F32)]
        return jnp.concatenate(pieces, axis=0)

    out = windows_backward(
        load((xt, xu), (ext, exu)),
        load((yt, yu), (eyt, eyu)),
        gain[...],
        wqkv,
        wout,
        bias,
        gw_ref,
        gb_ref,
    )
    for n in range(24):
        dx_ref[n // 6, n % 6] = out[12 * n : 12 * n + 12].astype(BF16)


def south_kernel(
    xt, xs, yt, ys, ext, exs, eyt, eys, gain, wqkv, wout, bias, gw_in, gb_in, dx_ref, sum_ref, gw_ref, gb_ref
):
    first = pl.program_id(0) == 0
    start_sums(first, gw_ref, gb_ref, gw_in, gb_in)

    def load(refs, east):
        rows = [r[lv, la].astype(F32) for r, lv, la in lat_rows(refs, (0, 1))]
        erows = [r[lv, la].astype(F32) for r, lv, la in lat_rows(east, (0, 1))]
        pieces = [row[6 + 12 * n : 18 + 12 * n] for n in range(2) for row in rows]
        for row, erow in zip(rows, erows):
            pieces += [row[30:36], erow]
        return jnp.concatenate(pieces, axis=0)

    out = windows_backward(
        load((xt, xs), (ext, exs)),
        load((yt, ys), (eyt, eys)),
        gain[...],
        wqkv,
        wout,
        bias,
        gw_ref,
        gb_ref,
    )
    for n in range(12):
        row = jnp.concatenate(
            [out[W * k + 12 * n : W * k + 12 * n + 12] for k in range(3)], axis=0
        )
        dx_ref[n // 6, n % 6] = row.astype(BF16)

    @pl.when(pl.program_id(0) == pl.num_programs(0) - 1)
    def _():
        whole = jnp.concatenate([gw_ref[n] for n in range(4)], axis=1)
        for t in range(6):
            sum_ref[D * t : D * t + D] = whole[:, 128 * t : 128 * t + 128]
        for t in range(7):
            sum_ref[WROWS + W * t : WROWS + W * t + W] = gb_ref[:, 128 * t : 128 * t + 128]
        sum_ref[WROWS + BROWS :] = jnp.zeros((ROWS - WROWS - BROWS, 128), F32)


def whole(shape):
    return pl.BlockSpec(shape, lambda *_: (0,) * len(shape))


PARAMS = pltpu.CompilerParams(vmem_limit_bytes=56 * 1024 * 1024)
GW = (4, D, D)
GB = (W, LANES)


def cost(count):
    return pl.CostEstimate(
        flops=count * 144 * 192 * 192 * 40, bytes_accessed=count * 144 * 192 * 6, transcendentals=0
    )


def const_specs():
    return [whole((1, D)), whole((D, 768)), whole((D, D)), whole((W, LANES))]


def inner_windows(x, y, consts):
    levels = x.shape[0]

    def rows(shift):
        return pl.BlockSpec((2, 3, 36, D), lambda i, b: (i, 2 * b + shift, 0, 0))

    return pl.pallas_call(
        inner_kernel,
        grid=(levels // 2, 3),
        in_specs=[rows(1), rows(2), rows(1), rows(2)] + const_specs(),
        out_specs=[pl.BlockSpec((2, 6, 24, D), lambda i, b: (i, b, 0, 0)), whole(GW), whole(GB)],
        out_shape=[
            jax.ShapeDtypeStruct((levels, 18, 24, D), BF16),
            jax.ShapeDtypeStruct(GW, F32),
            jax.ShapeDtypeStruct(GB, F32),
        ],
        compiler_params=PARAMS,
        cost_estimate=cost(24),
        name="inner_windows",
    )(x, x, y, y, *consts)


def east_windows(x, y, ex, ey, consts, sums):
    levels = x.shape[0]

    def rows(shift, lon):
        return pl.BlockSpec((4, 3, lon, D), lambda i, b: (i, 2 * b + shift, 0, 0))

    return pl.pallas_call(
        east_kernel,
        grid=(levels // 4, 3),
        in_specs=[rows(1, 36), rows(2, 36), rows(1, 36), rows(2, 36)]
        + [rows(1, 6), rows(2, 6), rows(1, 6), rows(2, 6)]
        + const_specs()
        + [whole(GW), whole(GB)],
        out_specs=[pl.BlockSpec((4, 6, 12, D), lambda i, b: (i, b, 0, 0)), whole(GW), whole(GB)],
        out_shape=[
            jax.ShapeDtypeStruct((levels, 18, 12, D), BF16),
            jax.ShapeDtypeStruct(GW, F32),
            jax.ShapeDtypeStruct(GB, F32),
        ],
        compiler_params=PARAMS,
        cost_estimate=cost(12),
        name="east_windows",
    )(x, x, y, y, ex, ex, ey, ey, *consts, *sums)


def south_windows(x, y, sx, sy, ex, ey, cx, cy, consts, sums):
    levels = x.shape[0]

    def rows(block, lon):
        return pl.BlockSpec((2, 3, lon, D), lambda i: (i, block, 0, 0))

    return pl.pallas_call(
        south_kernel,
        grid=(levels // 2,),
        in_specs=[rows(7, 36), rows(0, 36), rows(7, 36), rows(0, 36)]
        + [rows(7, 6), rows(0, 6), rows(7, 6), rows(0, 6)]
        + const_specs()
        + [whole(GW), whole(GB)],
        out_specs=[pl.BlockSpec((2, 6, 36, D), lambda i: (i, 0, 0, 0)), whole((ROWS, 128))],
        out_shape=[
            jax.ShapeDtypeStruct((levels, 6, 36, D), BF16),
            jax.ShapeDtypeStruct((ROWS, 128), F32),
        ],
        scratch_shapes=[pltpu.VMEM(GW, F32), pltpu.VMEM(GB, F32)],
        compiler_params=PARAMS,
        cost_estimate=cost(12),
        name="south_windows",
    )(x, sx, y, sy, ex, cx, ey, cy, *consts, *sums)


def finish_kernel(factor, sum_ref, gain_ref, w_ref, gq_ref, go_ref, gb_ref, gg_ref):
    both = jnp.concatenate(
        [sum_ref[D * t : D * t + D].astype(F32) for t in range(6)], axis=1
    )
    gq = both[:, : 3 * D] * factor
    gq_ref[...] = gq
    go_ref[...] = both[:, 3 * D :] * factor
    gg_ref[...] = jnp.sum(gq * w_ref[...].astype(F32), axis=1, keepdims=True) / gain_ref[...]
    base = WROWS + 6 * W
    rest = sum_ref[base : base + W].astype(F32).T
    for h in range(HEADS):
        main = sum_ref[WROWS + W * h : WROWS + W * h + W].astype(F32).T
        gb_ref[h, :128] = main
        gb_ref[h, 128:] = rest[16 * h : 16 * h + 16]


def finish(sums, gain_col, qkv_weight, factor):
    return pl.pallas_call(
        lambda *refs: finish_kernel(factor, *refs),
        out_shape=[
            jax.ShapeDtypeStruct((D, 3 * D), F32),
            jax.ShapeDtypeStruct((D, D), F32),
            jax.ShapeDtypeStruct((HEADS, W, W), F32),
            jax.ShapeDtypeStruct((D, 1), F32),
        ],
        compiler_params=PARAMS,
        name="finish_sums",
    )(sums, gain_col, qkv_weight)


def score_lanes(bias):
    turned = jnp.transpose(bias, (2, 0, 1))
    return jnp.concatenate(
        [
            turned[:, :, :128].reshape(W, HEADS * 128),
            turned[:, :, 128:].reshape(W, HEADS * 16),
            jnp.zeros((W, 32), F32),
        ],
        axis=1,
    )


def make_consts(ln_gain, qkv_weight, out_weight, pair_bias):
    wqkv = jnp.pad(qkv_weight.reshape(D, 3, D), ((0, 0), (0, 0), (0, 64))).reshape(D, 768)
    bias = score_lanes(pair_bias) * LOG2E
    return [ln_gain.reshape(1, D), wqkv, out_weight, bias]


def shift(value, axes, steps):
    sizes = [lax.axis_size(a) for a in axes]
    total = 1
    for s in sizes:
        total *= s
    pairs = []
    for source in range(total):
        rest, place = source, []
        for s in reversed(sizes):
            place.append(rest % s)
            rest //= s
        place.reverse()
        target = 0
        for p, s, d in zip(place, sizes, steps):
            target = target * s + (p + d) % s
        pairs.append((source, target))
    return lax.ppermute(value, axes if len(axes) > 1 else axes[0], pairs)


def moved(value, axis, to_of):
    count = lax.axis_size(axis)
    return lax.ppermute(value, axis, [(n, to_of(n)) for n in range(count)])


def flip(value, axis, bits):
    return moved(value, axis, lambda n: n ^ bits)


def lon_core(n):
    return n % 2


def sum_over_devices(sums):
    lon = lax.axis_index("lon")
    core = lon % 2
    y = (lon // 2) % 4
    halves = sums.reshape(2, ROWS // 2, 128)
    low = halves.astype(BF16)
    got = flip(lax.dynamic_index_in_dim(low, 1 - core, 0, keepdims=False), "lon", 1)
    mine = lax.dynamic_index_in_dim(halves, core, 0, keepdims=False) + got.astype(F32)
    quarters = mine.reshape(4, ROWS // 8, 128)
    qlow = quarters.astype(BF16)
    total = lax.dynamic_index_in_dim(quarters, y, 0, keepdims=False)
    for step in range(1, 4):
        piece = lax.dynamic_index_in_dim(qlow, y ^ step, 0, keepdims=False)
        total = total + flip(piece, "lon", 2 * step).astype(F32)
    low = total.astype(BF16)
    for step in range(1, 4):
        total = total + flip(low, "lat", 2 * step).astype(F32)
    low = total.astype(BF16)
    total = (
        total
        + flip(low, "lat", 1).astype(F32)
        + flip(low, "lon", 8).astype(F32)
        + shift_x(low).astype(F32)
    )
    low = total.astype(BF16)
    others = [low] + [flip(low, "lon", 2 * step) for step in range(1, 4)]
    stacked = jnp.stack(others)
    line = jnp.concatenate(
        [lax.dynamic_index_in_dim(stacked, y ^ n, 0, keepdims=True) for n in range(4)], axis=0
    )
    other = flip(line, "lon", 1)
    pair = jnp.stack([line, other])
    return jnp.concatenate(
        [
            lax.dynamic_index_in_dim(pair, core ^ n, 0, keepdims=False).reshape(ROWS // 2, 128)
            for n in range(2)
        ],
        axis=0,
    )


def shift_x(value):
    lat = lax.axis_size("lat")
    total = lax.axis_size("lon") * lat
    pairs = []
    for source in range(total):
        lon_at, lat_at = source // lat, source % lat
        pairs.append((source, (lon_at ^ 8) * lat + (lat_at ^ 1)))
    return lax.ppermute(value, ("lon", "lat"), pairs)


def local(tokens, cotangent, ln_gain, qkv_weight, out_weight, pair_bias):
    levels, lat_count, lon_count, _ = tokens.shape
    ex = shift(tokens[:, :, :HALF_LON], ("lon",), (-1,))
    ey = shift(cotangent[:, :, :HALF_LON], ("lon",), (-1,))
    sx = shift(tokens[:, :HALF_LAT], ("lat",), (-1,))
    sy = shift(cotangent[:, :HALF_LAT], ("lat",), (-1,))
    cx = shift(tokens[:, :HALF_LAT, :HALF_LON], ("lon", "lat"), (-1, -1))
    cy = shift(cotangent[:, :HALF_LAT, :HALF_LON], ("lon", "lat"), (-1, -1))
    consts = make_consts(ln_gain, qkv_weight, out_weight, pair_bias)
    last = lax.axis_index("lat") == lax.axis_size("lat") - 1
    region = (jnp.arange(W) // WIN_LON) % WIN_LAT >= HALF_LAT
    apart = jnp.broadcast_to(region[:, None] != region[None, :], (HEADS, W, W))
    masked = jnp.where(apart & last, F32(-1e30), pair_bias)
    edge_consts = consts[:3] + [score_lanes(masked) * LOG2E]
    inner, gw, gb = inner_windows(tokens, cotangent, consts)
    east, gw, gb = east_windows(tokens, cotangent, ex, ey, consts, (gw, gb))
    south, sums = south_windows(
        tokens, cotangent, sx, sy, ex, ey, cx, cy, edge_consts, (gw, gb)
    )
    back_lon = jnp.concatenate([east[:, :, HALF_LON:], south[:, :HALF_LAT, 30:]], axis=1)
    got_lon = shift(back_lon, ("lon",), (1,))
    got_lat = shift(south[:, HALF_LAT:, :30], ("lat",), (1,))
    got_both = shift(south[:, HALF_LAT:, 30:], ("lon", "lat"), (1, 1))
    grad_x = jnp.concatenate(
        [
            jnp.concatenate([got_both, got_lat], axis=2),
            jnp.concatenate([got_lon[:, :18], inner, east[:, :, :HALF_LON]], axis=2),
            jnp.concatenate([got_lon[:, 18:], south[:, :HALF_LAT, :30]], axis=2),
        ],
        axis=1,
    )
    sums = sum_over_devices(sums)
    factor = float(
        levels * lat_count * lax.axis_size("lat") * lon_count * lax.axis_size("lon")
    ) ** (-0.5)
    gq, go, gbias, gg = finish(sums, ln_gain.reshape(D, 1), qkv_weight, factor)
    return (grad_x, gq, go, gbias, gg.reshape(D))


def solution(mesh):
    placed = (P(None, "lat", "lon", None), P(None, "lat", "lon", None), P(), P(), P(), P())
    return jax.shard_map(
        local,
        mesh=mesh,
        in_specs=placed,
        out_specs=(P(None, "lat", "lon", None), P(), P(), P(), P()),
        check_vma=False,
    )
```

time: 770 us -> 191 us (0.25)
  matrix products: 230 us -> 0 us
  local copies, waits for them, and re-layouts: 211 us -> 20.6 us
  other arithmetic: 156 us -> 10.4 us
  Pallas kernels: 0 us -> 99.1 us
  blocking collectives: 67.9 us -> 0 us
  waiting for transfers between devices: 59.1 us -> 23.6 us
  starting transfers between devices: 20.8 us -> 35.5 us
  between operations: 14.2 us -> 1.03 us
    dot_general x160 -> x0, matrix products: 188 us -> none  [the longest x16 42.3 us: window_grads(): jnp.dot(d_packed, qkv_weight.T, preferred_element_type=jnp.float32)]
    pallas_call x0 -> x4, Pallas kernels: none -> 99.1 us  [the longest x1 46.4 us: inner_windows(): pl.pallas_call(inner_kernel, grid=(levels // 2, 3), in_specs=[rows(1), ro...]
    psum x1 -> x0, blocking collectives: 67.9 us -> none  [local(): lax.psum((partial_grads[0], partial_grads[1], partial_grads[2], partial_g...]
    reshape x52 -> x6, local copies, waits for them, and re-layouts: 58.1 us -> 2.29 us  [the longest x1 0.87 us: make_consts(): jnp.pad(qkv_weight.reshape(D, 3, D), ((0, 0), (0, 0), (0, 64)))]
    psum x1 -> x0, waiting for transfers between devices: 55.4 us -> none  [local(): lax.psum((partial_grads[0], partial_grads[1], partial_grads[2], partial_g...]
    reduce_sum x48 -> x0, other arithmetic: 49.1 us -> none  [the longest x16 19.9 us: window_grads(): jnp.mean(centred * centred, axis=-1, keepdims=True) + 1e-05]
    sub x16 -> x0, matrix products: 42.1 us -> none  [window_grads(): exp_scores = jnp.exp(scores - row_peak)]
    convert_element_type x49 -> x4, other arithmetic: 39.2 us -> 0.18 us  [the longest x3 0.15 us: sum_over_devices(): low = total.astype(BF16)]
  transfers between devices with their start and end apart: 7 -> 23, of which waited for: 2 -> 12; matrix products, arithmetic and copies ran while one was open for 8% -> 11% of each run, Pallas kernels for 0% -> 38%
where the time goes in v1:
time: 191 us; the launch traced here: 190 us
  Pallas kernels  99.1 us (52%)
  starting transfers between devices  35.5 us (19%)
  waiting for transfers between devices  23.6 us (12%)
  local copies, waits for them, and re-layouts  20.6 us (11%)
  other arithmetic  10.4 us (5%)
    pallas_call x1, Pallas kernels, inner_windows(): pl.pallas_call(inner_kernel, grid=(levels // 2, 3), in_specs=[rows(1), ro...  46.4 us
    pallas_call x1, Pallas kernels, east_windows(): pl.pallas_call(east_kernel, grid=(levels // 4, 3), in_specs=[rows(1, 36),...  25.4 us
    pallas_call x1, Pallas kernels, south_windows(): pl.pallas_call(south_kernel, grid=(levels // 2,), in_specs=[rows(7, 36),...  24.9 us
    ppermute x9, starting transfers between devices, shift(): return lax.ppermute(value, axes if len(axes) > 1 else axes[0], pairs)  17.1 us
    ppermute x13, starting transfers between devices, moved(): return lax.ppermute(value, axis, [(n, to_of(n)) for n in range(count)])  16.2 us
    ppermute x9, waiting for transfers between devices, shift(): return lax.ppermute(value, axes if len(axes) > 1 else axes[0], pairs)  11.7 us
    ppermute x13, waiting for transfers between devices, moved(): return lax.ppermute(value, axis, [(n, to_of(n)) for n in range(count)])  11.7 us
    unnamed x28, local copies, waits for them, and re-layouts  7.21 us
  transfers between devices with their start and end apart: 23, of which 12 were waited for; matrix products, arithmetic and copies ran while one was open for 11% of the time, Pallas kernels for 38%

profile of v1, /device:TPU:0, one launch (start us, length us, event | category | flops | bytes accessed | tf_op | source)
XLA Modules:
  0.0 190.3 jit_solution(15262038157548596783)
XLA Ops:
  0.6 2.9 %copy.78.xt.xu = bf16[8,24,36,192]{3,2,1,0:T(8,128)(2,1)S(1)} copy(bf16[8,24,36,192]{3,1,2,0:T(8,128)(2,1)} %param.6) | data formatting | bytes 5308416 | tf_op args[0]
  4.5 6.6 %collective-permute-start = (bf16[8,3,36,192]{3,2,1,0:T(8,128)(2,1)}, bf16[8,3,36,192]{3,2,1,0:T(8,128)(2,1)}, u32[]{:S(2)}, u32[]{:S(2)}) collective-permute-start(bf16[8,3,36,192]{3,2,1,0:T(8,128)(2,1)} %slice.72), channel_id=1, source_target_pairs={{0,7},{1,0},{2,1},{3,2},{4,3},{5,4},{6,5},{7,6},{8,15},{9,8},{10,9... | collective-permute-start | bytes 995336 | tf_op jit(solution)/shard_map/ppermute | solution.py:401
  13.2 1.3 slice.56
  14.6 2.7 %collective-permute-start.2 = (bf16[8,24,6,192]{3,1,2,0:T(8,128)(2,1)S(1)}, bf16[8,24,6,192]{3,1,2,0:T(8,128)(2,1)}, u32[]{:S(2)}, u32[]{:S(2)}) collective-permute-start(bf16[8,24,6,192]{3,1,2,0:T(8,128)(2,1)S(1)} %slice.56), channel_id=1, source_target_pairs={{0,120},{8,0},{16,8},{24,16},{32,24},{40,32},{48,40},{56,48},{64,5... | collective-permute-start | bytes 1327112 | tf_op jit(solution)/shard_map/ppermute | solution.py:401
  17.3 2.4 %collective-permute-start.3 = (bf16[8,3,6,192]{3,2,1,0:T(8,128)(2,1)S(1)}, bf16[8,3,6,192]{3,2,1,0:T(8,128)(2,1)S(1)}, u32[]{:S(2)}, u32[]{:S(2)}) collective-permute-start(bf16[8,3,6,192]{3,2,1,0:T(8,128)(2,1)S(1)} %slice.74), channel_id=1, source_target_pairs={{0,127},{1,120},{2,121},{3,122},{4,123},{5,124},{6,125},{7,126},{8... | collective-permute-start | bytes 165896 | tf_op jit(solution)/shard_map/ppermute | solution.py:401
  24.4 46.4 %inner_windows.1 = (bf16[8,18,24,192]{3,2,1,0:T(8,128)(2,1)}, f32[4,192,192]{2,1,0:T(8,128)}, f32[144,896]{1,0:T(8,128)}) custom-call(bf16[8,24,36,192]{3,2,1,0:T(8,128)(2,1)} %copy-done, bf16[8,24,36,192]{3,2,1,0:T(8,128)(2,1)} %copy-done, bf16[8,24,36,192]{3,2,1,0:T(8,128)(2,1)} %copy-done.1, bf16[8,24,36,192]{3,2,1,0:T(8,128)(2,1)} %copy-done.1, ...), custom_call_target="tpu_custom_call" | custom-call | flops 5096079360 | bytes 3981312 | tf_op jit(solution)/shard_map/inner_windows/pallas_call | solution.py:271
  71.7 1.5 collective-permute-start.5
  73.1 2.1 %copy.80.ext.exu = bf16[8,24,6,192]{3,2,1,0:T(8,128)(2,1)} copy(bf16[8,24,6,192]{3,1,2,0:T(8,128)(2,1)} %collective-permute-done.2) | data formatting | bytes 884736 | tf_op jit(solution)/shard_map/ppermute | solution.py:401
  75.2 2.1 %copy.81.eyt.eyu = bf16[8,24,6,192]{3,2,1,0:T(8,128)(2,1)} copy(bf16[8,24,6,192]{3,1,2,0:T(8,128)(2,1)} %collective-permute-done.4) | data formatting | bytes 884736 | tf_op jit(solution)/shard_map/ppermute | solution.py:401
  77.3 25.4 %east_windows.1 = (bf16[8,18,12,192]{3,2,1,0:T(8,128)(2,1)}, f32[4,192,192]{2,1,0:T(8,128)}, f32[144,896]{1,0:T(8,128)}) custom-call(bf16[8,24,36,192]{3,2,1,0:T(8,128)(2,1)} %copy-done, bf16[8,24,36,192]{3,2,1,0:T(8,128)(2,1)} %copy-done, bf16[8,24,36,192]{3,2,1,0:T(8,128)(2,1)} %copy-done.1, bf16[8,24,36,192]{3,2,1,0:T(8,128)(2,1)} %copy-done.1, ...), custom_call_target="tpu_custom_call" | custom-call | flops 2548039680 | bytes 1990656 | tf_op jit(solution)/shard_map/east_windows/pallas_call | solution.py:293
  103.5 24.9 %south_windows.1 = (bf16[8,6,36,192]{3,2,1,0:T(8,128)(2,1)}, f32[2176,128]{1,0:T(8,128)}) custom-call(bf16[8,24,36,192]{3,2,1,0:T(8,128)(2,1)} %copy-done, bf16[8,3,36,192]{3,2,1,0:T(8,128)(2,1)} %collective-permute-done.xs, bf16[8,24,36,192]{3,2,1,0:T(8,128)(2,1)} %copy-done.1, bf16[8,3,36,192]{3,2,1,0:T(8,128)(2,1)} %collective-permute-done.1.ys, ...), custom_call_target="tpu_custom_call" | custom-call | flops 2548039680 | bytes 1990656 | tf_op jit(solution)/shard_map/south_windows/pallas_call | solution.py:318
  128.4 1.2 fusion
  131.8 1.1 bitcast_add_fusion
  133.1 2.3 %collective-permute-start.11 = (bf16[272,128]{1,0:T(8,128)(2,1)S(1)}, bf16[272,128]{1,0:T(8,128)(2,1)S(1)}, u32[]{:S(2)}, u32[]{:S(2)}) collective-permute-start(bf16[272,128]{1,0:T(8,128)(2,1)S(1)} %get-tuple-element.62), channel_id=1, source_target_pairs={{0,32},{8,40},{16,48},{24,56},{32,0},{40,8},{48,16},{56,24},{64,96... | collective-permute-start | bytes 208904 | tf_op jit(solution)/shard_map/ppermute | solution.py:406
  135.4 1.8 collective-permute-start.10
  137.4 2.9 %collective-permute-done.12 = bf16[272,128]{1,0:T(8,128)(2,1)S(1)} collective-permute-done((bf16[272,128]{1,0:T(8,128)(2,1)S(1)}, bf16[272,128]{1,0:T(8,128)(2,1)S(1)}, u32[]{:S(2)}, u32[]{:S(2)}) %collective-permute-start.12) | collective-permute-done | bytes 69664 | tf_op jit(solution)/shard_map/ppermute | solution.py:406
  141.0 3.6 %collective-permute-start.14 = (bf16[272,128]{1,0:T(8,128)(2,1)S(1)}, bf16[272,128]{1,0:T(8,128)(2,1)S(1)}, u32[]{:S(2)}, u32[]{:S(2)}) collective-permute-start(bf16[272,128]{1,0:T(8,128)(2,1)S(1)} %get-tuple-element.44), channel_id=1, source_target_pairs={{0,4},{1,5},{2,6},{3,7},{4,0},{5,1},{6,2},{7,3},{8,12},{9,13},{10,... | collective-permute-start | bytes 208904 | tf_op jit(solution)/shard_map/ppermute | solution.py:406
  145.1 1.8 collective-permute-done.15
  147.5 1.4 collective-permute-done.13
  149.0 2.2 %collective-permute-start.18 = (bf16[272,128]{1,0:T(8,128)(2,1)S(1)}, bf16[272,128]{1,0:T(8,128)(2,1)S(1)}, u32[]{:S(2)}, u32[]{:S(2)}) collective-permute-start(bf16[272,128]{1,0:T(8,128)(2,1)S(1)} %fusion.5), channel_id=1, source_target_pairs={{0,65},{1,64},{2,67},{3,66},{4,69},{5,68},{6,71},{7,70},{8,73},{9,... | collective-permute-start | bytes 208904 | tf_op jit(solution)/shard_map/ppermute | solution.py:465
  151.1 2.6 %collective-permute-start.16 = (bf16[272,128]{1,0:T(8,128)(2,1)S(1)}, bf16[272,128]{1,0:T(8,128)(2,1)S(1)}, u32[]{:S(2)}, u32[]{:S(2)}) collective-permute-start(bf16[272,128]{1,0:T(8,128)(2,1)S(1)} %fusion.5), channel_id=1, source_target_pairs={{0,1},{1,0},{2,3},{3,2},{4,5},{5,4},{6,7},{7,6},{8,9},{9,8},{10,11... | collective-permute-start | bytes 208904 | tf_op jit(solution)/shard_map/ppermute | solution.py:406
  155.4 1.5 collective-permute-done.16
  157.0 2.0 %collective-permute-start.21 = (bf16[272,128]{1,0:T(8,128)(2,1)S(1)}, bf16[272,128]{1,0:T(8,128)(2,1)S(1)}, u32[]{:S(2)}, u32[]{:S(2)}) collective-permute-start(bf16[272,128]{1,0:T(8,128)(2,1)S(1)} %add_convert_fusion), channel_id=1, source_target_pairs={{0,48},{8,56},{16,32},{24,40},{32,16},{40,24},{48,0},{56,8},{64,11... | collective-permute-start | bytes 208904 | tf_op jit(solution)/shard_map/ppermute | solution.py:406
  160.0 1.2 collective-permute-start.19
  161.3 2.7 %collective-permute-start.7 = (bf16[8,3,30,192]{3,2,1,0:T(8,128)(2,1)S(1)}, bf16[8,3,30,192]{3,2,1,0:T(8,128)(2,1)S(1)}, u32[]{:S(2)}, u32[]{:S(2)}) collective-permute-start(bf16[8,3,30,192]{3,2,1,0:T(8,128)(2,1)S(1)} %get-tuple-element.50), channel_id=1, source_target_pairs={{0,1},{1,2},{2,3},{3,4},{4,5},{5,6},{6,7},{7,0},{8,9},{9,10},{10,1... | collective-permute-start | bytes 829448 | tf_op jit(solution)/shard_map/ppermute | solution.py:401
  164.0 1.9 collective-permute-done.8
  166.0 1.6 collective-permute-done.21
  167.8 9.8 %collective-permute-done.6 = bf16[8,3,6,192]{3,2,1,0:T(8,128)(2,1)S(1)} collective-permute-done((bf16[8,3,6,192]{3,2,1,0:T(8,128)(2,1)S(1)}, bf16[8,3,6,192]{3,2,1,0:T(8,128)(2,1)S(1)}, u32[]{:S(2)}, u32[]{:S(2)}) %collective-permute-start.6) | collective-permute-done | bytes 55328 | tf_op jit(solution)/shard_map/ppermute | solution.py:401
  177.7 4.9 %maximum_maximum_fusion = bf16[8,24,36,192]{3,2,1,0:T(8,128)(2,1)S(1)} fusion(bf16[8,3,30,192]{3,2,1,0:T(8,128)(2,1)S(1)} %get-tuple-element.51, bf16[8,3,6,192]{3,2,1,0:T(8,128)(2,1)S(1)} %copy.91, bf16[8,18,6,192]{3,2,1,0:T(8,128)(2,1)S(1)} %get-tuple-element.46, bf16[8,18,24,192]{3,2,1,0:T(8,128)(2,1)S(1)} %copy-done.4, ...), kind=kLoop, calls=%fused_computation | loop fusion | flops 18579456 | bytes 5308416 | tf_op jit(solution)/shard_map/concatenate | solution.py:491
  182.6 2.5 %copy.86 = bf16[8,24,36,192]{3,1,2,0:T(8,128)(2,1)} copy(bf16[8,24,36,192]{3,2,1,0:T(8,128)(2,1)S(1)} %maximum_maximum_fusion) | data formatting | bytes 5308416
  186.3 2.4 %finish_sums.1 = (f32[192,576]{1,0:T(8,128)}, f32[192,192]{1,0:T(8,128)}, f32[6,144,144]{2,1,0:T(8,128)}, f32[192,1]{1,0:T(8,128)}) custom-call(bf16[2176,128]{1,0:T(8,128)(2,1)} %pad_maximum_fusion.1.refs_0_, f32[192,1]{1,0:T(8,128)} %copy.85.refs_1_, bf16[192,576]{1,0:T(8,128)(2,1)} %refs_2_.1), custom_call_target="tpu_custom_call" | custom-call | tf_op jit(solution)/shard_map/finish_sums/pallas_call | solution.py:354
  188.7 1.6 reduce
  (92 shorter events, 18.0 us)
Async XLA Ops:
  0.6 10.4 %copy-start.2 = (bf16[8,24,36,192]{3,1,2,0:T(8,128)(2,1)S(1)}, bf16[8,24,36,192]{3,1,2,0:T(8,128)(2,1)}, u32[]{:S(2)}) copy-start(bf16[8,24,36,192]{3,1,2,0:T(8,128)(2,1)} %param.7) | copy-start | bytes 7962628
  3.6 13.7 %copy-start = (bf16[8,24,36,192]{3,2,1,0:T(8,128)(2,1)}, bf16[8,24,36,192]{3,2,1,0:T(8,128)(2,1)S(1)}, u32[]{:S(2)}) copy-start(bf16[8,24,36,192]{3,2,1,0:T(8,128)(2,1)S(1)} %copy.78.xt.xu) | copy-start | bytes 7962628
  4.5 16.6 %copy-start.3 = (f32[6,144,144]{2,1,0:T(8,128)S(1)}, f32[6,144,144]{2,1,0:T(8,128)}, u32[]{:S(2)}) copy-start(f32[6,144,144]{2,1,0:T(8,128)} %param.11) | copy-start | bytes 1492996
  4.5 98.4 %collective-permute-start = (bf16[8,3,36,192]{3,2,1,0:T(8,128)(2,1)}, bf16[8,3,36,192]{3,2,1,0:T(8,128)(2,1)}, u32[]{:S(2)}, u32[]{:S(2)}) collective-permute-start(bf16[8,3,36,192]{3,2,1,0:T(8,128)(2,1)} %slice.72), channel_id=1, source_target_pairs={{0,7},{1,0},{2,1},{3,2},{4,3},{5,4},{6,5},{7,6},{8,15},{9,8},{10,9... | collective-permute-start | bytes 995336 | tf_op jit(solution)/shard_map/ppermute | solution.py:401
  11.8 5.4 %copy-start.1 = (bf16[8,24,36,192]{3,2,1,0:T(8,128)(2,1)}, bf16[8,24,36,192]{3,2,1,0:T(8,128)(2,1)S(1)}, u32[]{:S(2)}) copy-start(bf16[8,24,36,192]{3,2,1,0:T(8,128)(2,1)S(1)} %copy.79.yt.yu) | copy-start | bytes 7962628
  12.7 8.7 %copy-start.7 = (bf16[192,576]{1,0:T(8,128)(2,1)S(1)}, bf16[192,576]{1,0:T(8,128)(2,1)}, u32[]{:S(2)}) copy-start(bf16[192,576]{1,0:T(8,128)(2,1)} %refs_2_.1) | copy-start | bytes 663556
  12.7 90.1 %collective-permute-start.1 = (bf16[8,3,36,192]{3,2,1,0:T(8,128)(2,1)}, bf16[8,3,36,192]{3,2,1,0:T(8,128)(2,1)}, u32[]{:S(2)}, u32[]{:S(2)}) collective-permute-start(bf16[8,3,36,192]{3,2,1,0:T(8,128)(2,1)} %slice.73), channel_id=1, source_target_pairs={{0,7},{1,0},{2,1},{3,2},{4,3},{5,4},{6,5},{7,6},{8,15},{9,8},{10,9... | collective-permute-start | bytes 995336 | tf_op jit(solution)/shard_map/ppermute | solution.py:401
  14.6 57.1 %collective-permute-start.2 = (bf16[8,24,6,192]{3,1,2,0:T(8,128)(2,1)S(1)}, bf16[8,24,6,192]{3,1,2,0:T(8,128)(2,1)}, u32[]{:S(2)}, u32[]{:S(2)}) collective-permute-start(bf16[8,24,6,192]{3,1,2,0:T(8,128)(2,1)S(1)} %slice.56), channel_id=1, source_target_pairs={{0,120},{8,0},{16,8},{24,16},{32,24},{40,32},{48,40},{56,48},{64,5... | collective-permute-start | bytes 1327112 | tf_op jit(solution)/shard_map/ppermute | solution.py:401
  17.3 85.5 %collective-permute-start.3 = (bf16[8,3,6,192]{3,2,1,0:T(8,128)(2,1)S(1)}, bf16[8,3,6,192]{3,2,1,0:T(8,128)(2,1)S(1)}, u32[]{:S(2)}, u32[]{:S(2)}) collective-permute-start(bf16[8,3,6,192]{3,2,1,0:T(8,128)(2,1)S(1)} %slice.74), channel_id=1, source_target_pairs={{0,127},{1,120},{2,121},{3,122},{4,123},{5,124},{6,125},{7,126},{8... | collective-permute-start | bytes 165896 | tf_op jit(solution)/shard_map/ppermute | solution.py:401
  20.5 54.7 %collective-permute-start.4 = (bf16[8,24,6,192]{3,1,2,0:T(8,128)(2,1)}, bf16[8,24,6,192]{3,1,2,0:T(8,128)(2,1)}, u32[]{:S(2)}, u32[]{:S(2)}) collective-permute-start(bf16[8,24,6,192]{3,1,2,0:T(8,128)(2,1)} %slice.58), channel_id=1, source_target_pairs={{0,120},{8,0},{16,8},{24,16},{32,24},{40,32},{48,40},{56,48},{64,5... | collective-permute-start | bytes 1327112 | tf_op jit(solution)/shard_map/ppermute | solution.py:401
  71.7 31.1 %collective-permute-start.5 = (bf16[8,3,6,192]{3,2,1,0:T(8,128)(2,1)S(1)}, bf16[8,3,6,192]{3,2,1,0:T(8,128)(2,1)S(1)}, u32[]{:S(2)}, u32[]{:S(2)}) collective-permute-start(bf16[8,3,6,192]{3,2,1,0:T(8,128)(2,1)S(1)} %slice.75), channel_id=1, source_target_pairs={{0,127},{1,120},{2,121},{3,122},{4,123},{5,124},{6,125},{7,126},{8... | collective-permute-start | bytes 165896 | tf_op jit(solution)/shard_map/ppermute | solution.py:401
  103.5 27.1 %copy-start.10 = (f32[192]{0:T(256)S(1)}, f32[192]{0:T(256)}, u32[]{:S(2)}) copy-start(f32[192]{0:T(256)} %param.8) | copy-start | bytes 2308
  128.4 8.8 %copy-start.5 = (bf16[8,18,12,192]{3,2,1,0:T(8,128)(2,1)S(1)}, bf16[8,18,12,192]{3,2,1,0:T(8,128)(2,1)}, u32[]{:S(2)}) copy-start(bf16[8,18,12,192]{3,2,1,0:T(8,128)(2,1)} %get-tuple-element.22) | copy-start | bytes 1990660
  128.4 16.7 %copy-start.6 = (bf16[8,6,36,192]{3,2,1,0:T(8,128)(2,1)S(1)}, bf16[8,6,36,192]{3,2,1,0:T(8,128)(2,1)}, u32[]{:S(2)}) copy-start(bf16[8,6,36,192]{3,2,1,0:T(8,128)(2,1)} %get-tuple-element.21) | copy-start | bytes 1990660
  129.6 2.2 %collective-permute-start.9 = (bf16[1088,128]{1,0:T(8,128)(2,1)S(1)}, bf16[1088,128]{1,0:T(8,128)(2,1)S(1)}, u32[]{:S(2)}, u32[]{:S(2)}) collective-permute-start(bf16[1088,128]{1,0:T(8,128)(2,1)S(1)} %fusion), channel_id=1, source_target_pairs={{0,8},{8,0},{16,24},{24,16},{32,40},{40,32},{48,56},{56,48},{64,72... | collective-permute-start | bytes 835592 | tf_op jit(solution)/shard_map/ppermute | solution.py:406
  133.0 7.2 %collective-permute-start.12 = (bf16[272,128]{1,0:T(8,128)(2,1)S(1)}, bf16[272,128]{1,0:T(8,128)(2,1)S(1)}, u32[]{:S(2)}, u32[]{:S(2)}) collective-permute-start(bf16[272,128]{1,0:T(8,128)(2,1)S(1)} %get-tuple-element.61), channel_id=1, source_target_pairs={{0,48},{8,56},{16,32},{24,40},{32,16},{40,24},{48,0},{56,8},{64,11... | collective-permute-start | bytes 208904 | tf_op jit(solution)/shard_map/ppermute | solution.py:406
  133.1 7.2 %collective-permute-start.11 = (bf16[272,128]{1,0:T(8,128)(2,1)S(1)}, bf16[272,128]{1,0:T(8,128)(2,1)S(1)}, u32[]{:S(2)}, u32[]{:S(2)}) collective-permute-start(bf16[272,128]{1,0:T(8,128)(2,1)S(1)} %get-tuple-element.62), channel_id=1, source_target_pairs={{0,32},{8,40},{16,48},{24,56},{32,0},{40,8},{48,16},{56,24},{64,96... | collective-permute-start | bytes 208904 | tf_op jit(solution)/shard_map/ppermute | solution.py:406
  135.4 5.4 %collective-permute-start.10 = (bf16[272,128]{1,0:T(8,128)(2,1)S(1)}, bf16[272,128]{1,0:T(8,128)(2,1)S(1)}, u32[]{:S(2)}, u32[]{:S(2)}) collective-permute-start(bf16[272,128]{1,0:T(8,128)(2,1)S(1)} %get-tuple-element.60), channel_id=1, source_target_pairs={{0,16},{8,24},{16,0},{24,8},{32,48},{40,56},{48,32},{56,40},{64,80... | collective-permute-start | bytes 208904 | tf_op jit(solution)/shard_map/ppermute | solution.py:406
  140.8 6.0 %collective-permute-start.15 = (bf16[272,128]{1,0:T(8,128)(2,1)S(1)}, bf16[272,128]{1,0:T(8,128)(2,1)S(1)}, u32[]{:S(2)}, u32[]{:S(2)}) collective-permute-start(bf16[272,128]{1,0:T(8,128)(2,1)S(1)} %get-tuple-element.44), channel_id=1, source_target_pairs={{0,6},{1,7},{2,4},{3,5},{4,2},{5,3},{6,0},{7,1},{8,14},{9,15},{10,... | collective-permute-start | bytes 208904 | tf_op jit(solution)/shard_map/ppermute | solution.py:406
  141.0 6.5 %collective-permute-start.14 = (bf16[272,128]{1,0:T(8,128)(2,1)S(1)}, bf16[272,128]{1,0:T(8,128)(2,1)S(1)}, u32[]{:S(2)}, u32[]{:S(2)}) collective-permute-start(bf16[272,128]{1,0:T(8,128)(2,1)S(1)} %get-tuple-element.44), channel_id=1, source_target_pairs={{0,4},{1,5},{2,6},{3,7},{4,0},{5,1},{6,2},{7,3},{8,12},{9,13},{10,... | collective-permute-start | bytes 208904 | tf_op jit(solution)/shard_map/ppermute | solution.py:406
  144.6 4.3 %collective-permute-start.13 = (bf16[272,128]{1,0:T(8,128)(2,1)S(1)}, bf16[272,128]{1,0:T(8,128)(2,1)S(1)}, u32[]{:S(2)}, u32[]{:S(2)}) collective-permute-start(bf16[272,128]{1,0:T(8,128)(2,1)S(1)} %get-tuple-element.44), channel_id=1, source_target_pairs={{0,2},{1,3},{2,0},{3,1},{4,6},{5,7},{6,4},{7,5},{8,10},{9,11},{10,... | collective-permute-start | bytes 208904 | tf_op jit(solution)/shard_map/ppermute | solution.py:406
  149.0 5.6 %collective-permute-start.18 = (bf16[272,128]{1,0:T(8,128)(2,1)S(1)}, bf16[272,128]{1,0:T(8,128)(2,1)S(1)}, u32[]{:S(2)}, u32[]{:S(2)}) collective-permute-start(bf16[272,128]{1,0:T(8,128)(2,1)S(1)} %fusion.5), channel_id=1, source_target_pairs={{0,65},{1,64},{2,67},{3,66},{4,69},{5,68},{6,71},{7,70},{8,73},{9,... | collective-permute-start | bytes 208904 | tf_op jit(solution)/shard_map/ppermute | solution.py:465
  151.1 4.3 %collective-permute-start.17 = (bf16[272,128]{1,0:T(8,128)(2,1)S(1)}, bf16[272,128]{1,0:T(8,128)(2,1)S(1)}, u32[]{:S(2)}, u32[]{:S(2)}) collective-permute-start(bf16[272,128]{1,0:T(8,128)(2,1)S(1)} %fusion.5), channel_id=1, source_target_pairs={{0,64},{8,72},{16,80},{24,88},{32,96},{40,104},{48,112},{56,120},{... | collective-permute-start | bytes 208904 | tf_op jit(solution)/shard_map/ppermute | solution.py:406
  151.1 5.8 %collective-permute-start.16 = (bf16[272,128]{1,0:T(8,128)(2,1)S(1)}, bf16[272,128]{1,0:T(8,128)(2,1)S(1)}, u32[]{:S(2)}, u32[]{:S(2)}) collective-permute-start(bf16[272,128]{1,0:T(8,128)(2,1)S(1)} %fusion.5), channel_id=1, source_target_pairs={{0,1},{1,0},{2,3},{3,2},{4,5},{5,4},{6,7},{7,6},{8,9},{9,8},{10,11... | collective-permute-start | bytes 208904 | tf_op jit(solution)/shard_map/ppermute | solution.py:406
  153.9 23.8 %copy-start.4 = (bf16[8,18,24,192]{3,2,1,0:T(8,128)(2,1)S(1)}, bf16[8,18,24,192]{3,2,1,0:T(8,128)(2,1)}, u32[]{:S(2)}) copy-start(bf16[8,18,24,192]{3,2,1,0:T(8,128)(2,1)} %get-tuple-element.23) | copy-start | bytes 3981316
  154.0 11.8 %collective-permute-start.8 = (bf16[8,21,6,192]{3,0,2,1:T(8,128)(2,1)S(1)}, bf16[8,21,6,192]{3,0,2,1:T(8,128)(2,1)S(1)}, u32[]{:S(2)}, u32[]{:S(2)}) collective-permute-start(bf16[8,21,6,192]{3,0,2,1:T(8,128)(2,1)S(1)} %copy.82), channel_id=1, source_target_pairs={{0,8},{8,16},{16,24},{24,32},{32,40},{40,48},{48,56},{56,64},{64,7... | collective-permute-start | bytes 1161224 | tf_op jit(solution)/shard_map/ppermute | solution.py:401
  157.0 10.6 %collective-permute-start.21 = (bf16[272,128]{1,0:T(8,128)(2,1)S(1)}, bf16[272,128]{1,0:T(8,128)(2,1)S(1)}, u32[]{:S(2)}, u32[]{:S(2)}) collective-permute-start(bf16[272,128]{1,0:T(8,128)(2,1)S(1)} %add_convert_fusion), channel_id=1, source_target_pairs={{0,48},{8,56},{16,32},{24,40},{32,16},{40,24},{48,0},{56,8},{64,11... | collective-permute-start | bytes 208904 | tf_op jit(solution)/shard_map/ppermute | solution.py:406
  159.0 8.6 %collective-permute-start.20 = (bf16[272,128]{1,0:T(8,128)(2,1)S(1)}, bf16[272,128]{1,0:T(8,128)(2,1)S(1)}, u32[]{:S(2)}, u32[]{:S(2)}) collective-permute-start(bf16[272,128]{1,0:T(8,128)(2,1)S(1)} %add_convert_fusion), channel_id=1, source_target_pairs={{0,32},{8,40},{16,48},{24,56},{32,0},{40,8},{48,16},{56,24},{64,96... | collective-permute-start | bytes 208904 | tf_op jit(solution)/shard_map/ppermute | solution.py:406
  160.0 7.6 %collective-permute-start.19 = (bf16[272,128]{1,0:T(8,128)(2,1)S(1)}, bf16[272,128]{1,0:T(8,128)(2,1)S(1)}, u32[]{:S(2)}, u32[]{:S(2)}) collective-permute-start(bf16[272,128]{1,0:T(8,128)(2,1)S(1)} %add_convert_fusion), channel_id=1, source_target_pairs={{0,16},{8,24},{16,0},{24,8},{32,48},{40,56},{48,32},{56,40},{64,80... | collective-permute-start | bytes 208904 | tf_op jit(solution)/shard_map/ppermute | solution.py:406
  161.3 16.4 %collective-permute-start.7 = (bf16[8,3,30,192]{3,2,1,0:T(8,128)(2,1)S(1)}, bf16[8,3,30,192]{3,2,1,0:T(8,128)(2,1)S(1)}, u32[]{:S(2)}, u32[]{:S(2)}) collective-permute-start(bf16[8,3,30,192]{3,2,1,0:T(8,128)(2,1)S(1)} %get-tuple-element.50), channel_id=1, source_target_pairs={{0,1},{1,2},{2,3},{3,4},{4,5},{5,6},{6,7},{7,0},{8,9},{9,10},{10,1... | collective-permute-start | bytes 829448 | tf_op jit(solution)/shard_map/ppermute | solution.py:401
  165.8 11.8 %collective-permute-start.6 = (bf16[8,3,6,192]{3,2,1,0:T(8,128)(2,1)S(1)}, bf16[8,3,6,192]{3,2,1,0:T(8,128)(2,1)S(1)}, u32[]{:S(2)}, u32[]{:S(2)}) collective-permute-start(bf16[8,3,6,192]{3,2,1,0:T(8,128)(2,1)S(1)} %get-tuple-element.48), channel_id=1, source_target_pairs={{0,9},{1,10},{2,11},{3,12},{4,13},{5,14},{6,15},{7,8},{8,17},{9,18... | collective-permute-start | bytes 165896 | tf_op jit(solution)/shard_map/ppermute | solution.py:401
  167.8 17.4 %collective-permute-start.22 = (bf16[4,272,128]{2,1,0:T(8,128)(2,1)S(1)}, bf16[4,272,128]{2,1,0:T(8,128)(2,1)S(1)}, u32[]{:S(2)}, u32[]{:S(2)}) collective-permute-start(bf16[4,272,128]{2,1,0:T(8,128)(2,1)S(1)} %get-tuple-element.54), channel_id=1, source_target_pairs={{0,8},{8,0},{16,24},{24,16},{32,40},{40,32},{48,56},{56,48},{64,72... | collective-permute-start | bytes 835592 | tf_op jit(solution)/shard_map/ppermute | solution.py:406
  (2 other events, 1.3 us)

commit v2 on v1

v2 whole, which is shorter than its diff:
```python
import jax
import jax.numpy as jnp
from jax import lax
from jax.experimental import pallas as pl
from jax.experimental.pallas import tpu as pltpu
from jax.sharding import PartitionSpec as P

WIN_LEV = 2
WIN_LAT = 6
WIN_LON = 12
W = 144
HEADS = 6
HEAD = 32
D = 192
HALF_LAT = 3
HALF_LON = 6
LANES = 896
LOG2E = 1.4426950408889634
SCALE = HEAD**-0.5
F32 = jnp.float32
BF16 = jnp.bfloat16
WROWS = 6 * D
BROWS = 7 * W
ROWS = 2176

NN = (((1,), (0,)), ((), ()))
NT = (((1,), (1,)), ((), ()))
TN = (((0,), (0,)), ((), ()))


def mm(a, b, dims):
    return lax.dot_general(a, b, dims, preferred_element_type=F32)


def pair_rows(rows, c):
    part = rows[:128, 64 * c : 64 * c + 64]
    first = lax.broadcasted_iota(jnp.int32, (1, 64), 1) < HEAD
    zero = jnp.zeros_like(part)
    return jnp.concatenate([jnp.where(first, part, zero), jnp.where(first, zero, part)], axis=0)


def rest_rows(rows):
    head_of = lax.broadcasted_iota(jnp.int32, (1, D), 1) // HEAD
    rest = rows[128:]
    zero = jnp.zeros_like(rest)
    return jnp.concatenate(
        [jnp.where(head_of == h, rest, zero) for h in range(HEADS)] + [zero, zero], axis=0
    )


def fold_rest(rest):
    head_of = lax.broadcasted_iota(jnp.int32, (1, D), 1) // HEAD
    total = rest[:16]
    for h in range(1, HEADS):
        total = jnp.where(head_of == h, rest[16 * h : 16 * h + 16], total)
    return total


class Window:
    def __init__(self, fetch, put, bias_at, refs):
        self.fetch, self.put, self.bias_at, self.refs = fetch, put, bias_at, refs

    def front(self):
        r = self.refs
        x, dy = self.fetch()
        mean = jnp.mean(x, axis=-1, keepdims=True)
        centred = x - mean
        self.inv_std = lax.rsqrt(jnp.mean(centred * centred, axis=-1, keepdims=True) + 1e-05)
        self.unit = centred * self.inv_std
        self.normed = (self.unit * r["gain"][...]).astype(BF16)
        self.dy = dy
        self.dyb = dy.astype(BF16)
        packed = mm(self.normed, r["wqkv"][...], NN).astype(BF16)
        self.q = packed[:, 0:192]
        self.k = packed[:, 256:448]
        self.v = packed[:, 512:704]
        self.da = mm(self.dyb, r["wout_t"][...], NN).astype(BF16)
        self.kt = self.k.T
        self.vt = self.v.T
        self.raw, self.low, self.dv, self.dk, self.at, self.dqt = {}, {}, {}, {}, {}, {}
        self.qm, self.dam = {}, {}

    def scores(self, c):
        if c < 3:
            cols = slice(64 * c, 64 * c + 64)
            self.qm[c] = pair_rows(self.q, c)
            self.dam[c] = pair_rows(self.da, c)
            k, v = self.k[:, cols], self.v[:, cols]
        else:
            self.qm[c] = rest_rows(self.q)
            self.dam[c] = rest_rows(self.da)
            k, v = self.k, self.v
        self.raw[c] = (mm(k, self.qm[c], NT), mm(v, self.dam[c], NT))

    def softmax(self, c):
        lanes = slice(256 * c, 256 * c + 256) if c < 3 else slice(768, 896)
        raw, dp = self.raw.pop(c)
        s = raw * (SCALE * LOG2E) + self.refs["bias"][self.bias_at, :, lanes]
        e = jnp.exp2(s - jnp.max(s, axis=0, keepdims=True))
        p = e * (1.0 / jnp.sum(e, axis=0, keepdims=True))
        ds = p * (dp - jnp.sum(p * dp, axis=0, keepdims=True))
        self.refs["gb"][:, lanes] += ds
        self.low[c] = (p.astype(BF16), ds.astype(BF16))

    def products(self, c):
        pb, dsb = self.low.pop(c)
        self.dv[c] = mm(pb, self.dam.pop(c), NN)
        self.dk[c] = mm(dsb, self.qm.pop(c), NN)
        if c < 3:
            self.at[c] = mm(self.vt[64 * c : 64 * c + 64], pb, NN)
            self.dqt[c] = mm(self.kt[64 * c : 64 * c + 64], dsb, NN)
        else:
            self.at[c] = fold_rest(mm(pb, self.v, TN))
            self.dqt[c] = fold_rest(mm(dsb, self.k, TN))

    def back(self):
        r = self.refs

        def queries(parts):
            main = [p for c in range(3) for p in (parts[c][:32, :128], parts[c][32:, 128:])]
            return jnp.concatenate([jnp.concatenate(main, axis=0).T, parts[3]], axis=0)

        def keys(parts):
            return jnp.concatenate([parts[c] for c in range(3)], axis=1) + parts[3]

        self.a = queries(self.at).astype(BF16)
        self.dqb = (queries(self.dqt) * SCALE).astype(BF16)
        self.dkb = (keys(self.dk) * SCALE).astype(BF16)
        self.dvb = keys(self.dv).astype(BF16)
        w = r["wqkv_t"]
        dn = mm(self.dqb, w[0:192], NN) + mm(self.dkb, w[192:384], NN) + mm(self.dvb, w[384:576], NN)
        du = dn * r["gain"][...]
        dx = self.inv_std * (
            du
            - jnp.mean(du, axis=-1, keepdims=True)
            - self.unit * jnp.mean(du * self.unit, axis=-1, keepdims=True)
        )
        self.put(self.dy + dx)

    def steps(self):
        yield self.front
        yield lambda: self.scores(0)
        yield lambda: (self.scores(1), self.softmax(0))
        yield lambda: (self.scores(2), self.softmax(1), self.products(0))
        yield lambda: (self.scores(3), self.softmax(2), self.products(1))
        yield lambda: (self.softmax(3), self.products(2))
        yield lambda: self.products(3)
        yield self.back


STAGGER = 4


def run_windows(windows, gw_ref):
    plans = [list(w.steps()) for w in windows]
    for tick in range(STAGGER * (len(plans) - 1) + len(plans[0])):
        for n in reversed(range(len(plans))):
            at = tick - STAGGER * n
            if 0 <= at < len(plans[n]):
                plans[n][at]()
    normed = jnp.concatenate([w.normed for w in windows], axis=0)
    for n, name in enumerate(("dqb", "dkb", "dvb")):
        gw_ref[n] += mm(normed, jnp.concatenate([getattr(w, name) for w in windows], axis=0), TN)
    gw_ref[3] += mm(
        jnp.concatenate([w.a for w in windows], axis=0),
        jnp.concatenate([w.dyb for w in windows], axis=0),
        TN,
    )


def fetch_rows(low, high, start, stride):
    lats = [pl.ds(start + n, 24, stride=stride) for n in range(WIN_LAT)]
    return jnp.concatenate(
        [
            jnp.concatenate([low[at, :] for at in lats], axis=0),
            jnp.concatenate([high[at, :] for at in lats], axis=0)[:, :64],
        ],
        axis=1,
    )


def put_rows(low, high, start, stride, value):
    right = jnp.concatenate([value[:, 128:], jnp.zeros((W, 64), F32)], axis=1)
    for n in range(WIN_LAT):
        at = pl.ds(start + n, 24, stride=stride)
        low[at, :] = value[24 * n : 24 * n + 24, :128]
        high[at, :] = right[24 * n : 24 * n + 24]


def keep(low, high, at, rows):
    wide = rows.astype(F32)
    n = rows.shape[0]
    low[at : at + n, :] = wide[:, :128]
    high[at : at + n, :64] = wide[:, 128:]


def kept(low, high, at, n):
    return jnp.concatenate([low[at : at + n, :], high[at : at + n, :64]], axis=1).astype(BF16)


def window_of(scratch, start, stride, bias_at, refs):
    x0, x1, y0, y1, o0, o1 = scratch

    def fetch():
        return fetch_rows(x0, x1, start, stride), fetch_rows(y0, y1, start, stride)

    def put(value):
        put_rows(o0, o1, start, stride, value)

    return Window(fetch, put, bias_at, refs)


def regroup(rows, back=False):
    if back:
        order = [la * 2 + lv for lv in range(2) for la in range(6)]
    else:
        order = [lv * 6 + la for la in range(6) for lv in range(2)]
    return jnp.concatenate([rows[12 * n : 12 * n + 12] for n in order], axis=0)


def lay_bias(pair_ref, last_ref, bias_ref):
    turned = [regroup(regroup(pair_ref[h]).T) * LOG2E for h in range(HEADS)]
    flat = jnp.concatenate(
        [t[:, :128] for t in turned] + [t[:, 128:] for t in turned] + [jnp.zeros((W, 32), F32)],
        axis=1,
    )
    bias_ref[0] = flat
    key_south = lax.broadcasted_iota(jnp.int32, (W, LANES), 0) >= W // 2
    lane = lax.broadcasted_iota(jnp.int32, (W, LANES), 1)
    query_south = (lane >= 768) | (lane % 128 >= W // 2)
    apart = (key_south != query_south) & (last_ref[...] > 0)
    bias_ref[1] = jnp.where(apart, F32(-1e30), flat)


def inner_kernel(
    x0, x1, x2, x3, y0, y1, y2, y3, gain, wqkv, wqkv_t, wout_t, pair, last, dx_ref, gw_ref, gb_ref, bias_ref, *scratch
):
    @pl.when(pl.program_id(0) == 0)
    def _():
        gw_ref[...] = jnp.zeros_like(gw_ref)
        gb_ref[...] = jnp.zeros_like(gb_ref)
        lay_bias(pair, last, bias_ref)

    xs, ys = (x0, x1, x2, x3), (y0, y1, y2, y3)

    def place(lv, lon):
        return 24 * (24 * (lon // 12) + 12 * lv + lon % 12)

    for lv in range(2):
        for lon in range(24):
            keep(scratch[0], scratch[1], place(lv, lon), xs[lon // 6][lv, lon % 6])
            keep(scratch[2], scratch[3], place(lv, lon), ys[lon // 6][lv, lon % 6])
    refs = dict(
        gain=gain, wqkv=wqkv, wqkv_t=wqkv_t, wout_t=wout_t, bias=bias_ref, gb=gb_ref
    )
    run_windows(
        [
            window_of(scratch, 576 * k + 3 + 6 * a, 24, 0, refs)
            for k in range(2)
            for a in range(3)
        ],
        gw_ref,
    )
    for lv in range(2):
        for lon in range(24):
            dx_ref[lv, lon] = kept(scratch[4], scratch[5], place(lv, lon), 24)


def edge_kernel(
    x, y, e, s, c, gain, wqkv, wqkv_t, wout_t, bias, gw_in, gb_in, oe_ref, os_ref, sum_ref, gw_ref, gb_ref, *scratch
):
    @pl.when(pl.program_id(0) == 0)
    def _():
        gw_ref[...] = gw_in[...]
        gb_ref[...] = gb_in[...]

    def place(lv, lon):
        if lon < 12:
            return 32 * (12 * lv + lon)
        return 768 + 16 * (24 * ((lon - 12) // 12) + 12 * lv + lon % 12)

    for n, own in enumerate((x, y)):
        low, high = scratch[2 * n], scratch[2 * n + 1]
        for lv in range(2):
            for lon in range(6):
                at = place(lv, lon)
                keep(low, high, at, own[lv, 30 + lon])
                keep(low, high, at + 24, s[n, lv, 30 + lon])
                at = place(lv, 6 + lon)
                keep(low, high, at, e[n, lv, lon])
                keep(low, high, at + 24, c[n, lv, lon])
            for lon in range(24):
                at = place(lv, 12 + lon)
                keep(low, high, at, own[lv, 6 + lon].astype(F32)[16:])
                keep(low, high, at + 8, s[n, lv, 6 + lon])
    refs = dict(
        gain=gain, wqkv=wqkv, wqkv_t=wqkv_t, wout_t=wout_t, bias=bias, gb=gb_ref
    )
    run_windows(
        [window_of(scratch, 3 + 6 * a, 32, int(a == 3), refs) for a in range(4)]
        + [window_of(scratch, 768 + 384 * k + 5, 16, 1, refs) for k in range(2)],
        gw_ref,
    )
    for lv in range(2):
        for lon in range(12):
            oe_ref[lv, lon] = kept(scratch[4], scratch[5], place(lv, lon), 32)
        for lon in range(24):
            os_ref[lv, lon] = kept(scratch[4], scratch[5], place(lv, 12 + lon), 16)

    @pl.when(pl.program_id(0) == pl.num_programs(0) - 1)
    def _():
        whole = jnp.concatenate([gw_ref[n] for n in range(4)], axis=1)
        for t in range(6):
            sum_ref[D * t : D * t + D] = whole[:, 128 * t : 128 * t + 128]
        for t in range(7):
            sum_ref[WROWS + W * t : WROWS + W * t + W] = gb_ref[:, 128 * t : 128 * t + 128]
        sum_ref[WROWS + BROWS :] = jnp.zeros((ROWS - WROWS - BROWS, 128), F32)


def whole(shape):
    return pl.BlockSpec(shape, lambda *_: (0,) * len(shape))


PARAMS = pltpu.CompilerParams(vmem_limit_bytes=60 * 1024 * 1024)
GW = (4, D, D)
GB = (W, LANES)
BIAS = (2, W, LANES)


def cost(count):
    return pl.CostEstimate(
        flops=count * 144 * 192 * 192 * 40, bytes_accessed=count * 144 * 192 * 6, transcendentals=0
    )


def const_specs():
    return [whole((1, D)), whole((D, 768)), whole((3 * D, D)), whole((D, D))]


def halves(rows):
    return [pltpu.VMEM((rows, 128), F32) for _ in range(6)]


def inner_windows(x, y, consts, pair_bias, last):
    levels = x.shape[0]

    def cols(n):
        return pl.BlockSpec((2, 6, 24, D), lambda i: (i, n, 0, 0))

    four = [cols(n) for n in range(1, 5)]
    return pl.pallas_call(
        inner_kernel,
        grid=(levels // 2,),
        in_specs=four + four + const_specs() + [whole((HEADS, W, W)), whole((1, 1))],
        out_specs=[
            pl.BlockSpec((2, 24, 24, D), lambda i: (i, 0, 0, 0)),
            whole(GW),
            whole(GB),
            whole(BIAS),
        ],
        out_shape=[
            jax.ShapeDtypeStruct((levels, 24, 24, D), BF16),
            jax.ShapeDtypeStruct(GW, F32),
            jax.ShapeDtypeStruct(GB, F32),
            jax.ShapeDtypeStruct(BIAS, F32),
        ],
        scratch_shapes=halves(1152),
        compiler_params=PARAMS,
        cost_estimate=cost(24),
        name="inner_windows",
    )(x, x, x, x, y, y, y, y, *consts, pair_bias, last)


def edge_windows(x, y, e, s, c, consts, bias, sums):
    levels = x.shape[0]

    def both(lon, lat):
        return pl.BlockSpec((2, 2, lon, lat, D), lambda i: (0, i, 0, 0, 0))

    def one(lon, lat):
        return pl.BlockSpec((2, lon, lat, D), lambda i: (i, 0, 0, 0))

    return pl.pallas_call(
        edge_kernel,
        grid=(levels // 2,),
        in_specs=[one(36, 24), one(36, 24), both(6, 24), both(36, 3), both(6, 3)]
        + const_specs()
        + [whole(BIAS), whole(GW), whole(GB)],
        out_specs=[one(12, 32), one(24, 16), whole((ROWS, 128))],
        out_shape=[
            jax.ShapeDtypeStruct((levels, 12, 32, D), BF16),
            jax.ShapeDtypeStruct((levels, 24, 16, D), BF16),
            jax.ShapeDtypeStruct((ROWS, 128), F32),
        ],
        scratch_shapes=[pltpu.VMEM(GW, F32), pltpu.VMEM(GB, F32)] + halves(1536),
        compiler_params=PARAMS,
        cost_estimate=cost(24),
        name="edge_windows",
    )(x, y, e, s, c, *consts, bias, *sums)


def assemble_kernel(inner, oe, os_, gl, gs, gc, out_ref):
    row = lax.broadcasted_iota(jnp.int32, (8, D), 0)

    def head(got, tile):
        wide = jnp.concatenate([got.astype(F32), jnp.zeros((5, D), F32)], axis=0)
        return jnp.where(row < 3, wide, tile)

    for lon in range(36):
        if lon < 6:
            rows = gl[0, lon].astype(F32)
            got = gc[0, lon]
        elif lon < 30:
            rows = inner[0, lon - 6].astype(F32)
            tail = os_[0, lon - 6].astype(F32)[:8]
            rows = jnp.concatenate([rows[:16], jnp.where(row >= 5, tail, rows[16:])], axis=0)
            got = gs[0, lon - 6]
        else:
            rows = oe[0, lon - 30].astype(F32)[:24]
            got = gs[0, lon - 6]
        out_ref[0, lon] = jnp.concatenate([head(got, rows[:8]), rows[8:]], axis=0).astype(BF16)


def assemble(inner, oe, os_, got_lon, got_lat, got_both):
    levels = inner.shape[0]

    def one(lon, lat):
        return pl.BlockSpec((1, lon, lat, D), lambda i: (i, 0, 0, 0))

    return pl.pallas_call(
        assemble_kernel,
        grid=(levels,),
        in_specs=[one(24, 24), one(12, 32), one(24, 16), one(6, 24), one(30, 3), one(6, 3)],
        out_specs=one(36, 24),
        out_shape=jax.ShapeDtypeStruct((levels, 36, 24, D), BF16),
        compiler_params=PARAMS,
        cost_estimate=pl.CostEstimate(flops=0, bytes_accessed=6_000_000, transcendentals=0),
        name="assemble",
    )(inner, oe, os_, got_lon, got_lat, got_both)


def finish_kernel(factor, sum_ref, gain_ref, w_ref, gq_ref, go_ref, gb_ref, gg_ref):
    both = jnp.concatenate(
        [sum_ref[D * t : D * t + D].astype(F32) for t in range(6)], axis=1
    )
    gq = both[:, : 3 * D] * factor
    gq_ref[...] = gq
    go_ref[...] = both[:, 3 * D :] * factor
    products = (gq * w_ref[...].astype(F32)).T
    gg_ref[...] = jnp.sum(products, axis=0, keepdims=True) / gain_ref[...]
    base = WROWS + 6 * W
    rest = sum_ref[base : base + W].astype(F32)
    for h in range(HEADS):
        main = sum_ref[WROWS + W * h : WROWS + W * h + W].astype(F32)
        turned = jnp.concatenate([main, rest[:, 16 * h : 16 * h + 16]], axis=1)
        gb_ref[h] = regroup(regroup(turned, True).T, True)


def finish(sums, gain_row, qkv_weight, factor):
    return pl.pallas_call(
        lambda *refs: finish_kernel(factor, *refs),
        out_shape=[
            jax.ShapeDtypeStruct((D, 3 * D), F32),
            jax.ShapeDtypeStruct((D, D), F32),
            jax.ShapeDtypeStruct((HEADS, W, W), F32),
            jax.ShapeDtypeStruct((1, D), F32),
        ],
        compiler_params=PARAMS,
        name="finish_sums",
    )(sums, gain_row, qkv_weight)


def make_consts(ln_gain, qkv_weight, out_weight):
    wqkv = jnp.pad(qkv_weight.reshape(D, 3, D), ((0, 0), (0, 0), (0, 64))).reshape(D, 768)
    return [ln_gain.reshape(1, D), wqkv, qkv_weight.T, out_weight.T]


def shift(value, axes, steps):
    sizes = [lax.axis_size(a) for a in axes]
    total = 1
    for s in sizes:
        total *= s
    pairs = []
    for source in range(total):
        rest, place = source, []
        for s in reversed(sizes):
            place.append(rest % s)
            rest //= s
        place.reverse()
        target = 0
        for p, s, d in zip(place, sizes, steps):
            target = target * s + (p + d) % s
        pairs.append((source, target))
    return lax.ppermute(value, axes if len(axes) > 1 else axes[0], pairs)


def moved(value, axis, to_of):
    count = lax.axis_size(axis)
    return lax.ppermute(value, axis, [(n, to_of(n)) for n in range(count)])


def flip(value, axis, bits):
    return moved(value, axis, lambda n: n ^ bits)


def lon_core(n):
    return n % 2


def sum_over_devices(sums):
    lon = lax.axis_index("lon")
    core = lon % 2
    y = (lon // 2) % 4
    halves = sums.reshape(2, ROWS // 2, 128)
    low = halves.astype(BF16)
    got = flip(lax.dynamic_index_in_dim(low, 1 - core, 0, keepdims=False), "lon", 1)
    mine = lax.dynamic_index_in_dim(halves, core, 0, keepdims=False) + got.astype(F32)
    quarters = mine.reshape(4, ROWS // 8, 128)
    qlow = quarters.astype(BF16)
    total = lax.dynamic_index_in_dim(quarters, y, 0, keepdims=False)
    for step in range(1, 4):
        piece = lax.dynamic_index_in_dim(qlow, y ^ step, 0, keepdims=False)
        total = total + flip(piece, "lon", 2 * step).astype(F32)
    low = total.astype(BF16)
    for step in range(1, 4):
        total = total + flip(low, "lat", 2 * step).astype(F32)
    low = total.astype(BF16)
    total = (
        total
        + flip(low, "lat", 1).astype(F32)
        + flip(low, "lon", 8).astype(F32)
        + shift_x(low).astype(F32)
    )
    low = total.astype(BF16)
    others = [low] + [flip(low, "lon", 2 * step) for step in range(1, 4)]
    stacked = jnp.stack(others)
    line = jnp.concatenate(
        [lax.dynamic_index_in_dim(stacked, y ^ n, 0, keepdims=True) for n in range(4)], axis=0
    )
    other = flip(line, "lon", 1)
    pair = jnp.stack([line, other])
    return jnp.concatenate(
        [
            lax.dynamic_index_in_dim(pair, core ^ n, 0, keepdims=False).reshape(ROWS // 2, 128)
            for n in range(2)
        ],
        axis=0,
    )


def shift_x(value):
    lat = lax.axis_size("lat")
    total = lax.axis_size("lon") * lat
    pairs = []
    for source in range(total):
        lon_at, lat_at = source // lat, source % lat
        pairs.append((source, (lon_at ^ 8) * lat + (lat_at ^ 1)))
    return lax.ppermute(value, ("lon", "lat"), pairs)


def local(tokens, cotangent, ln_gain, qkv_weight, out_weight, pair_bias):
    levels, lat_count, lon_count, _ = tokens.shape
    x = jnp.transpose(tokens, (0, 2, 1, 3))
    y = jnp.transpose(cotangent, (0, 2, 1, 3))
    s = shift(jnp.stack([x[:, :, :HALF_LAT], y[:, :, :HALF_LAT]]), ("lat",), (-1,))
    e = shift(jnp.stack([x[:, :HALF_LON], y[:, :HALF_LON]]), ("lon",), (-1,))
    c = shift(
        jnp.stack([x[:, :HALF_LON, :HALF_LAT], y[:, :HALF_LON, :HALF_LAT]]), ("lon", "lat"), (-1, -1)
    )
    consts = make_consts(ln_gain, qkv_weight, out_weight)
    last = (lax.axis_index("lat") == lax.axis_size("lat") - 1).astype(jnp.int32).reshape(1, 1)
    inner, gw, gb, bias = inner_windows(x, y, consts, pair_bias, last)
    oe, os_, sums = edge_windows(x, y, e, s, c, consts, bias, (gw, gb))
    back_lat = jnp.concatenate([os_[:, :, 8:11], oe[:, :HALF_LON, 24:27]], axis=1)
    got_lat = shift(back_lat, ("lat",), (1,))
    got_lon = shift(oe[:, HALF_LON:, :24], ("lon",), (1,))
    got_both = shift(oe[:, HALF_LON:, 24:27], ("lon", "lat"), (1, 1))
    sums = sum_over_devices(sums)
    grad_x = assemble(inner, oe, os_, got_lon, got_lat, got_both)
    factor = float(
        levels * lat_count * lax.axis_size("lat") * lon_count * lax.axis_size("lon")
    ) ** (-0.5)
    gq, go, gbias, gg = finish(sums, ln_gain.reshape(1, D), qkv_weight, factor)
    return (jnp.transpose(grad_x, (0, 2, 1, 3)), gq, go, gbias, gg.reshape(D))


def solution(mesh):
    placed = (P(None, "lat", "lon", None), P(None, "lat", "lon", None), P(), P(), P(), P())
    return jax.shard_map(
        local,
        mesh=mesh,
        in_specs=placed,
        out_specs=(P(None, "lat", "lon", None), P(), P(), P(), P()),
        check_vma=False,
    )
```

time: 191 us -> 151 us (0.79)
  Pallas kernels: 99.1 us -> 65.9 us
  waiting for transfers between devices: 23.6 us -> 33.2 us
  local copies, waits for them, and re-layouts: 20.6 us -> 13.5 us
  other arithmetic: 10.4 us -> 4.1 us
  starting transfers between devices: 35.5 us -> 32.5 us
    pallas_call x3, Pallas kernels: 96.7 us -> 63.3 us  [the longest x1 30.6 us: edge_windows(): pl.pallas_call(edge_kernel, grid=(levels // 2,), in_specs=[one(36, 24), o...]
    ppermute x9 -> x6, waiting for transfers between devices: 11.7 us -> 18.3 us  [shift(): return lax.ppermute(value, axes if len(axes) > 1 else axes[0], pairs)]
    another operation x1 -> x4, local copies, waits for them, and re-layouts: 0.01 us -> 4.86 us  [the longest x2 2.45 us: local(): jnp.stack([x[:, :, :HALF_LAT], y[:, :, :HALF_LAT]])]
    concatenate x2 -> x1, other arithmetic: 5.1 us -> 0.35 us  [local(): jnp.concatenate([os_[:, :, 8:11], oe[:, :HALF_LON, 24:27]], axis=1)]
    unnamed x28 -> x18, local copies, waits for them, and re-layouts: 7.21 us -> 2.58 us
    slice x15 -> x3, local copies, waits for them, and re-layouts: 5.38 us -> 1.39 us  [the longest x1 1.26 us: local(): os_[:, :, 8:11]]
    ppermute x9 -> x6, starting transfers between devices: 17.1 us -> 14.4 us  [shift(): return lax.ppermute(value, axes if len(axes) > 1 else axes[0], pairs)]
    ppermute x13, waiting for transfers between devices: 11.7 us -> 14.1 us  [moved(): return lax.ppermute(value, axis, [(n, to_of(n)) for n in range(count)])]
  transfers between devices with their start and end apart: 23 -> 20, of which waited for: 12 -> 10; matrix products, arithmetic and copies ran while one was open for 11% -> 7% of each run, Pallas kernels for 38% -> 22%
where the time goes in v2:
time: 151 us; the launch traced here: 150 us
  Pallas kernels  65.9 us (44%)
  waiting for transfers between devices  33.2 us (22%)
  starting transfers between devices  32.5 us (22%)
  local copies, waits for them, and re-layouts  13.5 us (9%)
  other arithmetic  4.1 us (3%)
    pallas_call x1, Pallas kernels, edge_windows(): pl.pallas_call(edge_kernel, grid=(levels // 2,), in_specs=[one(36, 24), o...  30.6 us
    pallas_call x1, Pallas kernels, inner_windows(): pl.pallas_call(inner_kernel, grid=(levels // 2,), in_specs=four + four +...  25.8 us
    ppermute x6, waiting for transfers between devices, shift(): return lax.ppermute(value, axes if len(axes) > 1 else axes[0], pairs)  18.3 us
    ppermute x13, starting transfers between devices, moved(): return lax.ppermute(value, axis, [(n, to_of(n)) for n in range(count)])  15.7 us
    ppermute x6, starting transfers between devices, shift(): return lax.ppermute(value, axes if len(axes) > 1 else axes[0], pairs)  14.4 us
    ppermute x13, waiting for transfers between devices, moved(): return lax.ppermute(value, axis, [(n, to_of(n)) for n in range(count)])  14.1 us
    pallas_call x1, Pallas kernels, assemble(): pl.pallas_call(assemble_kernel, grid=(levels,), in_specs=[one(24, 24), on...  6.94 us
  transfers between devices with their start and end apart: 20, of which 10 were waited for; matrix products, arithmetic and copies ran while one was open for 7% of the time, Pallas kernels for 22%

profile of v2, /device:TPU:0, one launch (start us, length us, event | category | flops | bytes accessed | tf_op | source)
XLA Modules:
  0.0 150.1 jit_solution(7274099185489473691)
XLA Ops:
  0.6 1.3 slice_bitcast_fusion.2
  2.2 3.5 %collective-permute-start = (bf16[2,8,6,24,192]{4,3,2,1,0:T(8,128)(2,1)S(1)}, bf16[2,8,6,24,192]{4,3,2,1,0:T(8,128)(2,1)}, u32[]{:S(2)}, u32[]{:S(2)}) collective-permute-start(bf16[2,8,6,24,192]{4,3,2,1,0:T(8,128)(2,1)S(1)} %pad_maximum_fusion), channel_id=1, source_target_pairs={{0,120},{8,0},{16,8},{24,16},{32,24},{40,32},{48,40},{56,48},{64,5... | collective-permute-start | bytes 2654216 | tf_op jit(solution)/shard_map/ppermute | solution.py:494
  5.7 1.9 %slice_bitcast_fusion = (bf16[1,8,36,3,192]{4,3,2,1,0:T(4,128)(2,1)S(1)}, bf16[1,8,36,3,192]{4,3,2,1,0:T(4,128)(2,1)S(1)}) fusion(bf16[8,36,24,192]{3,2,1,0:T(8,128)(2,1)} %bitcast.59, bf16[8,36,24,192]{3,2,1,0:T(8,128)(2,1)} %bitcast.51), kind=kLoop, calls=%fused_computation.6 | loop fusion | bytes 1327104 | tf_op jit(solution)/shard_map/stack | solution.py:565
  7.7 0.9 pad_maximum_fusion.1
  9.1 6.3 %collective-permute-start.1 = (bf16[2,8,36,3,192]{4,1,3,2,0:T(8,128)(2,1)S(1)}, bf16[2,8,36,3,192]{4,1,3,2,0:T(8,128)(2,1)}, u32[]{:S(2)}, u32[]{:S(2)}) collective-permute-start(bf16[2,8,36,3,192]{4,1,3,2,0:T(8,128)(2,1)S(1)} %copy.21), channel_id=1, source_target_pairs={{0,7},{1,0},{2,1},{3,2},{4,3},{5,4},{6,5},{7,6},{8,15},{9,8},{10,9... | collective-permute-start | bytes 1990664 | tf_op jit(solution)/shard_map/ppermute | solution.py:494
  15.4 1.1 slice_bitcast_fusion.4
  18.9 25.8 %inner_windows.1 = (bf16[8,24,24,192]{3,2,1,0:T(8,128)(2,1)}, f32[4,192,192]{2,1,0:T(8,128)}, f32[144,896]{1,0:T(8,128)}, f32[2,144,896]{2,1,0:T(8,128)}) custom-call(bf16[8,36,24,192]{3,2,1,0:T(8,128)(2,1)} %bitcast.53, bf16[8,36,24,192]{3,2,1,0:T(8,128)(2,1)} %bitcast.54, bf16[8,36,24,192]{3,2,1,0:T(8,128)(2,1)} %bitcast.55, ...), custom_call_target="tpu_custom_call" | custom-call | flops 5096079360 | bytes 3981312 | tf_op jit(solution)/shard_map/inner_windows/pallas_call | solution.py:351
  44.8 2.6 %copy.22.s = bf16[2,8,36,3,192]{4,3,2,1,0:T(4,128)(2,1)} copy(bf16[2,8,36,3,192]{4,1,3,2,0:T(8,128)(2,1)} %collective-permute-done.1) | data formatting | bytes 1327104 | tf_op jit(solution)/shard_map/ppermute | solution.py:494
  48.1 30.6 %edge_windows.1 = (bf16[8,12,32,192]{3,2,1,0:T(8,128)(2,1)}, bf16[8,24,16,192]{3,2,1,0:T(8,128)(2,1)}, f32[2176,128]{1,0:T(8,128)}) custom-call(bf16[8,36,24,192]{3,2,1,0:T(8,128)(2,1)} %bitcast.57, bf16[8,36,24,192]{3,2,1,0:T(8,128)(2,1)} %bitcast.65, bf16[2,8,6,24,192]{4,3,2,1,0:T(8,128)(2,1)} %collective-permute-done.e, ...), custom_call_target="tpu_custom_call" | custom-call | flops 5096079360 | bytes 3981312 | tf_op jit(solution)/shard_map/edge_windows/pallas_call | solution.py:383
  78.7 1.1 fusion
  80.4 1.2 collective-permute-done.6
  81.6 1.1 bitcast_add_fusion
  83.2 3.8 %collective-permute-start.7 = (bf16[272,128]{1,0:T(8,128)(2,1)S(1)}, bf16[272,128]{1,0:T(8,128)(2,1)S(1)}, u32[]{:S(2)}, u32[]{:S(2)}) collective-permute-start(bf16[272,128]{1,0:T(8,128)(2,1)S(1)} %get-tuple-element.39), channel_id=1, source_target_pairs={{0,16},{8,24},{16,0},{24,8},{32,48},{40,56},{48,32},{56,40},{64,80... | collective-permute-start | bytes 208904 | tf_op jit(solution)/shard_map/ppermute | solution.py:499
  87.0 3.1 %collective-permute-done.9 = bf16[272,128]{1,0:T(8,128)(2,1)S(1)} collective-permute-done((bf16[272,128]{1,0:T(8,128)(2,1)S(1)}, bf16[272,128]{1,0:T(8,128)(2,1)S(1)}, u32[]{:S(2)}, u32[]{:S(2)}) %collective-permute-start.9) | collective-permute-done | bytes 69664 | tf_op jit(solution)/shard_map/ppermute | solution.py:499
  90.7 2.7 %collective-permute-start.12 = (bf16[272,128]{1,0:T(8,128)(2,1)S(1)}, bf16[272,128]{1,0:T(8,128)(2,1)S(1)}, u32[]{:S(2)}, u32[]{:S(2)}) collective-permute-start(bf16[272,128]{1,0:T(8,128)(2,1)S(1)} %get-tuple-element.27), channel_id=1, source_target_pairs={{0,6},{1,7},{2,4},{3,5},{4,2},{5,3},{6,0},{7,1},{8,14},{9,15},{10,... | collective-permute-start | bytes 208904 | tf_op jit(solution)/shard_map/ppermute | solution.py:499
  93.4 1.4 collective-permute-start.10
  94.9 1.4 collective-permute-done.12
  96.3 2.9 %collective-permute-done.11 = bf16[272,128]{1,0:T(8,128)(2,1)S(1)} collective-permute-done((bf16[272,128]{1,0:T(8,128)(2,1)S(1)}, bf16[272,128]{1,0:T(8,128)(2,1)S(1)}, u32[]{:S(2)}, u32[]{:S(2)}) %collective-permute-start.11) | collective-permute-done | bytes 69664 | tf_op jit(solution)/shard_map/ppermute | solution.py:499
  99.3 2.3 %collective-permute-start.15 = (bf16[272,128]{1,0:T(8,128)(2,1)S(1)}, bf16[272,128]{1,0:T(8,128)(2,1)S(1)}, u32[]{:S(2)}, u32[]{:S(2)}) collective-permute-start(bf16[272,128]{1,0:T(8,128)(2,1)S(1)} %fusion.5), channel_id=1, source_target_pairs={{0,65},{1,64},{2,67},{3,66},{4,69},{5,68},{6,71},{7,70},{8,73},{9,... | collective-permute-start | bytes 208904 | tf_op jit(solution)/shard_map/ppermute | solution.py:558
  101.8 2.3 %collective-permute-start.13 = (bf16[272,128]{1,0:T(8,128)(2,1)S(1)}, bf16[272,128]{1,0:T(8,128)(2,1)S(1)}, u32[]{:S(2)}, u32[]{:S(2)}) collective-permute-start(bf16[272,128]{1,0:T(8,128)(2,1)S(1)} %fusion.5), channel_id=1, source_target_pairs={{0,1},{1,0},{2,3},{3,2},{4,5},{5,4},{6,7},{7,6},{8,9},{9,8},{10,11... | collective-permute-start | bytes 208904 | tf_op jit(solution)/shard_map/ppermute | solution.py:499
  104.9 1.0 collective-permute-done.14
  105.9 1.7 %collective-permute-done.13 = bf16[272,128]{1,0:T(8,128)(2,1)S(1)} collective-permute-done((bf16[272,128]{1,0:T(8,128)(2,1)S(1)}, bf16[272,128]{1,0:T(8,128)(2,1)S(1)}, u32[]{:S(2)}, u32[]{:S(2)}) %collective-permute-start.13) | collective-permute-done | bytes 69664 | tf_op jit(solution)/shard_map/ppermute | solution.py:499
  107.7 2.0 %collective-permute-start.18 = (bf16[272,128]{1,0:T(8,128)(2,1)S(1)}, bf16[272,128]{1,0:T(8,128)(2,1)S(1)}, u32[]{:S(2)}, u32[]{:S(2)}) collective-permute-start(bf16[272,128]{1,0:T(8,128)(2,1)S(1)} %add_convert_fusion), channel_id=1, source_target_pairs={{0,48},{8,56},{16,32},{24,40},{32,16},{40,24},{48,0},{56,8},{64,11... | collective-permute-start | bytes 208904 | tf_op jit(solution)/shard_map/ppermute | solution.py:499
  109.7 1.0 collective-permute-start.17
  110.7 1.1 collective-permute-start.16
  112.1 1.3 slice.37
  113.4 2.1 %collective-permute-done.17 = bf16[272,128]{1,0:T(8,128)(2,1)S(1)} collective-permute-done((bf16[272,128]{1,0:T(8,128)(2,1)S(1)}, bf16[272,128]{1,0:T(8,128)(2,1)S(1)}, u32[]{:S(2)}, u32[]{:S(2)}) %collective-permute-start.17) | collective-permute-done | bytes 69664 | tf_op jit(solution)/shard_map/ppermute | solution.py:499
  116.1 2.3 %collective-permute-start.4 = (bf16[8,30,3,192]{3,2,1,0:T(4,128)(2,1)S(1)}, bf16[8,30,3,192]{3,2,1,0:T(4,128)(2,1)S(1)}, u32[]{:S(2)}, u32[]{:S(2)}) collective-permute-start(bf16[8,30,3,192]{3,2,1,0:T(4,128)(2,1)S(1)} %pad_maximum_fusion.3), channel_id=1, source_target_pairs={{0,1},{1,2},{2,3},{3,4},{4,5},{5,6},{6,7},{7,0},{8,9},{9,10},{10,1... | collective-permute-start | bytes 829448 | tf_op jit(solution)/shard_map/ppermute | solution.py:494
  118.4 1.8 %collective-permute-start.5 = (bf16[8,6,3,192]{3,2,1,0:T(4,128)(2,1)S(1)}, bf16[8,6,3,192]{3,2,1,0:T(4,128)(2,1)S(1)}, u32[]{:S(2)}, u32[]{:S(2)}) collective-permute-start(bf16[8,6,3,192]{3,2,1,0:T(4,128)(2,1)S(1)} %get-tuple-element.29), channel_id=1, source_target_pairs={{0,9},{1,10},{2,11},{3,12},{4,13},{5,14},{6,15},{7,8},{8,17},{9,18... | collective-permute-start | bytes 165896 | tf_op jit(solution)/shard_map/ppermute | solution.py:494
  120.2 18.3 %collective-permute-done.5.gc = bf16[8,6,3,192]{3,2,1,0:T(4,128)(2,1)S(1)} collective-permute-done((bf16[8,6,3,192]{3,2,1,0:T(4,128)(2,1)S(1)}, bf16[8,6,3,192]{3,2,1,0:T(4,128)(2,1)S(1)}, u32[]{:S(2)}, u32[]{:S(2)}) %collective-permute-start.5) | collective-permute-done | bytes 55328 | tf_op jit(solution)/shard_map/ppermute | solution.py:494
  139.5 6.9 %assemble.1 = bf16[8,36,24,192]{3,2,1,0:T(8,128)(2,1)} custom-call(bf16[8,24,24,192]{3,2,1,0:T(8,128)(2,1)} %get-tuple-element.16.inner, bf16[8,12,32,192]{3,2,1,0:T(8,128)(2,1)} %get-tuple-element.20.oe, bf16[8,24,16,192]{3,2,1,0:T(8,128)(2,1)} %get-tuple-element.21.os_, bf16[8,6,24,192]{3,2,1,0:T(8,128)(2,1)} %copy-done.3, ...), custom_call_target="tpu_custom_call" | custom-call | bytes 6000000 | tf_op jit(solution)/shard_map/assemble/pallas_call | solution.py:430
  147.5 2.6 %finish_sums.1 = (f32[192,576]{1,0:T(8,128)}, f32[192,192]{1,0:T(8,128)}, f32[6,144,144]{2,1,0:T(8,128)}, f32[1,192]{1,0:T(1,128)}) custom-call(bf16[2176,128]{1,0:T(8,128)(2,1)} %pad_maximum_fusion.2.refs_0_, f32[1,192]{1,0:T(1,128)} %bitcast.86, bf16[192,576]{1,0:T(8,128)(2,1)} %refs_2_.1), custom_call_target="tpu_custom_call" | custom-call | tf_op jit(solution)/shard_map/finish_sums/pallas_call | solution.py:460
  (56 shorter events, 9.5 us)
Async XLA Ops:
  2.2 45.2 %collective-permute-start = (bf16[2,8,6,24,192]{4,3,2,1,0:T(8,128)(2,1)S(1)}, bf16[2,8,6,24,192]{4,3,2,1,0:T(8,128)(2,1)}, u32[]{:S(2)}, u32[]{:S(2)}) collective-permute-start(bf16[2,8,6,24,192]{4,3,2,1,0:T(8,128)(2,1)S(1)} %pad_maximum_fusion), channel_id=1, source_target_pairs={{0,120},{8,0},{16,8},{24,16},{32,24},{40,32},{48,40},{56,48},{64,5... | collective-permute-start | bytes 2654216 | tf_op jit(solution)/shard_map/ppermute | solution.py:494
  8.6 8.5 %copy-start.2 = (bf16[192,576]{1,0:T(8,128)(2,1)S(1)}, bf16[192,576]{1,0:T(8,128)(2,1)}, u32[]{:S(2)}) copy-start(bf16[192,576]{1,0:T(8,128)(2,1)} %refs_2_.1) | copy-start | bytes 663556
  9.1 35.6 %collective-permute-start.1 = (bf16[2,8,36,3,192]{4,1,3,2,0:T(8,128)(2,1)S(1)}, bf16[2,8,36,3,192]{4,1,3,2,0:T(8,128)(2,1)}, u32[]{:S(2)}, u32[]{:S(2)}) collective-permute-start(bf16[2,8,36,3,192]{4,1,3,2,0:T(8,128)(2,1)S(1)} %copy.21), channel_id=1, source_target_pairs={{0,7},{1,0},{2,1},{3,2},{4,3},{5,4},{6,5},{7,6},{8,15},{9,8},{10,9... | collective-permute-start | bytes 1990664 | tf_op jit(solution)/shard_map/ppermute | solution.py:494
  16.5 1.7 %copy-start.6 = (bf16[192,192]{1,0:T(8,128)(2,1)S(1)}, bf16[192,192]{1,0:T(8,128)(2,1)}, u32[]{:S(2)}) copy-start(bf16[192,192]{1,0:T(8,128)(2,1)} %param.10) | copy-start | bytes 221188
  16.7 30.7 %collective-permute-start.2 = (bf16[2,8,6,3,192]{4,3,2,1,0:T(4,128)(2,1)S(1)}, bf16[2,8,6,3,192]{4,3,2,1,0:T(4,128)(2,1)S(1)}, u32[]{:S(2)}, u32[]{:S(2)}) collective-permute-start(bf16[2,8,6,3,192]{4,3,2,1,0:T(4,128)(2,1)S(1)} %pad_maximum_fusion.6), channel_id=1, source_target_pairs={{0,127},{1,120},{2,121},{3,122},{4,123},{5,124},{6,125},{7,126},{8... | collective-permute-start | bytes 331784 | tf_op jit(solution)/shard_map/ppermute | solution.py:494
  17.3 1.7 %copy-start.1 = (bf16[192,576]{0,1:T(8,128)(2,1)}, bf16[192,576]{0,1:T(8,128)(2,1)S(1)}, u32[]{:S(2)}) copy-start(bf16[192,576]{0,1:T(8,128)(2,1)S(1)} %copy.17) | copy-start | bytes 663556
  47.4 0.7 copy-start.7
  79.8 1.8 %collective-permute-start.6 = (bf16[1088,128]{1,0:T(8,128)(2,1)S(1)}, bf16[1088,128]{1,0:T(8,128)(2,1)S(1)}, u32[]{:S(2)}, u32[]{:S(2)}) collective-permute-start(bf16[1088,128]{1,0:T(8,128)(2,1)S(1)} %fusion), channel_id=1, source_target_pairs={{0,8},{8,0},{16,24},{24,16},{32,40},{40,32},{48,56},{56,48},{64,72... | collective-permute-start | bytes 835592 | tf_op jit(solution)/shard_map/ppermute | solution.py:499
  82.8 29.1 %copy-start = (bf16[8,12,32,192]{3,2,1,0:T(8,128)(2,1)S(1)}, bf16[8,12,32,192]{3,2,1,0:T(8,128)(2,1)}, u32[]{:S(2)}) copy-start(bf16[8,12,32,192]{3,2,1,0:T(8,128)(2,1)} %get-tuple-element.20.oe) | copy-start | bytes 3538948
  82.8 7.2 %collective-permute-start.9 = (bf16[272,128]{1,0:T(8,128)(2,1)S(1)}, bf16[272,128]{1,0:T(8,128)(2,1)S(1)}, u32[]{:S(2)}, u32[]{:S(2)}) collective-permute-start(bf16[272,128]{1,0:T(8,128)(2,1)S(1)} %get-tuple-element.40), channel_id=1, source_target_pairs={{0,48},{8,56},{16,32},{24,40},{32,16},{40,24},{48,0},{56,8},{64,11... | collective-permute-start | bytes 208904 | tf_op jit(solution)/shard_map/ppermute | solution.py:499
  82.9 7.2 %collective-permute-start.8 = (bf16[272,128]{1,0:T(8,128)(2,1)S(1)}, bf16[272,128]{1,0:T(8,128)(2,1)S(1)}, u32[]{:S(2)}, u32[]{:S(2)}) collective-permute-start(bf16[272,128]{1,0:T(8,128)(2,1)S(1)} %get-tuple-element.41), channel_id=1, source_target_pairs={{0,32},{8,40},{16,48},{24,56},{32,0},{40,8},{48,16},{56,24},{64,96... | collective-permute-start | bytes 208904 | tf_op jit(solution)/shard_map/ppermute | solution.py:499
  83.2 7.4 %collective-permute-start.7 = (bf16[272,128]{1,0:T(8,128)(2,1)S(1)}, bf16[272,128]{1,0:T(8,128)(2,1)S(1)}, u32[]{:S(2)}, u32[]{:S(2)}) collective-permute-start(bf16[272,128]{1,0:T(8,128)(2,1)S(1)} %get-tuple-element.39), channel_id=1, source_target_pairs={{0,16},{8,24},{16,0},{24,8},{32,48},{40,56},{48,32},{56,40},{64,80... | collective-permute-start | bytes 208904 | tf_op jit(solution)/shard_map/ppermute | solution.py:499
  90.7 5.6 %collective-permute-start.12 = (bf16[272,128]{1,0:T(8,128)(2,1)S(1)}, bf16[272,128]{1,0:T(8,128)(2,1)S(1)}, u32[]{:S(2)}, u32[]{:S(2)}) collective-permute-start(bf16[272,128]{1,0:T(8,128)(2,1)S(1)} %get-tuple-element.27), channel_id=1, source_target_pairs={{0,6},{1,7},{2,4},{3,5},{4,2},{5,3},{6,0},{7,1},{8,14},{9,15},{10,... | collective-permute-start | bytes 208904 | tf_op jit(solution)/shard_map/ppermute | solution.py:499
  93.4 5.8 %collective-permute-start.11 = (bf16[272,128]{1,0:T(8,128)(2,1)S(1)}, bf16[272,128]{1,0:T(8,128)(2,1)S(1)}, u32[]{:S(2)}, u32[]{:S(2)}) collective-permute-start(bf16[272,128]{1,0:T(8,128)(2,1)S(1)} %get-tuple-element.27), channel_id=1, source_target_pairs={{0,4},{1,5},{2,6},{3,7},{4,0},{5,1},{6,2},{7,3},{8,12},{9,13},{10,... | collective-permute-start | bytes 208904 | tf_op jit(solution)/shard_map/ppermute | solution.py:499
  93.4 5.8 %collective-permute-start.10 = (bf16[272,128]{1,0:T(8,128)(2,1)S(1)}, bf16[272,128]{1,0:T(8,128)(2,1)S(1)}, u32[]{:S(2)}, u32[]{:S(2)}) collective-permute-start(bf16[272,128]{1,0:T(8,128)(2,1)S(1)} %get-tuple-element.27), channel_id=1, source_target_pairs={{0,2},{1,3},{2,0},{3,1},{4,6},{5,7},{6,4},{7,5},{8,10},{9,11},{10,... | collective-permute-start | bytes 208904 | tf_op jit(solution)/shard_map/ppermute | solution.py:499
  99.3 5.6 %collective-permute-start.15 = (bf16[272,128]{1,0:T(8,128)(2,1)S(1)}, bf16[272,128]{1,0:T(8,128)(2,1)S(1)}, u32[]{:S(2)}, u32[]{:S(2)}) collective-permute-start(bf16[272,128]{1,0:T(8,128)(2,1)S(1)} %fusion.5), channel_id=1, source_target_pairs={{0,65},{1,64},{2,67},{3,66},{4,69},{5,68},{6,71},{7,70},{8,73},{9,... | collective-permute-start | bytes 208904 | tf_op jit(solution)/shard_map/ppermute | solution.py:558
  101.6 4.3 %collective-permute-start.14 = (bf16[272,128]{1,0:T(8,128)(2,1)S(1)}, bf16[272,128]{1,0:T(8,128)(2,1)S(1)}, u32[]{:S(2)}, u32[]{:S(2)}) collective-permute-start(bf16[272,128]{1,0:T(8,128)(2,1)S(1)} %fusion.5), channel_id=1, source_target_pairs={{0,64},{8,72},{16,80},{24,88},{32,96},{40,104},{48,112},{56,120},{... | collective-permute-start | bytes 208904 | tf_op jit(solution)/shard_map/ppermute | solution.py:499
  101.8 5.8 %collective-permute-start.13 = (bf16[272,128]{1,0:T(8,128)(2,1)S(1)}, bf16[272,128]{1,0:T(8,128)(2,1)S(1)}, u32[]{:S(2)}, u32[]{:S(2)}) collective-permute-start(bf16[272,128]{1,0:T(8,128)(2,1)S(1)} %fusion.5), channel_id=1, source_target_pairs={{0,1},{1,0},{2,3},{3,2},{4,5},{5,4},{6,7},{7,6},{8,9},{9,8},{10,11... | collective-permute-start | bytes 208904 | tf_op jit(solution)/shard_map/ppermute | solution.py:499
  107.7 5.7 %collective-permute-start.18 = (bf16[272,128]{1,0:T(8,128)(2,1)S(1)}, bf16[272,128]{1,0:T(8,128)(2,1)S(1)}, u32[]{:S(2)}, u32[]{:S(2)}) collective-permute-start(bf16[272,128]{1,0:T(8,128)(2,1)S(1)} %add_convert_fusion), channel_id=1, source_target_pairs={{0,48},{8,56},{16,32},{24,40},{32,16},{40,24},{48,0},{56,8},{64,11... | collective-permute-start | bytes 208904 | tf_op jit(solution)/shard_map/ppermute | solution.py:499
  109.7 5.8 %collective-permute-start.17 = (bf16[272,128]{1,0:T(8,128)(2,1)S(1)}, bf16[272,128]{1,0:T(8,128)(2,1)S(1)}, u32[]{:S(2)}, u32[]{:S(2)}) collective-permute-start(bf16[272,128]{1,0:T(8,128)(2,1)S(1)} %add_convert_fusion), channel_id=1, source_target_pairs={{0,32},{8,40},{16,48},{24,56},{32,0},{40,8},{48,16},{56,24},{64,96... | collective-permute-start | bytes 208904 | tf_op jit(solution)/shard_map/ppermute | solution.py:499
  110.7 4.8 %collective-permute-start.16 = (bf16[272,128]{1,0:T(8,128)(2,1)S(1)}, bf16[272,128]{1,0:T(8,128)(2,1)S(1)}, u32[]{:S(2)}, u32[]{:S(2)}) collective-permute-start(bf16[272,128]{1,0:T(8,128)(2,1)S(1)} %add_convert_fusion), channel_id=1, source_target_pairs={{0,16},{8,24},{16,0},{24,8},{32,48},{40,56},{48,32},{56,40},{64,80... | collective-permute-start | bytes 208904 | tf_op jit(solution)/shard_map/ppermute | solution.py:499
  112.0 26.5 %collective-permute-start.3 = (bf16[8,6,24,192]{3,2,1,0:T(8,128)(2,1)S(1)}, bf16[8,6,24,192]{3,2,1,0:T(8,128)(2,1)S(1)}, u32[]{:S(2)}, u32[]{:S(2)}) collective-permute-start(bf16[8,6,24,192]{3,2,1,0:T(8,128)(2,1)S(1)} %slice.36), channel_id=1, source_target_pairs={{0,8},{8,16},{16,24},{24,32},{32,40},{40,48},{48,56},{56,64},{64,7... | collective-permute-start | bytes 1327112 | tf_op jit(solution)/shard_map/ppermute | solution.py:494
  115.7 30.8 %collective-permute-start.19 = (bf16[4,272,128]{2,1,0:T(8,128)(2,1)S(1)}, bf16[4,272,128]{2,1,0:T(8,128)(2,1)S(1)}, u32[]{:S(2)}, u32[]{:S(2)}) collective-permute-start(bf16[4,272,128]{2,1,0:T(8,128)(2,1)S(1)} %get-tuple-element.33), channel_id=1, source_target_pairs={{0,8},{8,0},{16,24},{24,16},{32,40},{40,32},{48,56},{56,48},{64,72... | collective-permute-start | bytes 835592 | tf_op jit(solution)/shard_map/ppermute | solution.py:499
  116.1 22.4 %collective-permute-start.4 = (bf16[8,30,3,192]{3,2,1,0:T(4,128)(2,1)S(1)}, bf16[8,30,3,192]{3,2,1,0:T(4,128)(2,1)S(1)}, u32[]{:S(2)}, u32[]{:S(2)}) collective-permute-start(bf16[8,30,3,192]{3,2,1,0:T(4,128)(2,1)S(1)} %pad_maximum_fusion.3), channel_id=1, source_target_pairs={{0,1},{1,2},{2,3},{3,4},{4,5},{5,6},{6,7},{7,0},{8,9},{9,10},{10,1... | collective-permute-start | bytes 829448 | tf_op jit(solution)/shard_map/ppermute | solution.py:494
  118.4 20.1 %collective-permute-start.5 = (bf16[8,6,3,192]{3,2,1,0:T(4,128)(2,1)S(1)}, bf16[8,6,3,192]{3,2,1,0:T(4,128)(2,1)S(1)}, u32[]{:S(2)}, u32[]{:S(2)}) collective-permute-start(bf16[8,6,3,192]{3,2,1,0:T(4,128)(2,1)S(1)} %get-tuple-element.29), channel_id=1, source_target_pairs={{0,9},{1,10},{2,11},{3,12},{4,13},{5,14},{6,15},{7,8},{8,17},{9,18... | collective-permute-start | bytes 165896 | tf_op jit(solution)/shard_map/ppermute | solution.py:494
  138.5 0.6 copy-start.5
  138.5 0.8 copy-start.4
  138.5 1.0 copy-start.3

commit v3 on v2

--- a/solution.py
+++ b/solution.py
@@ -149,6 +149,7 @@
 
 
 STAGGER = 4
+EARLY = 3
 
 
 def run_windows(windows, gw_ref):
@@ -232,7 +233,33 @@
     bias_ref[1] = jnp.where(apart, F32(-1e30), flat)
 
 
-def inner_kernel(
+def start_windows(scratch, xs, ys, place):
+    for lv in range(2):
+        for lon in range(24):
+            keep(scratch[0], scratch[1], place(lv, lon), xs[lon // 6][lv, lon % 6])
+            keep(scratch[2], scratch[3], place(lv, lon), ys[lon // 6][lv, lon % 6])
+
+
+def inner_steps(xs, ys, consts, bias, dx_ref, gw_ref, gb_ref, scratch):
+    def place(lv, lon):
+        return 24 * (24 * (lon // 12) + 12 * lv + lon % 12)
+
+    start_windows(scratch, xs, ys, place)
+    refs = dict(zip(("gain", "wqkv", "wqkv_t", "wout_t"), consts), bias=bias, gb=gb_ref)
+    run_windows(
+        [
+            window_of(scratch, 576 * k + 3 + 6 * a, 24, 0, refs)
+            for k in range(2)
+            for a in range(3)
+        ],
+        gw_ref,
+    )
+    for lv in range(2):
+        for lon in range(24):
+            dx_ref[lv, lon] = kept(scratch[4], scratch[5], place(lv, lon), 24)
+
+
+def early_kernel(
     x0, x1, x2, x3, y0, y1, y2, y3, gain, wqkv, wqkv_t, wout_t, pair, last, dx_ref, gw_ref, gb_ref, bias_ref, *scratch
 ):
     @pl.when(pl.program_id(0) == 0)
@@ -241,71 +268,20 @@
         gb_ref[...] = jnp.zeros_like(gb_ref)
         lay_bias(pair, last, bias_ref)
 
-    xs, ys = (x0, x1, x2, x3), (y0, y1, y2, y3)
-
-    def place(lv, lon):
-        return 24 * (24 * (lon // 12) + 12 * lv + lon % 12)
-
-    for lv in range(2):
-        for lon in range(24):
-            keep(scratch[0], scratch[1], place(lv, lon), xs[lon // 6][lv, lon % 6])
-            keep(scratch[2], scratch[3], place(lv, lon), ys[lon // 6][lv, lon % 6])
-    refs = dict(
-        gain=gain, wqkv=wqkv, wqkv_t=wqkv_t, wout_t=wout_t, bias=bias_ref, gb=gb_ref
-    )
-    run_windows(
-        [
-            window_of(scratch, 576 * k + 3 + 6 * a, 24, 0, refs)
-            for k in range(2)
-            for a in range(3)
-        ],
-        gw_ref,
-    )
-    for lv in range(2):
-        for lon in range(24):
-            dx_ref[lv, lon] = kept(scratch[4], scratch[5], place(lv, lon), 24)
-
-
-def edge_kernel(
-    x, y, e, s, c, gain, wqkv, wqkv_t, wout_t, bias, gw_in, gb_in, oe_ref, os_ref, sum_ref, gw_ref, gb_ref, *scratch
+    consts = (gain, wqkv, wqkv_t, wout_t)
+    inner_steps((x0, x1, x2, x3), (y0, y1, y2, y3), consts, bias_ref, dx_ref, gw_ref, gb_ref, scratch)
+
+
+def late_kernel(
+    x0, x1, x2, x3, y0, y1, y2, y3, gain, wqkv, wqkv_t, wout_t, bias, gw_in, gb_in, _, dx_ref, sum_ref, gw_ref, gb_ref, *scratch
 ):
     @pl.when(pl.program_id(0) == 0)
     def _():
         gw_ref[...] = gw_in[...]
         gb_ref[...] = gb_in[...]
 
-    def place(lv, lon):
-        if lon < 12:
-            return 32 * (12 * lv + lon)
-        return 768 + 16 * (24 * ((lon - 12) // 12) + 12 * lv + lon % 12)
-
-    for n, own in enumerate((x, y)):
-        low, high = scratch[2 * n], scratch[2 * n + 1]
-        for lv in range(2):
-            for lon in range(6):
-                at = place(lv, lon)
-                keep(low, high, at, own[lv, 30 + lon])
-                keep(low, high, at + 24, s[n, lv, 30 + lon])
-                at = place(lv, 6 + lon)
-                keep(low, high, at, e[n, lv, lon])
-                keep(low, high, at + 24, c[n, lv, lon])
-            for lon in range(24):
-                at = place(lv, 12 + lon)
-                keep(low, high, at, own[lv, 6 + lon].astype(F32)[16:])
-                keep(low, high, at + 8, s[n, lv, 6 + lon])
-    refs = dict(
-        gain=gain, wqkv=wqkv, wqkv_t=wqkv_t, wout_t=wout_t, bias=bias, gb=gb_ref
-    )
-    run_windows(
-        [window_of(scratch, 3 + 6 * a, 32, int(a == 3), refs) for a in range(4)]
-        + [window_of(scratch, 768 + 384 * k + 5, 16, 1, refs) for k in range(2)],
-        gw_ref,
-    )
-    for lv in range(2):
-        for lon in range(12):
-            oe_ref[lv, lon] = kept(scratch[4], scratch[5], place(lv, lon), 32)
-        for lon in range(24):
-            os_ref[lv, lon] = kept(scratch[4], scratch[5], place(lv, 12 + lon), 16)
+    consts = (gain, wqkv, wqkv_t, wout_t)
+    inner_steps((x0, x1, x2, x3), (y0, y1, y2, y3), consts, bias, dx_ref, gw_ref, gb_ref, scratch)
 
     @pl.when(pl.program_id(0) == pl.num_programs(0) - 1)
     def _():
@@ -317,6 +293,112 @@
         sum_ref[WROWS + BROWS :] = jnp.zeros((ROWS - WROWS - BROWS, 128), F32)
 
 
+def split(rows):
+    return rows[:, :128], jnp.concatenate(
+        [rows[:, 128:], jnp.zeros((rows.shape[0], 64), F32)], axis=1
+    )
+
+
+def joined(low, high, at):
+    return jnp.concatenate([low[at, :], high[at, :][:, :64]], axis=1)
+
+
+def dense(left, right):
+    return jnp.concatenate(
+        [left, jnp.concatenate([right[:48], right[48:]], axis=1)], axis=0
+    ).astype(BF16)
+
+
+def undense(packed):
+    wide = packed.astype(F32)
+    tail = wide[96:]
+    high = jnp.concatenate([tail[:, :64], tail[:, 64:]], axis=0)
+    return wide[:96], jnp.concatenate([high, jnp.zeros((96, 64), F32)], axis=1)
+
+
+def pack_kernel(x, y, e_ref, s_ref, c_ref, low, high):
+    for n, own in enumerate((x, y)):
+        for lv in range(2):
+            base = 128 * (2 * n + lv)
+            for lon in range(36):
+                if lon < 6:
+                    e_ref[n, lv, lon] = own[lv, lon]
+                    at = pl.ds(base + 96 + lon, 3, stride=8)
+                else:
+                    at = pl.ds(base + lon - 6, 3, stride=32)
+                left, right = split(own[lv, lon].astype(F32)[:8])
+                low[at, :] = left[:3]
+                high[at, :] = right[:3]
+            s_ref[n, lv] = dense(low[base : base + 96, :], high[base : base + 96, :][:, :64])
+            c_ref[n, lv] = joined(low, high, pl.ds(base + 96, 24)).astype(BF16)
+
+
+def edge_kernel(
+    x, y, e, s, c, gain, wqkv, wqkv_t, wout_t, bias, gw_in, gb_in, oe_ref, os_ref, be_ref, bs_ref, bc_ref, gw_ref, gb_ref, *scratch
+):
+    @pl.when(pl.program_id(0) == 0)
+    def _():
+        gw_ref[...] = gw_in[...]
+        gb_ref[...] = gb_in[...]
+
+    def place(lv, lon):
+        if lon < 12:
+            return 32 * (12 * lv + lon)
+        return 768 + 16 * (24 * ((lon - 12) // 12) + 12 * lv + lon % 12)
+
+    def south(lv, t):
+        return [
+            pl.ds(place(lv, 12) + 8 + t, 12, stride=16),
+            pl.ds(place(lv, 24) + 8 + t, 12, stride=16),
+            pl.ds(place(lv, 0) + 24 + t, 6, stride=32),
+        ]
+
+    def corner(lv, t):
+        return pl.ds(place(lv, 6) + 24 + t, 6, stride=32)
+
+    for n, own in enumerate((x, y)):
+        low, high = scratch[2 * n], scratch[2 * n + 1]
+        for lv in range(2):
+            for lon in range(6):
+                keep(low, high, place(lv, lon), own[lv, 30 + lon])
+                keep(low, high, place(lv, 6 + lon), e[n, lv, lon])
+            for lon in range(24):
+                keep(low, high, place(lv, 12 + lon), own[lv, 6 + lon].astype(F32)[16:])
+            left, right = undense(s[n, lv])
+            cleft, cright = split(c[n, lv].astype(F32))
+            for t in range(3):
+                for m, at in enumerate(south(lv, t)):
+                    rows = slice(32 * t + 12 * m, 32 * t + min(12 * m + 12, 30))
+                    low[at, :] = left[rows]
+                    high[at, :] = right[rows]
+                low[corner(lv, t), :] = cleft[8 * t : 8 * t + 6]
+                high[corner(lv, t), :] = cright[8 * t : 8 * t + 6]
+    refs = dict(
+        gain=gain, wqkv=wqkv, wqkv_t=wqkv_t, wout_t=wout_t, bias=bias, gb=gb_ref
+    )
+    run_windows(
+        [window_of(scratch, 3 + 6 * a, 32, int(a == 3), refs) for a in range(4)]
+        + [window_of(scratch, 768 + 384 * k + 5, 16, 1, refs) for k in range(2)],
+        gw_ref,
+    )
+    low, high = scratch[4], scratch[5]
+    pad = jnp.zeros((2, D), F32)
+    for lv in range(2):
+        for lon in range(6):
+            oe_ref[lv, lon] = kept(low, high, place(lv, lon), 24)
+            be_ref[lv, lon] = kept(low, high, place(lv, 6 + lon), 24)
+        for lon in range(24):
+            os_ref[lv, lon] = kept(low, high, place(lv, 12 + lon), 8)
+        parts = []
+        corners = []
+        for t in range(3):
+            parts += [joined(low, high, at) for at in south(lv, t)] + [pad]
+            corners += [joined(low, high, corner(lv, t)), pad]
+        rows = jnp.concatenate(parts, axis=0)
+        bs_ref[lv] = dense(rows[:, :128], rows[:, 128:])
+        bc_ref[lv] = jnp.concatenate(corners, axis=0).astype(BF16)
+
+
 def whole(shape):
     return pl.BlockSpec(shape, lambda *_: (0,) * len(shape))
 
@@ -341,98 +423,159 @@
     return [pltpu.VMEM((rows, 128), F32) for _ in range(6)]
 
 
-def inner_windows(x, y, consts, pair_bias, last):
-    levels = x.shape[0]
-
+def inner_specs(first):
     def cols(n):
-        return pl.BlockSpec((2, 6, 24, D), lambda i: (i, n, 0, 0))
+        return pl.BlockSpec((2, 6, 24, D), lambda i: (i + first, n, 0, 0))
 
     four = [cols(n) for n in range(1, 5)]
+    return four + four, pl.BlockSpec((2, 24, 24, D), lambda i: (i + first, 0, 0, 0))
+
+
+def early_windows(x, y, consts, pair_bias, last, steps):
+    ins, out = inner_specs(0)
     return pl.pallas_call(
-        inner_kernel,
-        grid=(levels // 2,),
-        in_specs=four + four + const_specs() + [whole((HEADS, W, W)), whole((1, 1))],
-        out_specs=[
-            pl.BlockSpec((2, 24, 24, D), lambda i: (i, 0, 0, 0)),
-            whole(GW),
-            whole(GB),
-            whole(BIAS),
-        ],
+        early_kernel,
+        grid=(steps,),
+        in_specs=ins + const_specs() + [whole((HEADS, W, W)), whole((1, 1))],
+        out_specs=[out, whole(GW), whole(GB), whole(BIAS)],
         out_shape=[
-            jax.ShapeDtypeStruct((levels, 24, 24, D), BF16),
+            jax.ShapeDtypeStruct((x.shape[0], 24, 24, D), BF16),
             jax.ShapeDtypeStruct(GW, F32),
             jax.ShapeDtypeStruct(GB, F32),
             jax.ShapeDtypeStruct(BIAS, F32),
         ],
         scratch_shapes=halves(1152),
         compiler_params=PARAMS,
-        cost_estimate=cost(24),
-        name="inner_windows",
+        cost_estimate=cost(6 * steps),
+        name="early_windows",
     )(x, x, x, x, y, y, y, y, *consts, pair_bias, last)
+
+
+def late_windows(x, y, consts, bias, sums, inner, first):
+    steps = x.shape[0] // 2 - first
+    ins, out = inner_specs(first)
+    return pl.pallas_call(
+        late_kernel,
+        grid=(steps,),
+        in_specs=ins
+        + const_specs()
+        + [whole(BIAS), whole(GW), whole(GB), pl.BlockSpec(memory_space=pl.ANY)],
+        out_specs=[out, whole((ROWS, 128))],
+        out_shape=[
+            jax.ShapeDtypeStruct(inner.shape, BF16),
+            jax.ShapeDtypeStruct((ROWS, 128), F32),
+        ],
+        scratch_shapes=[pltpu.VMEM(GW, F32), pltpu.VMEM(GB, F32)] + halves(1152),
+        input_output_aliases={15: 0},
+        compiler_params=PARAMS,
+        cost_estimate=cost(6 * steps),
+        name="late_windows",
+    )(x, x, x, x, y, y, y, y, *consts, bias, *sums, inner)
+
+
+def both(*rest):
+    zeros = (0,) * len(rest)
+    return pl.BlockSpec((2, 2) + rest, lambda i: (0, i) + zeros)
+
+
+def one(*rest):
+    zeros = (0,) * len(rest)
+    return pl.BlockSpec((2,) + rest, lambda i: (i,) + zeros)
+
+
+def pack_halo(x, y):
+    levels = x.shape[0]
+    return pl.pallas_call(
+        pack_kernel,
+        grid=(levels // 2,),
+        in_specs=[one(36, 24, D), one(36, 24, D)],
+        out_specs=[both(6, 24, D), both(144, 128), both(24, D)],
+        out_shape=[
+            jax.ShapeDtypeStruct((2, levels, 6, 24, D), BF16),
+            jax.ShapeDtypeStruct((2, levels, 144, 128), BF16),
+            jax.ShapeDtypeStruct((2, levels, 24, D), BF16),
+        ],
+        scratch_shapes=[pltpu.VMEM((512, 128), F32), pltpu.VMEM((512, 128), F32)],
+        compiler_params=PARAMS,
+        name="pack_halo",
+    )(x, y)
 
 
 def edge_windows(x, y, e, s, c, consts, bias, sums):
     levels = x.shape[0]
-
-    def both(lon, lat):
-        return pl.BlockSpec((2, 2, lon, lat, D), lambda i: (0, i, 0, 0, 0))
-
-    def one(lon, lat):
-        return pl.BlockSpec((2, lon, lat, D), lambda i: (i, 0, 0, 0))
-
     return pl.pallas_call(
         edge_kernel,
         grid=(levels // 2,),
-        in_specs=[one(36, 24), one(36, 24), both(6, 24), both(36, 3), both(6, 3)]
+        in_specs=[one(36, 24, D), one(36, 24, D), both(6, 24, D), both(144, 128), both(24, D)]
         + const_specs()
         + [whole(BIAS), whole(GW), whole(GB)],
-        out_specs=[one(12, 32), one(24, 16), whole((ROWS, 128))],
+        out_specs=[
+            one(6, 24, D),
+            one(24, 8, D),
+            one(6, 24, D),
+            one(144, 128),
+            one(24, D),
+            whole(GW),
+            whole(GB),
+        ],
         out_shape=[
-            jax.ShapeDtypeStruct((levels, 12, 32, D), BF16),
-            jax.ShapeDtypeStruct((levels, 24, 16, D), BF16),
-            jax.ShapeDtypeStruct((ROWS, 128), F32),
-        ],
-        scratch_shapes=[pltpu.VMEM(GW, F32), pltpu.VMEM(GB, F32)] + halves(1536),
+            jax.ShapeDtypeStruct((levels, 6, 24, D), BF16),
+            jax.ShapeDtypeStruct((levels, 24, 8, D), BF16),
+            jax.ShapeDtypeStruct((levels, 6, 24, D), BF16),
+            jax.ShapeDtypeStruct((levels, 144, 128), BF16),
+            jax.ShapeDtypeStruct((levels, 24, D), BF16),
+            jax.ShapeDtypeStruct(GW, F32),
+            jax.ShapeDtypeStruct(GB, F32),
+        ],
+        scratch_shapes=halves(1536),
         compiler_params=PARAMS,
         cost_estimate=cost(24),
         name="edge_windows",
     )(x, y, e, s, c, *consts, bias, *sums)
 
 
-def assemble_kernel(inner, oe, os_, gl, gs, gc, out_ref):
+def assemble_kernel(inner, oe, os_, gl, gs, gc, out_ref, low, high):
     row = lax.broadcasted_iota(jnp.int32, (8, D), 0)
-
-    def head(got, tile):
-        wide = jnp.concatenate([got.astype(F32), jnp.zeros((5, D), F32)], axis=0)
-        return jnp.where(row < 3, wide, tile)
-
-    for lon in range(36):
-        if lon < 6:
-            rows = gl[0, lon].astype(F32)
-            got = gc[0, lon]
-        elif lon < 30:
-            rows = inner[0, lon - 6].astype(F32)
-            tail = os_[0, lon - 6].astype(F32)[:8]
-            rows = jnp.concatenate([rows[:16], jnp.where(row >= 5, tail, rows[16:])], axis=0)
-            got = gs[0, lon - 6]
-        else:
-            rows = oe[0, lon - 30].astype(F32)[:24]
-            got = gs[0, lon - 6]
-        out_ref[0, lon] = jnp.concatenate([head(got, rows[:8]), rows[8:]], axis=0).astype(BF16)
+    for lv in range(2):
+        base = 288 * lv
+        left, right = undense(gs[lv])
+        cleft, cright = split(gc[lv].astype(F32))
+        for t in range(3):
+            at = pl.ds(base + 48 + t, 30, stride=8)
+            low[at, :] = left[32 * t : 32 * t + 30]
+            high[at, :] = right[32 * t : 32 * t + 30]
+            at = pl.ds(base + t, 6, stride=8)
+            low[at, :] = cleft[8 * t : 8 * t + 6]
+            high[at, :] = cright[8 * t : 8 * t + 6]
+        for lon in range(36):
+            if lon < 6:
+                rows = gl[lv, lon].astype(F32)
+            elif lon < 30:
+                rows = inner[lv, lon - 6].astype(F32)
+                tail = os_[lv, lon - 6].astype(F32)
+                rows = jnp.concatenate([rows[:16], jnp.where(row >= 5, tail, rows[16:])], axis=0)
+            else:
+                rows = oe[lv, lon - 30].astype(F32)
+            head = jnp.where(row < 3, joined(low, high, pl.ds(base + 8 * lon, 8)), rows[:8])
+            out_ref[lv, lon] = jnp.concatenate([head, rows[8:]], axis=0).astype(BF16)
 
 
 def assemble(inner, oe, os_, got_lon, got_lat, got_both):
     levels = inner.shape[0]
-
-    def one(lon, lat):
-        return pl.BlockSpec((1, lon, lat, D), lambda i: (i, 0, 0, 0))
-
     return pl.pallas_call(
         assemble_kernel,
-        grid=(levels,),
-        in_specs=[one(24, 24), one(12, 32), one(24, 16), one(6, 24), one(30, 3), one(6, 3)],
-        out_specs=one(36, 24),
+        grid=(levels // 2,),
+        in_specs=[
+            one(24, 24, D),
+            one(6, 24, D),
+            one(24, 8, D),
+            one(6, 24, D),
+            one(144, 128),
+            one(24, D),
+        ],
+        out_specs=one(36, 24, D),
         out_shape=jax.ShapeDtypeStruct((levels, 36, 24, D), BF16),
+        scratch_shapes=[pltpu.VMEM((576, 128), F32), pltpu.VMEM((576, 128), F32)],
         compiler_params=PARAMS,
         cost_estimate=pl.CostEstimate(flops=0, bytes_accessed=6_000_000, transcendentals=0),
         name="assemble",
@@ -562,19 +705,18 @@
     levels, lat_count, lon_count, _ = tokens.shape
     x = jnp.transpose(tokens, (0, 2, 1, 3))
     y = jnp.transpose(cotangent, (0, 2, 1, 3))
-    s = shift(jnp.stack([x[:, :, :HALF_LAT], y[:, :, :HALF_LAT]]), ("lat",), (-1,))
-    e = shift(jnp.stack([x[:, :HALF_LON], y[:, :HALF_LON]]), ("lon",), (-1,))
-    c = shift(
-        jnp.stack([x[:, :HALF_LON, :HALF_LAT], y[:, :HALF_LON, :HALF_LAT]]), ("lon", "lat"), (-1, -1)
-    )
+    e, s, c = pack_halo(x, y)
+    s = shift(s, ("lat",), (-1,))
+    e = shift(e, ("lon",), (-1,))
+    c = shift(c, ("lon", "lat"), (-1, -1))
     consts = make_consts(ln_gain, qkv_weight, out_weight)
     last = (lax.axis_index("lat") == lax.axis_size("lat") - 1).astype(jnp.int32).reshape(1, 1)
-    inner, gw, gb, bias = inner_windows(x, y, consts, pair_bias, last)
-    oe, os_, sums = edge_windows(x, y, e, s, c, consts, bias, (gw, gb))
-    back_lat = jnp.concatenate([os_[:, :, 8:11], oe[:, :HALF_LON, 24:27]], axis=1)
-    got_lat = shift(back_lat, ("lat",), (1,))
-    got_lon = shift(oe[:, HALF_LON:, :24], ("lon",), (1,))
-    got_both = shift(oe[:, HALF_LON:, 24:27], ("lon", "lat"), (1, 1))
+    inner, gw, gb, bias = early_windows(x, y, consts, pair_bias, last, EARLY)
+    oe, os_, be, bs, bc, gw, gb = edge_windows(x, y, e, s, c, consts, bias, (gw, gb))
+    got_lat = shift(bs, ("lat",), (1,))
+    got_lon = shift(be, ("lon",), (1,))
+    got_both = shift(bc, ("lon", "lat"), (1, 1))
+    inner, sums = late_windows(x, y, consts, bias, (gw, gb), inner, EARLY)
     sums = sum_over_devices(sums)
     grad_x = assemble(inner, oe, os_, got_lon, got_lat, got_both)
     factor = float(

time: 151 us -> 144 us (0.954)
  local copies, waits for them, and re-layouts: 13.5 us -> 5.13 us
  Pallas kernels: 65.9 us -> 72.7 us
  waiting for transfers between devices: 33.2 us -> 29.9 us
  other arithmetic: 4.1 us -> 2.43 us
    pallas_call x3 -> x5, Pallas kernels: 63.3 us -> 70.1 us  [the longest x1 30.9 us: edge_windows(): pl.pallas_call(edge_kernel, grid=(levels // 2,), in_specs=[one(36, 24, D)...]
    ppermute x6, waiting for transfers between devices: 18.3 us -> 12.3 us  [shift(): return lax.ppermute(value, axes if len(axes) > 1 else axes[0], pairs)]
    another operation x4 -> x0, local copies, waits for them, and re-layouts: 4.86 us -> none  [the longest x2 2.45 us: local(): jnp.stack([x[:, :, :HALF_LAT], y[:, :, :HALF_LAT]])]
    ppermute x13, starting transfers between devices: 15.7 us -> 18.9 us  [moved(): return lax.ppermute(value, axis, [(n, to_of(n)) for n in range(count)])]
    ppermute x1 -> x0, local copies, waits for them, and re-layouts: 2.64 us -> none  [shift(): return lax.ppermute(value, axes if len(axes) > 1 else axes[0], pairs)]
    ppermute x13, waiting for transfers between devices: 14.1 us -> 15.8 us  [moved(): return lax.ppermute(value, axis, [(n, to_of(n)) for n in range(count)])]
    unnamed x18 -> x26, local copies, waits for them, and re-layouts: 2.58 us -> 3.07 us
  transfers between devices with their start and end apart: 20 -> 20, of which waited for: 10 -> 13; matrix products, arithmetic and copies ran while one was open for 7% -> 1% of each run, Pallas kernels for 22% -> 17%
where the time goes in v3:
time: 144 us
  Pallas kernels  72.7 us (50%)
  starting transfers between devices  33 us (23%)
  waiting for transfers between devices  29.9 us (21%)
  local copies, waits for them, and re-layouts  5.13 us (4%)
  other arithmetic  2.43 us (2%)
    pallas_call x1, Pallas kernels, edge_windows(): pl.pallas_call(edge_kernel, grid=(levels // 2,), in_specs=[one(36, 24, D)...  30.9 us
    pallas_call x1, Pallas kernels, early_windows(): pl.pallas_call(early_kernel, grid=(steps,), in_specs=ins + const_specs()...  20.2 us
    ppermute x13, starting transfers between devices, moved(): return lax.ppermute(value, axis, [(n, to_of(n)) for n in range(count)])  18.9 us
    ppermute x13, waiting for transfers between devices, moved(): return lax.ppermute(value, axis, [(n, to_of(n)) for n in range(count)])  15.8 us
    ppermute x6, starting transfers between devices, shift(): return lax.ppermute(value, axes if len(axes) > 1 else axes[0], pairs)  13 us
    ppermute x6, waiting for transfers between devices, shift(): return lax.ppermute(value, axes if len(axes) > 1 else axes[0], pairs)  12.3 us
    pallas_call x1, Pallas kernels, late_windows(): pl.pallas_call(late_kernel, grid=(steps,), in_specs=ins + const_specs() +...  8.96 us
    pallas_call x1, Pallas kernels, pack_halo(): pl.pallas_call(pack_kernel, grid=(levels // 2,), in_specs=[one(36, 24, D)...  5.24 us
  transfers between devices with their start and end apart: 20, of which 13 were waited for; matrix products, arithmetic and copies ran while one was open for 1% of the time, Pallas kernels for 17%

profile of v3, /device:TPU:0, one launch (start us, length us, event | category | flops | bytes accessed | tf_op | source)
XLA Modules:
  0.0 144.0 jit_solution(1269407150974576504)
XLA Ops:
  0.6 5.2 %pack_halo.1 = (bf16[2,8,6,24,192]{4,3,2,1,0:T(8,128)(2,1)}, bf16[2,8,144,128]{3,2,1,0:T(8,128)(2,1)}, bf16[2,8,24,192]{3,2,1,0:T(8,128)(2,1)}) custom-call(bf16[8,36,24,192]{3,2,1,0:T(8,128)(2,1)} %bitcast.38, bf16[8,36,24,192]{3,2,1,0:T(8,128)(2,1)} %bitcast.48), custom_call_target="tpu_custom_call" | custom-call | tf_op jit(solution)/shard_map/pack_halo/pallas_call | solution.py:488
  5.9 3.5 %collective-permute-start = (bf16[2,8,6,24,192]{4,3,2,1,0:T(8,128)(2,1)}, bf16[2,8,6,24,192]{4,3,2,1,0:T(8,128)(2,1)S(1)}, u32[]{:S(2)}, u32[]{:S(2)}) collective-permute-start(bf16[2,8,6,24,192]{4,3,2,1,0:T(8,128)(2,1)} %get-tuple-element.26), channel_id=1, source_target_pairs={{0,120},{8,0},{16,8},{24,16},{32,24},{40,32},{48,40},{56,48},{64,5... | collective-permute-start | bytes 2654216 | tf_op jit(solution)/shard_map/ppermute | solution.py:637
  9.4 6.2 %collective-permute-start.1 = (bf16[2,8,144,128]{3,2,1,0:T(8,128)(2,1)}, bf16[2,8,144,128]{3,2,1,0:T(8,128)(2,1)S(1)}, u32[]{:S(2)}, u32[]{:S(2)}) collective-permute-start(bf16[2,8,144,128]{3,2,1,0:T(8,128)(2,1)} %get-tuple-element.27), channel_id=1, source_target_pairs={{0,7},{1,0},{2,1},{3,2},{4,3},{5,4},{6,5},{7,6},{8,15},{9,8},{10,9... | collective-permute-start | bytes 1769480 | tf_op jit(solution)/shard_map/ppermute | solution.py:637
  16.2 0.9 copy.18.wqkv
  17.8 20.2 %early_windows.1 = (bf16[8,24,24,192]{3,2,1,0:T(8,128)(2,1)}, f32[4,192,192]{2,1,0:T(8,128)}, f32[144,896]{1,0:T(8,128)}, f32[2,144,896]{2,1,0:T(8,128)}) custom-call(bf16[8,36,24,192]{3,2,1,0:T(8,128)(2,1)} %bitcast.39, bf16[8,36,24,192]{3,2,1,0:T(8,128)(2,1)} %bitcast.40, bf16[8,36,24,192]{3,2,1,0:T(8,128)(2,1)} %bitcast.41, ...), custom_call_target="tpu_custom_call" | custom-call | flops 3822059520 | bytes 2985984 | tf_op jit(solution)/shard_map/early_windows/pallas_call | solution.py:436
  39.4 30.9 %edge_windows.1 = (bf16[8,6,24,192]{3,2,1,0:T(8,128)(2,1)}, bf16[8,24,8,192]{3,2,1,0:T(8,128)(2,1)}, bf16[8,6,24,192]{3,2,1,0:T(8,128)(2,1)}, bf16[8,144,128]{2,...) custom-call(bf16[8,36,24,192]{3,2,1,0:T(8,128)(2,1)} %bitcast.43, ...), custom_call_target="tpu_custom_call" | custom-call | flops 5096079360 | bytes 3981312 | tf_op jit(solution)/shard_map/edge_windows/pallas_call | solution.py:506
  70.3 9.0 %late_windows.1 = (bf16[8,24,24,192]{3,2,1,0:T(8,128)(2,1)}, f32[2176,128]{1,0:T(8,128)}) custom-call(bf16[8,36,24,192]{3,2,1,0:T(8,128)(2,1)} %bitcast.44, bf16[8,36,24,192]{3,2,1,0:T(8,128)(2,1)} %bitcast.45, bf16[8,36,24,192]{3,2,1,0:T(8,128)(2,1)} %bitcast.46, bf16[8,36,24,192]{3,2,1,0:T(8,128)(2,1)} %bitcast.47, ...), custom_call_target="tpu_custom_call", output_to_operand_aliasing={{0}: (15, {})} | custom-call | flops 1274019840 | bytes 995328 | tf_op jit(solution)/shard_map/late_windows/pallas_call | solution.py:457
  79.2 1.1 fusion
  81.1 1.2 collective-permute-done.6
  82.3 1.1 bitcast_add_fusion
  83.6 1.4 collective-permute-start.8
  85.0 3.3 %collective-permute-start.9 = (bf16[272,128]{1,0:T(8,128)(2,1)S(1)}, bf16[272,128]{1,0:T(8,128)(2,1)S(1)}, u32[]{:S(2)}, u32[]{:S(2)}) collective-permute-start(bf16[272,128]{1,0:T(8,128)(2,1)S(1)} %get-tuple-element.56), channel_id=1, source_target_pairs={{0,48},{8,56},{16,32},{24,40},{32,16},{40,24},{48,0},{56,8},{64,11... | collective-permute-start | bytes 208904 | tf_op jit(solution)/shard_map/ppermute | solution.py:642
  88.6 1.1 collective-permute-done.8
  89.7 1.4 collective-permute-done.9
  91.2 1.7 %collective-permute-start.10 = (bf16[272,128]{1,0:T(8,128)(2,1)S(1)}, bf16[272,128]{1,0:T(8,128)(2,1)S(1)}, u32[]{:S(2)}, u32[]{:S(2)}) collective-permute-start(bf16[272,128]{1,0:T(8,128)(2,1)S(1)} %get-tuple-element.45), channel_id=1, source_target_pairs={{0,2},{1,3},{2,0},{3,1},{4,6},{5,7},{6,4},{7,5},{8,10},{9,11},{10,... | collective-permute-start | bytes 208904 | tf_op jit(solution)/shard_map/ppermute | solution.py:642
  92.9 3.6 %collective-permute-start.11 = (bf16[272,128]{1,0:T(8,128)(2,1)S(1)}, bf16[272,128]{1,0:T(8,128)(2,1)S(1)}, u32[]{:S(2)}, u32[]{:S(2)}) collective-permute-start(bf16[272,128]{1,0:T(8,128)(2,1)S(1)} %get-tuple-element.45), channel_id=1, source_target_pairs={{0,4},{1,5},{2,6},{3,7},{4,0},{5,1},{6,2},{7,3},{8,12},{9,13},{10,... | collective-permute-start | bytes 208904 | tf_op jit(solution)/shard_map/ppermute | solution.py:642
  96.5 3.3 %collective-permute-done.11 = bf16[272,128]{1,0:T(8,128)(2,1)S(1)} collective-permute-done((bf16[272,128]{1,0:T(8,128)(2,1)S(1)}, bf16[272,128]{1,0:T(8,128)(2,1)S(1)}, u32[]{:S(2)}, u32[]{:S(2)}) %collective-permute-start.11) | collective-permute-done | bytes 69664 | tf_op jit(solution)/shard_map/ppermute | solution.py:642
  99.8 2.2 %collective-permute-done.12 = bf16[272,128]{1,0:T(8,128)(2,1)S(1)} collective-permute-done((bf16[272,128]{1,0:T(8,128)(2,1)S(1)}, bf16[272,128]{1,0:T(8,128)(2,1)S(1)}, u32[]{:S(2)}, u32[]{:S(2)}) %collective-permute-start.12) | collective-permute-done | bytes 69664 | tf_op jit(solution)/shard_map/ppermute | solution.py:642
  102.1 2.6 %collective-permute-start.13 = (bf16[272,128]{1,0:T(8,128)(2,1)S(1)}, bf16[272,128]{1,0:T(8,128)(2,1)S(1)}, u32[]{:S(2)}, u32[]{:S(2)}) collective-permute-start(bf16[272,128]{1,0:T(8,128)(2,1)S(1)} %fusion.5), channel_id=1, source_target_pairs={{0,1},{1,0},{2,3},{3,2},{4,5},{5,4},{6,7},{7,6},{8,9},{9,8},{10,11... | collective-permute-start | bytes 208904 | tf_op jit(solution)/shard_map/ppermute | solution.py:642
  105.2 1.2 collective-permute-start.15
  106.3 1.7 %collective-permute-done.13 = bf16[272,128]{1,0:T(8,128)(2,1)S(1)} collective-permute-done((bf16[272,128]{1,0:T(8,128)(2,1)S(1)}, bf16[272,128]{1,0:T(8,128)(2,1)S(1)}, u32[]{:S(2)}, u32[]{:S(2)}) %collective-permute-start.13) | collective-permute-done | bytes 69664 | tf_op jit(solution)/shard_map/ppermute | solution.py:642
  108.1 0.9 collective-permute-done.14
  108.9 1.7 %collective-permute-done.15 = bf16[272,128]{1,0:T(8,128)(2,1)S(1)} collective-permute-done((bf16[272,128]{1,0:T(8,128)(2,1)S(1)}, bf16[272,128]{1,0:T(8,128)(2,1)S(1)}, u32[]{:S(2)}, u32[]{:S(2)}) %collective-permute-start.15) | collective-permute-done | bytes 69664 | tf_op jit(solution)/shard_map/ppermute | solution.py:701
  111.3 3.8 %collective-permute-start.17 = (bf16[272,128]{1,0:T(8,128)(2,1)S(1)}, bf16[272,128]{1,0:T(8,128)(2,1)S(1)}, u32[]{:S(2)}, u32[]{:S(2)}) collective-permute-start(bf16[272,128]{1,0:T(8,128)(2,1)S(1)} %add_convert_fusion), channel_id=1, source_target_pairs={{0,32},{8,40},{16,48},{24,56},{32,0},{40,8},{48,16},{56,24},{64,96... | collective-permute-start | bytes 208904 | tf_op jit(solution)/shard_map/ppermute | solution.py:642
  115.5 1.5 %collective-permute-start.4 = (bf16[8,144,128]{2,1,0:T(8,128)(2,1)S(1)}, bf16[8,144,128]{2,1,0:T(8,128)(2,1)S(1)}, u32[]{:S(2)}, u32[]{:S(2)}) collective-permute-start(bf16[8,144,128]{2,1,0:T(8,128)(2,1)S(1)} %copy-done.9), channel_id=1, source_target_pairs={{0,1},{1,2},{2,3},{3,4},{4,5},{5,6},{6,7},{7,0},{8,9},{9,10},{10,1... | collective-permute-start | bytes 884744 | tf_op jit(solution)/shard_map/ppermute | solution.py:637
  117.0 1.2 collective-permute-done.17
  118.2 2.5 %collective-permute-done.18 = bf16[272,128]{1,0:T(8,128)(2,1)S(1)} collective-permute-done((bf16[272,128]{1,0:T(8,128)(2,1)S(1)}, bf16[272,128]{1,0:T(8,128)(2,1)S(1)}, u32[]{:S(2)}, u32[]{:S(2)}) %collective-permute-start.18) | collective-permute-done | bytes 69664 | tf_op jit(solution)/shard_map/ppermute | solution.py:642
  120.9 1.5 %collective-permute-start.5 = (bf16[8,24,192]{2,1,0:T(8,128)(2,1)S(1)}, bf16[8,24,192]{2,1,0:T(8,128)(2,1)S(1)}, u32[]{:S(2)}, u32[]{:S(2)}) collective-permute-start(bf16[8,24,192]{2,1,0:T(8,128)(2,1)S(1)} %copy-done.11), channel_id=1, source_target_pairs={{0,9},{1,10},{2,11},{3,12},{4,13},{5,14},{6,15},{7,8},{8,17},{9,18... | collective-permute-start | bytes 221192 | tf_op jit(solution)/shard_map/ppermute | solution.py:637
  122.4 12.2 %collective-permute-done.5.gc = bf16[8,24,192]{2,1,0:T(8,128)(2,1)S(1)} collective-permute-done((bf16[8,24,192]{2,1,0:T(8,128)(2,1)S(1)}, bf16[8,24,192]{2,1,0:T(8,128)(2,1)S(1)}, u32[]{:S(2)}, u32[]{:S(2)}) %collective-permute-start.5) | collective-permute-done | bytes 73760 | tf_op jit(solution)/shard_map/ppermute | solution.py:637
  135.5 4.8 %assemble.1 = bf16[8,36,24,192]{3,2,1,0:T(8,128)(2,1)} custom-call(bf16[8,24,24,192]{3,2,1,0:T(8,128)(2,1)} %get-tuple-element.34.inner, bf16[8,6,24,192]{3,2,1,0:T(8,128)(2,1)} %get-tuple-element.35.oe, bf16[8,24,8,192]{3,2,1,0:T(8,128)(2,1)} %get-tuple-element.36.os_, bf16[8,6,24,192]{3,2,1,0:T(8,128)(2,1)} %copy-done.2, bf16[8,144,128]{2,1,0:T(8,128)(2,1)} %copy-done.3, ...), custom_call_target="tpu_custom_call" | custom-call | bytes 6000000 | tf_op jit(solution)/shard_map/assemble/pallas_call | solution.py:565
  140.5 0.8 pad_maximum_fusion.refs_0_
  141.4 2.6 %finish_sums.1 = (f32[192,576]{1,0:T(8,128)}, f32[192,192]{1,0:T(8,128)}, f32[6,144,144]{2,1,0:T(8,128)}, f32[1,192]{1,0:T(1,128)}) custom-call(bf16[2176,128]{1,0:T(8,128)(2,1)} %pad_maximum_fusion.refs_0_, f32[1,192]{1,0:T(1,128)} %bitcast.81, bf16[192,576]{1,0:T(8,128)(2,1)} %refs_2_.1), custom_call_target="tpu_custom_call" | custom-call | tf_op jit(solution)/shard_map/finish_sums/pallas_call | solution.py:603
  (54 shorter events, 6.9 us)
Async XLA Ops:
  0.6 15.3 %copy-start.1 = (bf16[192,576]{1,0:T(8,128)(2,1)S(1)}, bf16[192,576]{1,0:T(8,128)(2,1)}, u32[]{:S(2)}) copy-start(bf16[192,576]{1,0:T(8,128)(2,1)} %refs_2_.1) | copy-start | bytes 663556
  5.9 11.2 %copy-start.5 = (bf16[192,192]{1,0:T(8,128)(2,1)S(1)}, bf16[192,192]{1,0:T(8,128)(2,1)}, u32[]{:S(2)}) copy-start(bf16[192,192]{1,0:T(8,128)(2,1)} %param.10) | copy-start | bytes 221188
  5.9 32.3 %collective-permute-start = (bf16[2,8,6,24,192]{4,3,2,1,0:T(8,128)(2,1)}, bf16[2,8,6,24,192]{4,3,2,1,0:T(8,128)(2,1)S(1)}, u32[]{:S(2)}, u32[]{:S(2)}) collective-permute-start(bf16[2,8,6,24,192]{4,3,2,1,0:T(8,128)(2,1)} %get-tuple-element.26), channel_id=1, source_target_pairs={{0,120},{8,0},{16,8},{24,16},{32,24},{40,32},{48,40},{56,48},{64,5... | collective-permute-start | bytes 2654216 | tf_op jit(solution)/shard_map/ppermute | solution.py:637
  9.4 28.8 %collective-permute-start.1 = (bf16[2,8,144,128]{3,2,1,0:T(8,128)(2,1)}, bf16[2,8,144,128]{3,2,1,0:T(8,128)(2,1)S(1)}, u32[]{:S(2)}, u32[]{:S(2)}) collective-permute-start(bf16[2,8,144,128]{3,2,1,0:T(8,128)(2,1)} %get-tuple-element.27), channel_id=1, source_target_pairs={{0,7},{1,0},{2,1},{3,2},{4,3},{5,4},{6,5},{7,6},{8,15},{9,8},{10,9... | collective-permute-start | bytes 1769480 | tf_op jit(solution)/shard_map/ppermute | solution.py:637
  15.6 22.4 %collective-permute-start.2 = (bf16[2,8,24,192]{3,2,1,0:T(8,128)(2,1)}, bf16[2,8,24,192]{3,2,1,0:T(8,128)(2,1)S(1)}, u32[]{:S(2)}, u32[]{:S(2)}) collective-permute-start(bf16[2,8,24,192]{3,2,1,0:T(8,128)(2,1)} %get-tuple-element.28), channel_id=1, source_target_pairs={{0,127},{1,120},{2,121},{3,122},{4,123},{5,124},{6,125},{7,126},{8... | collective-permute-start | bytes 442376 | tf_op jit(solution)/shard_map/ppermute | solution.py:637
  16.1 1.7 %copy-start = (bf16[192,576]{0,1:T(8,128)(2,1)}, bf16[192,576]{0,1:T(8,128)(2,1)S(1)}, u32[]{:S(2)}) copy-start(bf16[192,576]{0,1:T(8,128)(2,1)S(1)} %copy.14) | copy-start | bytes 663556
  38.0 0.7 copy-start.10
  38.2 0.8 copy-start.8
  38.2 1.2 copy-start.6
  80.3 2.0 %collective-permute-start.6 = (bf16[1088,128]{1,0:T(8,128)(2,1)S(1)}, bf16[1088,128]{1,0:T(8,128)(2,1)S(1)}, u32[]{:S(2)}, u32[]{:S(2)}) collective-permute-start(bf16[1088,128]{1,0:T(8,128)(2,1)S(1)} %fusion), channel_id=1, source_target_pairs={{0,8},{8,0},{16,24},{24,16},{32,40},{40,32},{48,56},{56,48},{64,72... | collective-permute-start | bytes 835592 | tf_op jit(solution)/shard_map/ppermute | solution.py:642
  83.5 32.1 %copy-start.7 = (bf16[8,6,24,192]{3,2,1,0:T(8,128)(2,1)S(1)}, bf16[8,6,24,192]{3,2,1,0:T(8,128)(2,1)}, u32[]{:S(2)}) copy-start(bf16[8,6,24,192]{3,2,1,0:T(8,128)(2,1)} %get-tuple-element.37) | copy-start | bytes 1327108
  83.5 32.1 %copy-start.9 = (bf16[8,144,128]{2,1,0:T(8,128)(2,1)S(1)}, bf16[8,144,128]{2,1,0:T(8,128)(2,1)}, u32[]{:S(2)}) copy-start(bf16[8,144,128]{2,1,0:T(8,128)(2,1)} %get-tuple-element.38) | copy-start | bytes 884740
  83.5 5.1 %collective-permute-start.7 = (bf16[272,128]{1,0:T(8,128)(2,1)S(1)}, bf16[272,128]{1,0:T(8,128)(2,1)S(1)}, u32[]{:S(2)}, u32[]{:S(2)}) collective-permute-start(bf16[272,128]{1,0:T(8,128)(2,1)S(1)} %get-tuple-element.55), channel_id=1, source_target_pairs={{0,16},{8,24},{16,0},{24,8},{32,48},{40,56},{48,32},{56,40},{64,80... | collective-permute-start | bytes 208904 | tf_op jit(solution)/shard_map/ppermute | solution.py:642
  83.6 6.1 %collective-permute-start.8 = (bf16[272,128]{1,0:T(8,128)(2,1)S(1)}, bf16[272,128]{1,0:T(8,128)(2,1)S(1)}, u32[]{:S(2)}, u32[]{:S(2)}) collective-permute-start(bf16[272,128]{1,0:T(8,128)(2,1)S(1)} %get-tuple-element.57), channel_id=1, source_target_pairs={{0,32},{8,40},{16,48},{24,56},{32,0},{40,8},{48,16},{56,24},{64,96... | collective-permute-start | bytes 208904 | tf_op jit(solution)/shard_map/ppermute | solution.py:642
  85.0 6.2 %collective-permute-start.9 = (bf16[272,128]{1,0:T(8,128)(2,1)S(1)}, bf16[272,128]{1,0:T(8,128)(2,1)S(1)}, u32[]{:S(2)}, u32[]{:S(2)}) collective-permute-start(bf16[272,128]{1,0:T(8,128)(2,1)S(1)} %get-tuple-element.56), channel_id=1, source_target_pairs={{0,48},{8,56},{16,32},{24,40},{32,16},{40,24},{48,0},{56,8},{64,11... | collective-permute-start | bytes 208904 | tf_op jit(solution)/shard_map/ppermute | solution.py:642
  91.2 5.3 %collective-permute-start.10 = (bf16[272,128]{1,0:T(8,128)(2,1)S(1)}, bf16[272,128]{1,0:T(8,128)(2,1)S(1)}, u32[]{:S(2)}, u32[]{:S(2)}) collective-permute-start(bf16[272,128]{1,0:T(8,128)(2,1)S(1)} %get-tuple-element.45), channel_id=1, source_target_pairs={{0,2},{1,3},{2,0},{3,1},{4,6},{5,7},{6,4},{7,5},{8,10},{9,11},{10,... | collective-permute-start | bytes 208904 | tf_op jit(solution)/shard_map/ppermute | solution.py:642
  92.9 6.9 %collective-permute-start.11 = (bf16[272,128]{1,0:T(8,128)(2,1)S(1)}, bf16[272,128]{1,0:T(8,128)(2,1)S(1)}, u32[]{:S(2)}, u32[]{:S(2)}) collective-permute-start(bf16[272,128]{1,0:T(8,128)(2,1)S(1)} %get-tuple-element.45), channel_id=1, source_target_pairs={{0,4},{1,5},{2,6},{3,7},{4,0},{5,1},{6,2},{7,3},{8,12},{9,13},{10,... | collective-permute-start | bytes 208904 | tf_op jit(solution)/shard_map/ppermute | solution.py:642
  96.5 5.5 %collective-permute-start.12 = (bf16[272,128]{1,0:T(8,128)(2,1)S(1)}, bf16[272,128]{1,0:T(8,128)(2,1)S(1)}, u32[]{:S(2)}, u32[]{:S(2)}) collective-permute-start(bf16[272,128]{1,0:T(8,128)(2,1)S(1)} %get-tuple-element.45), channel_id=1, source_target_pairs={{0,6},{1,7},{2,4},{3,5},{4,2},{5,3},{6,0},{7,1},{8,14},{9,15},{10,... | collective-permute-start | bytes 208904 | tf_op jit(solution)/shard_map/ppermute | solution.py:642
  102.1 18.9 %copy-start.11 = (bf16[8,24,192]{2,1,0:T(8,128)(2,1)S(1)}, bf16[8,24,192]{2,1,0:T(8,128)(2,1)}, u32[]{:S(2)}) copy-start(bf16[8,24,192]{2,1,0:T(8,128)(2,1)} %get-tuple-element.39) | copy-start | bytes 221188
  102.1 6.0 %collective-permute-start.13 = (bf16[272,128]{1,0:T(8,128)(2,1)S(1)}, bf16[272,128]{1,0:T(8,128)(2,1)S(1)}, u32[]{:S(2)}, u32[]{:S(2)}) collective-permute-start(bf16[272,128]{1,0:T(8,128)(2,1)S(1)} %fusion.5), channel_id=1, source_target_pairs={{0,1},{1,0},{2,3},{3,2},{4,5},{5,4},{6,7},{7,6},{8,9},{9,8},{10,11... | collective-permute-start | bytes 208904 | tf_op jit(solution)/shard_map/ppermute | solution.py:642
  104.6 4.3 %collective-permute-start.14 = (bf16[272,128]{1,0:T(8,128)(2,1)S(1)}, bf16[272,128]{1,0:T(8,128)(2,1)S(1)}, u32[]{:S(2)}, u32[]{:S(2)}) collective-permute-start(bf16[272,128]{1,0:T(8,128)(2,1)S(1)} %fusion.5), channel_id=1, source_target_pairs={{0,64},{8,72},{16,80},{24,88},{32,96},{40,104},{48,112},{56,120},{... | collective-permute-start | bytes 208904 | tf_op jit(solution)/shard_map/ppermute | solution.py:642
  105.2 5.5 %collective-permute-start.15 = (bf16[272,128]{1,0:T(8,128)(2,1)S(1)}, bf16[272,128]{1,0:T(8,128)(2,1)S(1)}, u32[]{:S(2)}, u32[]{:S(2)}) collective-permute-start(bf16[272,128]{1,0:T(8,128)(2,1)S(1)} %fusion.5), channel_id=1, source_target_pairs={{0,65},{1,64},{2,67},{3,66},{4,69},{5,68},{6,71},{7,70},{8,73},{9,... | collective-permute-start | bytes 208904 | tf_op jit(solution)/shard_map/ppermute | solution.py:701
  110.8 6.3 %collective-permute-start.16 = (bf16[272,128]{1,0:T(8,128)(2,1)S(1)}, bf16[272,128]{1,0:T(8,128)(2,1)S(1)}, u32[]{:S(2)}, u32[]{:S(2)}) collective-permute-start(bf16[272,128]{1,0:T(8,128)(2,1)S(1)} %add_convert_fusion), channel_id=1, source_target_pairs={{0,16},{8,24},{16,0},{24,8},{32,48},{40,56},{48,32},{56,40},{64,80... | collective-permute-start | bytes 208904 | tf_op jit(solution)/shard_map/ppermute | solution.py:642
  111.3 6.9 %collective-permute-start.17 = (bf16[272,128]{1,0:T(8,128)(2,1)S(1)}, bf16[272,128]{1,0:T(8,128)(2,1)S(1)}, u32[]{:S(2)}, u32[]{:S(2)}) collective-permute-start(bf16[272,128]{1,0:T(8,128)(2,1)S(1)} %add_convert_fusion), channel_id=1, source_target_pairs={{0,32},{8,40},{16,48},{24,56},{32,0},{40,8},{48,16},{56,24},{64,96... | collective-permute-start | bytes 208904 | tf_op jit(solution)/shard_map/ppermute | solution.py:642
  115.2 5.5 %collective-permute-start.18 = (bf16[272,128]{1,0:T(8,128)(2,1)S(1)}, bf16[272,128]{1,0:T(8,128)(2,1)S(1)}, u32[]{:S(2)}, u32[]{:S(2)}) collective-permute-start(bf16[272,128]{1,0:T(8,128)(2,1)S(1)} %add_convert_fusion), channel_id=1, source_target_pairs={{0,48},{8,56},{16,32},{24,40},{32,16},{40,24},{48,0},{56,8},{64,11... | collective-permute-start | bytes 208904 | tf_op jit(solution)/shard_map/ppermute | solution.py:642
  115.5 19.1 %collective-permute-start.3 = (bf16[8,6,24,192]{3,2,1,0:T(8,128)(2,1)S(1)}, bf16[8,6,24,192]{3,2,1,0:T(8,128)(2,1)S(1)}, u32[]{:S(2)}, u32[]{:S(2)}) collective-permute-start(bf16[8,6,24,192]{3,2,1,0:T(8,128)(2,1)S(1)} %copy-done.7), channel_id=1, source_target_pairs={{0,8},{8,16},{16,24},{24,32},{32,40},{40,48},{48,56},{56,64},{64,7... | collective-permute-start | bytes 1327112 | tf_op jit(solution)/shard_map/ppermute | solution.py:637
  115.5 19.0 %collective-permute-start.4 = (bf16[8,144,128]{2,1,0:T(8,128)(2,1)S(1)}, bf16[8,144,128]{2,1,0:T(8,128)(2,1)S(1)}, u32[]{:S(2)}, u32[]{:S(2)}) collective-permute-start(bf16[8,144,128]{2,1,0:T(8,128)(2,1)S(1)} %copy-done.9), channel_id=1, source_target_pairs={{0,1},{1,2},{2,3},{3,4},{4,5},{5,6},{6,7},{7,0},{8,9},{9,10},{10,1... | collective-permute-start | bytes 884744 | tf_op jit(solution)/shard_map/ppermute | solution.py:637
  120.8 19.5 %collective-permute-start.19 = (bf16[4,272,128]{2,1,0:T(8,128)(2,1)S(1)}, bf16[4,272,128]{2,1,0:T(8,128)(2,1)S(1)}, u32[]{:S(2)}, u32[]{:S(2)}) collective-permute-start(bf16[4,272,128]{2,1,0:T(8,128)(2,1)S(1)} %get-tuple-element.49), channel_id=1, source_target_pairs={{0,8},{8,0},{16,24},{24,16},{32,40},{40,32},{48,56},{56,48},{64,72... | collective-permute-start | bytes 835592 | tf_op jit(solution)/shard_map/ppermute | solution.py:642
  120.9 13.7 %collective-permute-start.5 = (bf16[8,24,192]{2,1,0:T(8,128)(2,1)S(1)}, bf16[8,24,192]{2,1,0:T(8,128)(2,1)S(1)}, u32[]{:S(2)}, u32[]{:S(2)}) collective-permute-start(bf16[8,24,192]{2,1,0:T(8,128)(2,1)S(1)} %copy-done.11), channel_id=1, source_target_pairs={{0,9},{1,10},{2,11},{3,12},{4,13},{5,14},{6,15},{7,8},{8,17},{9,18... | collective-permute-start | bytes 221192 | tf_op jit(solution)/shard_map/ppermute | solution.py:637
  134.6 0.6 copy-start.4
  134.6 0.7 copy-start.3
  134.6 0.9 copy-start.2

commit v4 on v3

--- a/solution.py
+++ b/solution.py
@@ -148,7 +148,7 @@
         yield self.back
 
 
-STAGGER = 4
+STAGGER = 2
 EARLY = 3
 
 
@@ -260,20 +260,27 @@
 
 
 def early_kernel(
-    x0, x1, x2, x3, y0, y1, y2, y3, gain, wqkv, wqkv_t, wout_t, pair, last, dx_ref, gw_ref, gb_ref, bias_ref, *scratch
+    x0, x1, x2, x3, y0, y1, y2, y3, gain, weight, out_weight, pair, last, dx_ref, gw_ref, gb_ref, bias_ref, wqkv, wqkv_t, wout_t, *scratch
 ):
     @pl.when(pl.program_id(0) == 0)
     def _():
         gw_ref[...] = jnp.zeros_like(gw_ref)
         gb_ref[...] = jnp.zeros_like(gb_ref)
         lay_bias(pair, last, bias_ref)
+        part = weight[...]
+        gap = jnp.zeros((D, 64), BF16)
+        wqkv[...] = jnp.concatenate(
+            [p for n in range(3) for p in (part[:, D * n : D * n + D], gap)], axis=1
+        )
+        wqkv_t[...] = part.T
+        wout_t[...] = out_weight[...].T
 
     consts = (gain, wqkv, wqkv_t, wout_t)
     inner_steps((x0, x1, x2, x3), (y0, y1, y2, y3), consts, bias_ref, dx_ref, gw_ref, gb_ref, scratch)
 
 
 def late_kernel(
-    x0, x1, x2, x3, y0, y1, y2, y3, gain, wqkv, wqkv_t, wout_t, bias, gw_in, gb_in, _, dx_ref, sum_ref, gw_ref, gb_ref, *scratch
+    x0, x1, x2, x3, y0, y1, y2, y3, gain, wqkv, wqkv_t, wout_t, bias, gw_in, gb_in, core, _, dx_ref, give_ref, mine_ref, gw_ref, gb_ref, sum_ref, *scratch
 ):
     @pl.when(pl.program_id(0) == 0)
     def _():
@@ -291,6 +298,10 @@
         for t in range(7):
             sum_ref[WROWS + W * t : WROWS + W * t + W] = gb_ref[:, 128 * t : 128 * t + 128]
         sum_ref[WROWS + BROWS :] = jnp.zeros((ROWS - WROWS - BROWS, 128), F32)
+        first = core[...] == 0
+        upper, lower = sum_ref[: ROWS // 2], sum_ref[ROWS // 2 :]
+        give_ref[...] = jnp.where(first, lower, upper).astype(BF16)
+        mine_ref[...] = jnp.where(first, upper, lower)
 
 
 def split(rows):
@@ -304,25 +315,28 @@
 
 
 def dense(left, right):
+    half = left.shape[0] // 2
     return jnp.concatenate(
-        [left, jnp.concatenate([right[:48], right[48:]], axis=1)], axis=0
+        [left, jnp.concatenate([right[:half], right[half:]], axis=1)], axis=0
     ).astype(BF16)
 
 
 def undense(packed):
     wide = packed.astype(F32)
-    tail = wide[96:]
+    rows = 2 * packed.shape[0] // 3
+    tail = wide[rows:]
     high = jnp.concatenate([tail[:, :64], tail[:, 64:]], axis=0)
-    return wide[:96], jnp.concatenate([high, jnp.zeros((96, 64), F32)], axis=1)
+    return wide[:rows], jnp.concatenate([high, jnp.zeros((rows, 64), F32)], axis=1)
 
 
 def pack_kernel(x, y, e_ref, s_ref, c_ref, low, high):
     for n, own in enumerate((x, y)):
         for lv in range(2):
             base = 128 * (2 * n + lv)
+            east = jnp.concatenate([own[lv, lon].astype(F32) for lon in range(6)], axis=0)
+            e_ref[n, lv] = dense(east[:, :128], east[:, 128:])
             for lon in range(36):
                 if lon < 6:
-                    e_ref[n, lv, lon] = own[lv, lon]
                     at = pl.ds(base + 96 + lon, 3, stride=8)
                 else:
                     at = pl.ds(base + lon - 6, 3, stride=32)
@@ -361,9 +375,13 @@
         for lv in range(2):
             for lon in range(6):
                 keep(low, high, place(lv, lon), own[lv, 30 + lon])
-                keep(low, high, place(lv, 6 + lon), e[n, lv, lon])
             for lon in range(24):
                 keep(low, high, place(lv, 12 + lon), own[lv, 6 + lon].astype(F32)[16:])
+            left, right = undense(e[n, lv])
+            for lon in range(6):
+                at = place(lv, 6 + lon)
+                low[at : at + 24, :] = left[24 * lon : 24 * lon + 24]
+                high[at : at + 24, :] = right[24 * lon : 24 * lon + 24]
             left, right = undense(s[n, lv])
             cleft, cright = split(c[n, lv].astype(F32))
             for t in range(3):
@@ -386,7 +404,10 @@
     for lv in range(2):
         for lon in range(6):
             oe_ref[lv, lon] = kept(low, high, place(lv, lon), 24)
-            be_ref[lv, lon] = kept(low, high, place(lv, 6 + lon), 24)
+        east = jnp.concatenate(
+            [joined(low, high, pl.ds(place(lv, 6 + lon), 24)) for lon in range(6)], axis=0
+        )
+        be_ref[lv] = dense(east[:, :128], east[:, 128:])
         for lon in range(24):
             os_ref[lv, lon] = kept(low, high, place(lv, 12 + lon), 8)
         parts = []
@@ -431,27 +452,31 @@
     return four + four, pl.BlockSpec((2, 24, 24, D), lambda i: (i + first, 0, 0, 0))
 
 
-def early_windows(x, y, consts, pair_bias, last, steps):
+def early_windows(x, y, weights, pair_bias, last, steps):
     ins, out = inner_specs(0)
     return pl.pallas_call(
         early_kernel,
         grid=(steps,),
-        in_specs=ins + const_specs() + [whole((HEADS, W, W)), whole((1, 1))],
-        out_specs=[out, whole(GW), whole(GB), whole(BIAS)],
+        in_specs=ins
+        + [whole((1, D)), whole((D, 3 * D)), whole((D, D)), whole((HEADS, W, W)), whole((1, 1))],
+        out_specs=[out, whole(GW), whole(GB), whole(BIAS)] + const_specs()[1:],
         out_shape=[
             jax.ShapeDtypeStruct((x.shape[0], 24, 24, D), BF16),
             jax.ShapeDtypeStruct(GW, F32),
             jax.ShapeDtypeStruct(GB, F32),
             jax.ShapeDtypeStruct(BIAS, F32),
+            jax.ShapeDtypeStruct((D, 768), BF16),
+            jax.ShapeDtypeStruct((3 * D, D), BF16),
+            jax.ShapeDtypeStruct((D, D), BF16),
         ],
         scratch_shapes=halves(1152),
         compiler_params=PARAMS,
         cost_estimate=cost(6 * steps),
         name="early_windows",
-    )(x, x, x, x, y, y, y, y, *consts, pair_bias, last)
-
-
-def late_windows(x, y, consts, bias, sums, inner, first):
+    )(x, x, x, x, y, y, y, y, *weights, pair_bias, last)
+
+
+def late_windows(x, y, consts, bias, sums, core, inner, first):
     steps = x.shape[0] // 2 - first
     ins, out = inner_specs(first)
     return pl.pallas_call(
@@ -459,18 +484,20 @@
         grid=(steps,),
         in_specs=ins
         + const_specs()
-        + [whole(BIAS), whole(GW), whole(GB), pl.BlockSpec(memory_space=pl.ANY)],
-        out_specs=[out, whole((ROWS, 128))],
+        + [whole(BIAS), whole(GW), whole(GB), whole((1, 1)), pl.BlockSpec(memory_space=pl.ANY)],
+        out_specs=[out, whole((ROWS // 2, 128)), whole((ROWS // 2, 128))],
         out_shape=[
             jax.ShapeDtypeStruct(inner.shape, BF16),
-            jax.ShapeDtypeStruct((ROWS, 128), F32),
-        ],
-        scratch_shapes=[pltpu.VMEM(GW, F32), pltpu.VMEM(GB, F32)] + halves(1152),
-        input_output_aliases={15: 0},
+            jax.ShapeDtypeStruct((ROWS // 2, 128), BF16),
+            jax.ShapeDtypeStruct((ROWS // 2, 128), F32),
+        ],
+        scratch_shapes=[pltpu.VMEM(GW, F32), pltpu.VMEM(GB, F32), pltpu.VMEM((ROWS, 128), F32)]
+        + halves(1152),
+        input_output_aliases={16: 0},
         compiler_params=PARAMS,
         cost_estimate=cost(6 * steps),
         name="late_windows",
-    )(x, x, x, x, y, y, y, y, *consts, bias, *sums, inner)
+    )(x, x, x, x, y, y, y, y, *consts, bias, *sums, core, inner)
 
 
 def both(*rest):
@@ -489,9 +516,9 @@
         pack_kernel,
         grid=(levels // 2,),
         in_specs=[one(36, 24, D), one(36, 24, D)],
-        out_specs=[both(6, 24, D), both(144, 128), both(24, D)],
+        out_specs=[both(216, 128), both(144, 128), both(24, D)],
         out_shape=[
-            jax.ShapeDtypeStruct((2, levels, 6, 24, D), BF16),
+            jax.ShapeDtypeStruct((2, levels, 216, 128), BF16),
             jax.ShapeDtypeStruct((2, levels, 144, 128), BF16),
             jax.ShapeDtypeStruct((2, levels, 24, D), BF16),
         ],
@@ -506,13 +533,13 @@
     return pl.pallas_call(
         edge_kernel,
         grid=(levels // 2,),
-        in_specs=[one(36, 24, D), one(36, 24, D), both(6, 24, D), both(144, 128), both(24, D)]
+        in_specs=[one(36, 24, D), one(36, 24, D), both(216, 128), both(144, 128), both(24, D)]
         + const_specs()
         + [whole(BIAS), whole(GW), whole(GB)],
         out_specs=[
             one(6, 24, D),
             one(24, 8, D),
-            one(6, 24, D),
+            one(216, 128),
             one(144, 128),
             one(24, D),
             whole(GW),
@@ -521,7 +548,7 @@
         out_shape=[
             jax.ShapeDtypeStruct((levels, 6, 24, D), BF16),
             jax.ShapeDtypeStruct((levels, 24, 8, D), BF16),
-            jax.ShapeDtypeStruct((levels, 6, 24, D), BF16),
+            jax.ShapeDtypeStruct((levels, 216, 128), BF16),
             jax.ShapeDtypeStruct((levels, 144, 128), BF16),
             jax.ShapeDtypeStruct((levels, 24, D), BF16),
             jax.ShapeDtypeStruct(GW, F32),
@@ -547,9 +574,11 @@
             at = pl.ds(base + t, 6, stride=8)
             low[at, :] = cleft[8 * t : 8 * t + 6]
             high[at, :] = cright[8 * t : 8 * t + 6]
+        left, right = undense(gl[lv])
         for lon in range(36):
             if lon < 6:
-                rows = gl[lv, lon].astype(F32)
+                at = slice(24 * lon, 24 * lon + 24)
+                rows = jnp.concatenate([left[at], right[at, :64]], axis=1)
             elif lon < 30:
                 rows = inner[lv, lon - 6].astype(F32)
                 tail = os_[lv, lon - 6].astype(F32)
@@ -569,7 +598,7 @@
             one(24, 24, D),
             one(6, 24, D),
             one(24, 8, D),
-            one(6, 24, D),
+            one(216, 128),
             one(144, 128),
             one(24, D),
         ],
@@ -582,9 +611,15 @@
     )(inner, oe, os_, got_lon, got_lat, got_both)
 
 
-def finish_kernel(factor, sum_ref, gain_ref, w_ref, gq_ref, go_ref, gb_ref, gg_ref):
+def finish_kernel(
+    factor, line_ref, other_ref, core, gain_ref, w_ref, gq_ref, go_ref, gb_ref, gg_ref, sum_ref
+):
+    line, other = line_ref[...].astype(F32), other_ref[...].astype(F32)
+    first = core[...] == 0
+    sum_ref[: ROWS // 2] = jnp.where(first, line, other)
+    sum_ref[ROWS // 2 :] = jnp.where(first, other, line)
     both = jnp.concatenate(
-        [sum_ref[D * t : D * t + D].astype(F32) for t in range(6)], axis=1
+        [sum_ref[D * t : D * t + D] for t in range(6)], axis=1
     )
     gq = both[:, : 3 * D] * factor
     gq_ref[...] = gq
@@ -592,14 +627,14 @@
     products = (gq * w_ref[...].astype(F32)).T
     gg_ref[...] = jnp.sum(products, axis=0, keepdims=True) / gain_ref[...]
     base = WROWS + 6 * W
-    rest = sum_ref[base : base + W].astype(F32)
+    rest = sum_ref[base : base + W]
     for h in range(HEADS):
-        main = sum_ref[WROWS + W * h : WROWS + W * h + W].astype(F32)
+        main = sum_ref[WROWS + W * h : WROWS + W * h + W]
         turned = jnp.concatenate([main, rest[:, 16 * h : 16 * h + 16]], axis=1)
         gb_ref[h] = regroup(regroup(turned, True).T, True)
 
 
-def finish(sums, gain_row, qkv_weight, factor):
+def finish(line, other, core, gain_row, qkv_weight, factor):
     return pl.pallas_call(
         lambda *refs: finish_kernel(factor, *refs),
         out_shape=[
@@ -608,14 +643,10 @@
             jax.ShapeDtypeStruct((HEADS, W, W), F32),
             jax.ShapeDtypeStruct((1, D), F32),
         ],
+        scratch_shapes=[pltpu.VMEM((ROWS, 128), F32)],
         compiler_params=PARAMS,
         name="finish_sums",
-    )(sums, gain_row, qkv_weight)
-
-
-def make_consts(ln_gain, qkv_weight, out_weight):
-    wqkv = jnp.pad(qkv_weight.reshape(D, 3, D), ((0, 0), (0, 0), (0, 64))).reshape(D, 768)
-    return [ln_gain.reshape(1, D), wqkv, qkv_weight.T, out_weight.T]
+    )(line, other, core, gain_row, qkv_weight)
 
 
 def shift(value, axes, steps):
@@ -650,14 +681,9 @@
     return n % 2
 
 
-def sum_over_devices(sums):
-    lon = lax.axis_index("lon")
-    core = lon % 2
-    y = (lon // 2) % 4
-    halves = sums.reshape(2, ROWS // 2, 128)
-    low = halves.astype(BF16)
-    got = flip(lax.dynamic_index_in_dim(low, 1 - core, 0, keepdims=False), "lon", 1)
-    mine = lax.dynamic_index_in_dim(halves, core, 0, keepdims=False) + got.astype(F32)
+def sum_over_devices(give, mine):
+    y = (lax.axis_index("lon") // 2) % 4
+    mine = mine + flip(give, "lon", 1).astype(F32)
     quarters = mine.reshape(4, ROWS // 8, 128)
     qlow = quarters.astype(BF16)
     total = lax.dynamic_index_in_dim(quarters, y, 0, keepdims=False)
@@ -680,15 +706,7 @@
     line = jnp.concatenate(
         [lax.dynamic_index_in_dim(stacked, y ^ n, 0, keepdims=True) for n in range(4)], axis=0
     )
-    other = flip(line, "lon", 1)
-    pair = jnp.stack([line, other])
-    return jnp.concatenate(
-        [
-            lax.dynamic_index_in_dim(pair, core ^ n, 0, keepdims=False).reshape(ROWS // 2, 128)
-            for n in range(2)
-        ],
-        axis=0,
-    )
+    return line.reshape(ROWS // 2, 128), flip(line, "lon", 1).reshape(ROWS // 2, 128)
 
 
 def shift_x(value):
@@ -709,20 +727,25 @@
     s = shift(s, ("lat",), (-1,))
     e = shift(e, ("lon",), (-1,))
     c = shift(c, ("lon", "lat"), (-1, -1))
-    consts = make_consts(ln_gain, qkv_weight, out_weight)
+    gain = ln_gain.reshape(1, D)
+    core = (lax.axis_index("lon") % 2).astype(jnp.int32).reshape(1, 1)
     last = (lax.axis_index("lat") == lax.axis_size("lat") - 1).astype(jnp.int32).reshape(1, 1)
-    inner, gw, gb, bias = early_windows(x, y, consts, pair_bias, last, EARLY)
+    inner, gw, gb, bias, *laid = early_windows(
+        x, y, (gain, qkv_weight, out_weight), pair_bias, last, EARLY
+    )
+    consts = [gain] + laid
     oe, os_, be, bs, bc, gw, gb = edge_windows(x, y, e, s, c, consts, bias, (gw, gb))
     got_lat = shift(bs, ("lat",), (1,))
     got_lon = shift(be, ("lon",), (1,))
     got_both = shift(bc, ("lon", "lat"), (1, 1))
-    inner, sums = late_windows(x, y, consts, bias, (gw, gb), inner, EARLY)
-    sums = sum_over_devices(sums)
+    inner, give, mine = late_windows(x, y, consts, bias, (gw, gb), core, inner, EARLY)
+    give, got_lat, got_lon, got_both = lax.optimization_barrier((give, got_lat, got_lon, got_both))
+    sums = sum_over_devices(give, mine)
     grad_x = assemble(inner, oe, os_, got_lon, got_lat, got_both)
     factor = float(
         levels * lat_count * lax.axis_size("lat") * lon_count * lax.axis_size("lon")
     ) ** (-0.5)
-    gq, go, gbias, gg = finish(sums, ln_gain.reshape(1, D), qkv_weight, factor)
+    gq, go, gbias, gg = finish(*sums, core, gain, qkv_weight, factor)
     return (jnp.transpose(grad_x, (0, 2, 1, 3)), gq, go, gbias, gg.reshape(D))
 
 

time: 144 us -> 130 us (0.903); the launches traced: 144 us -> 128 us
  waiting for transfers between devices: 29.9 us -> 20.5 us
  local copies, waits for them, and re-layouts: 5.13 us -> 1.87 us
  Pallas kernels: 72.7 us -> 69.6 us
    ppermute x6, waiting for transfers between devices: 12.3 us -> 5.01 us  [shift(): return lax.ppermute(value, axes if len(axes) > 1 else axes[0], pairs)]
    ppermute x13, starting transfers between devices: 18.9 us -> 21.7 us  [moved(): return lax.ppermute(value, axis, [(n, to_of(n)) for n in range(count)])]
    pallas_call x1, Pallas kernels: 20.2 us -> 18.7 us  [early_windows(): pl.pallas_call(early_kernel, grid=(steps,), in_specs=ins + [whole((1, D))...]
    unnamed x26 -> x16, local copies, waits for them, and re-layouts: 3.07 us -> 1.81 us
  transfers between devices with their start and end apart: 20 -> 20, of which waited for: 13 -> 13; matrix products, arithmetic and copies ran while one was open for 1% -> 0% of each run, Pallas kernels for 17% -> 25%
where the time goes in v4:
time: 130 us; the launch traced here: 128 us
  Pallas kernels  69.6 us (54%)
  starting transfers between devices  33.9 us (26%)
  waiting for transfers between devices  20.5 us (16%)
  local copies, waits for them, and re-layouts  1.87 us (1%)
  other arithmetic  1.36 us (1%)
    pallas_call x1, Pallas kernels, edge_windows(): pl.pallas_call(edge_kernel, grid=(levels // 2,), in_specs=[one(36, 24, D)...  29.6 us
    ppermute x13, starting transfers between devices, moved(): return lax.ppermute(value, axis, [(n, to_of(n)) for n in range(count)])  21.7 us
    pallas_call x1, Pallas kernels, early_windows(): pl.pallas_call(early_kernel, grid=(steps,), in_specs=ins + [whole((1, D))...  18.7 us
    ppermute x13, waiting for transfers between devices, moved(): return lax.ppermute(value, axis, [(n, to_of(n)) for n in range(count)])  14.7 us
    ppermute x6, starting transfers between devices, shift(): return lax.ppermute(value, axes if len(axes) > 1 else axes[0], pairs)  12.1 us
    pallas_call x1, Pallas kernels, late_windows(): pl.pallas_call(late_kernel, grid=(steps,), in_specs=ins + const_specs() +...  8.51 us
    pallas_call x1, Pallas kernels, pack_halo(): pl.pallas_call(pack_kernel, grid=(levels // 2,), in_specs=[one(36, 24, D)...  5.22 us
    ppermute x6, waiting for transfers between devices, shift(): return lax.ppermute(value, axes if len(axes) > 1 else axes[0], pairs)  5.01 us
  transfers between devices with their start and end apart: 20, of which 13 were waited for; matrix products, arithmetic and copies ran while one was open for 0% of the time, Pallas kernels for 25%

profile of v4, /device:TPU:0, one launch (start us, length us, event | category | flops | bytes accessed | tf_op | source)
XLA Modules:
  0.0 128.0 jit_solution(10121904115480518428)
XLA Ops:
  0.6 5.2 %pack_halo.1 = (bf16[2,8,216,128]{3,2,1,0:T(8,128)(2,1)}, bf16[2,8,144,128]{3,2,1,0:T(8,128)(2,1)}, bf16[2,8,24,192]{3,2,1,0:T(8,128)(2,1)}) custom-call(bf16[8,36,24,192]{3,2,1,0:T(8,128)(2,1)} %bitcast.27, bf16[8,36,24,192]{3,2,1,0:T(8,128)(2,1)} %bitcast.37), custom_call_target="tpu_custom_call" | custom-call | tf_op jit(solution)/shard_map/pack_halo/pallas_call | solution.py:515
  5.8 3.5 %collective-permute-start = (bf16[2,8,216,128]{3,2,1,0:T(8,128)(2,1)}, bf16[2,8,216,128]{3,2,1,0:T(8,128)(2,1)S(1)}, u32[]{:S(2)}, u32[]{:S(2)}) collective-permute-start(bf16[2,8,216,128]{3,2,1,0:T(8,128)(2,1)} %get-tuple-element.37), channel_id=1, source_target_pairs={{0,120},{8,0},{16,8},{24,16},{32,24},{40,32},{48,40},{56,48},{64,5... | collective-permute-start | bytes 2654216 | tf_op jit(solution)/shard_map/ppermute | solution.py:668
  9.3 6.2 %collective-permute-start.1 = (bf16[2,8,144,128]{3,2,1,0:T(8,128)(2,1)}, bf16[2,8,144,128]{3,2,1,0:T(8,128)(2,1)S(1)}, u32[]{:S(2)}, u32[]{:S(2)}) collective-permute-start(bf16[2,8,144,128]{3,2,1,0:T(8,128)(2,1)} %get-tuple-element.38), channel_id=1, source_target_pairs={{0,7},{1,0},{2,1},{3,2},{4,3},{5,4},{6,5},{7,6},{8,15},{9,8},{10,9... | collective-permute-start | bytes 1769480 | tf_op jit(solution)/shard_map/ppermute | solution.py:668
  15.9 18.7 %early_windows.1 = (bf16[8,24,24,192]{3,2,1,0:T(8,128)(2,1)}, f32[4,192,192]{2,1,0:T(8,128)}, f32[144,896]{1,0:T(8,128)}, f32[2,144,896]{2,1,0:T(8,128)}, bf16[1...) custom-call(bf16[8,36,24,192]{3,2,1,0:T(8,128)(2,1)} %bitcast.28, ...), custom_call_target="tpu_custom_call" | custom-call | flops 3822059520 | bytes 2985984 | tf_op jit(solution)/shard_map/early_windows/pallas_call | solution.py:457
  34.6 2.3 %collective-permute-done.1.s = bf16[2,8,144,128]{3,2,1,0:T(8,128)(2,1)S(1)} collective-permute-done((bf16[2,8,144,128]{3,2,1,0:T(8,128)(2,1)}, bf16[2,8,144,128]{3,2,1,0:T(8,128)(2,1)S(1)}, u32[]{:S(2)}, u32[]{:S(2)}) %collective-permute-start.1) | collective-permute-done | bytes 589856 | tf_op jit(solution)/shard_map/ppermute | solution.py:668
  36.9 0.8 copy-done.6
  38.0 29.6 %edge_windows.1 = (bf16[8,6,24,192]{3,2,1,0:T(8,128)(2,1)}, bf16[8,24,8,192]{3,2,1,0:T(8,128)(2,1)}, bf16[8,216,128]{2,1,0:T(8,128)(2,1)}, bf16[8,144,128]{2,1,0...) custom-call(bf16[8,36,24,192]{3,2,1,0:T(8,128)(2,1)} %bitcast.32, ...), custom_call_target="tpu_custom_call" | custom-call | flops 5096079360 | bytes 3981312 | tf_op jit(solution)/shard_map/edge_windows/pallas_call | solution.py:533
  67.8 2.0 %collective-permute-start.3 = (bf16[8,144,128]{2,1,0:T(8,128)(2,1)}, bf16[8,144,128]{2,1,0:T(8,128)(2,1)S(1)}, u32[]{:S(2)}, u32[]{:S(2)}) collective-permute-start(bf16[8,144,128]{2,1,0:T(8,128)(2,1)} %get-tuple-element.49), channel_id=1, source_target_pairs={{0,1},{1,2},{2,3},{3,4},{4,5},{5,6},{6,7},{7,0},{8,9},{9,10},{10,1... | collective-permute-start | bytes 884744 | tf_op jit(solution)/shard_map/ppermute | solution.py:668
  69.8 8.5 %late_windows.1 = (bf16[8,24,24,192]{3,2,1,0:T(8,128)(2,1)}, bf16[1088,128]{1,0:T(8,128)(2,1)}, f32[1088,128]{1,0:T(8,128)}) custom-call(bf16[8,36,24,192]{3,2,1,0:T(8,128)(2,1)} %bitcast.33, bf16[8,36,24,192]{3,2,1,0:T(8,128)(2,1)} %bitcast.34, bf16[8,36,24,192]{3,2,1,0:T(8,128)(2,1)} %bitcast.35, ...), custom_call_target="tpu_custom_call", output_to_operand_aliasing={{0}: (16, {})} | custom-call | flops 1274019840 | bytes 995328 | tf_op jit(solution)/shard_map/late_windows/pallas_call | solution.py:482
  78.3 2.6 %collective-permute-done.5.gc = bf16[8,24,192]{2,1,0:T(8,128)(2,1)S(1)} collective-permute-done((bf16[8,24,192]{2,1,0:T(8,128)(2,1)}, bf16[8,24,192]{2,1,0:T(8,128)(2,1)S(1)}, u32[]{:S(2)}, u32[]{:S(2)}) %collective-permute-start.5) | collective-permute-done | bytes 73760 | tf_op jit(solution)/shard_map/ppermute | solution.py:668
  81.0 1.0 collective-permute-start.6
  82.0 1.4 %collective-permute-done.6 = bf16[1088,128]{1,0:T(8,128)(2,1)S(1)} collective-permute-done((bf16[1088,128]{1,0:T(8,128)(2,1)}, bf16[1088,128]{1,0:T(8,128)(2,1)S(1)}, u32[]{:S(2)}, u32[]{:S(2)}) %collective-permute-start.6) | collective-permute-done | bytes 278560 | tf_op jit(solution)/shard_map/ppermute | solution.py:673
  83.4 1.1 convert_add_fusion
  84.6 6.1 %collective-permute-start.9 = (bf16[272,128]{1,0:T(8,128)(2,1)S(1)}, bf16[272,128]{1,0:T(8,128)(2,1)S(1)}, u32[]{:S(2)}, u32[]{:S(2)}) collective-permute-start(bf16[272,128]{1,0:T(8,128)(2,1)S(1)} %get-tuple-element.68), channel_id=1, source_target_pairs={{0,48},{8,56},{16,32},{24,40},{32,16},{40,24},{48,0},{56,8},{64,11... | collective-permute-start | bytes 208904 | tf_op jit(solution)/shard_map/ppermute | solution.py:673
  90.8 1.4 %collective-permute-start.8 = (bf16[272,128]{1,0:T(8,128)(2,1)S(1)}, bf16[272,128]{1,0:T(8,128)(2,1)S(1)}, u32[]{:S(2)}, u32[]{:S(2)}) collective-permute-start(bf16[272,128]{1,0:T(8,128)(2,1)S(1)} %get-tuple-element.69), channel_id=1, source_target_pairs={{0,32},{8,40},{16,48},{24,56},{32,0},{40,8},{48,16},{56,24},{64,96... | collective-permute-start | bytes 208904 | tf_op jit(solution)/shard_map/ppermute | solution.py:673
  92.2 2.1 %collective-permute-done.9 = bf16[272,128]{1,0:T(8,128)(2,1)S(1)} collective-permute-done((bf16[272,128]{1,0:T(8,128)(2,1)S(1)}, bf16[272,128]{1,0:T(8,128)(2,1)S(1)}, u32[]{:S(2)}, u32[]{:S(2)}) %collective-permute-start.9) | collective-permute-done | bytes 69664 | tf_op jit(solution)/shard_map/ppermute | solution.py:673
  94.3 2.3 %collective-permute-done.8 = bf16[272,128]{1,0:T(8,128)(2,1)S(1)} collective-permute-done((bf16[272,128]{1,0:T(8,128)(2,1)S(1)}, bf16[272,128]{1,0:T(8,128)(2,1)S(1)}, u32[]{:S(2)}, u32[]{:S(2)}) %collective-permute-start.8) | collective-permute-done | bytes 69664 | tf_op jit(solution)/shard_map/ppermute | solution.py:673
  96.9 3.9 %collective-permute-start.10 = (bf16[272,128]{1,0:T(8,128)(2,1)S(1)}, bf16[272,128]{1,0:T(8,128)(2,1)S(1)}, u32[]{:S(2)}, u32[]{:S(2)}) collective-permute-start(bf16[272,128]{1,0:T(8,128)(2,1)S(1)} %get-tuple-element.61), channel_id=1, source_target_pairs={{0,2},{1,3},{2,0},{3,1},{4,6},{5,7},{6,4},{7,5},{8,10},{9,11},{10,... | collective-permute-start | bytes 208904 | tf_op jit(solution)/shard_map/ppermute | solution.py:673
  100.8 2.2 %collective-permute-done.12 = bf16[272,128]{1,0:T(8,128)(2,1)S(1)} collective-permute-done((bf16[272,128]{1,0:T(8,128)(2,1)S(1)}, bf16[272,128]{1,0:T(8,128)(2,1)S(1)}, u32[]{:S(2)}, u32[]{:S(2)}) %collective-permute-start.12) | collective-permute-done | bytes 69664 | tf_op jit(solution)/shard_map/ppermute | solution.py:673
  103.0 0.9 collective-permute-done.10
  104.3 4.4 %collective-permute-start.13 = (bf16[272,128]{1,0:T(8,128)(2,1)S(1)}, bf16[272,128]{1,0:T(8,128)(2,1)S(1)}, u32[]{:S(2)}, u32[]{:S(2)}) collective-permute-start(bf16[272,128]{1,0:T(8,128)(2,1)S(1)} %fusion.2), channel_id=1, source_target_pairs={{0,1},{1,0},{2,3},{3,2},{4,5},{5,4},{6,7},{7,6},{8,9},{9,8},{10,11... | collective-permute-start | bytes 208904 | tf_op jit(solution)/shard_map/ppermute | solution.py:673
  108.7 0.8 collective-permute-done.15
  109.5 2.2 %collective-permute-done.13 = bf16[272,128]{1,0:T(8,128)(2,1)S(1)} collective-permute-done((bf16[272,128]{1,0:T(8,128)(2,1)S(1)}, bf16[272,128]{1,0:T(8,128)(2,1)S(1)}, u32[]{:S(2)}, u32[]{:S(2)}) %collective-permute-start.13) | collective-permute-done | bytes 69664 | tf_op jit(solution)/shard_map/ppermute | solution.py:673
  111.8 1.4 %collective-permute-start.18 = (bf16[272,128]{1,0:T(8,128)(2,1)S(1)}, bf16[272,128]{1,0:T(8,128)(2,1)S(1)}, u32[]{:S(2)}, u32[]{:S(2)}) collective-permute-start(bf16[272,128]{1,0:T(8,128)(2,1)S(1)} %add_convert_fusion), channel_id=1, source_target_pairs={{0,48},{8,56},{16,32},{24,40},{32,16},{40,24},{48,0},{56,8},{64,11... | collective-permute-start | bytes 208904 | tf_op jit(solution)/shard_map/ppermute | solution.py:673
  113.2 2.1 %collective-permute-start.17 = (bf16[272,128]{1,0:T(8,128)(2,1)S(1)}, bf16[272,128]{1,0:T(8,128)(2,1)S(1)}, u32[]{:S(2)}, u32[]{:S(2)}) collective-permute-start(bf16[272,128]{1,0:T(8,128)(2,1)S(1)} %add_convert_fusion), channel_id=1, source_target_pairs={{0,32},{8,40},{16,48},{24,56},{32,0},{40,8},{48,16},{56,24},{64,96... | collective-permute-start | bytes 208904 | tf_op jit(solution)/shard_map/ppermute | solution.py:673
  115.3 0.7 collective-permute-start.16
  115.9 1.4 %collective-permute-done.18 = bf16[272,128]{1,0:T(8,128)(2,1)S(1)} collective-permute-done((bf16[272,128]{1,0:T(8,128)(2,1)S(1)}, bf16[272,128]{1,0:T(8,128)(2,1)S(1)}, u32[]{:S(2)}, u32[]{:S(2)}) %collective-permute-start.18) | collective-permute-done | bytes 69664 | tf_op jit(solution)/shard_map/ppermute | solution.py:673
  117.4 1.6 %collective-permute-done.17 = bf16[272,128]{1,0:T(8,128)(2,1)S(1)} collective-permute-done((bf16[272,128]{1,0:T(8,128)(2,1)S(1)}, bf16[272,128]{1,0:T(8,128)(2,1)S(1)}, u32[]{:S(2)}, u32[]{:S(2)}) %collective-permute-start.17) | collective-permute-done | bytes 69664 | tf_op jit(solution)/shard_map/ppermute | solution.py:673
  119.0 0.6 collective-permute-done.16
  119.8 4.8 %assemble.1 = bf16[8,36,24,192]{3,2,1,0:T(8,128)(2,1)} custom-call(bf16[8,24,24,192]{3,2,1,0:T(8,128)(2,1)} %get-tuple-element.45.inner, bf16[8,6,24,192]{3,2,1,0:T(8,128)(2,1)} %get-tuple-element.46.oe, bf16[8,24,8,192]{3,2,1,0:T(8,128)(2,1)} %get-tuple-element.47.os_, bf16[8,216,128]{2,1,0:T(8,128)(2,1)} %copy-done.1, bf16[8,144,128]{2,1,0:T(8,128)(2,1)} %copy-done.2, ...), custom_call_target="tpu_custom_call" | custom-call | bytes 6000000 | tf_op jit(solution)/shard_map/assemble/pallas_call | solution.py:594
  124.6 0.7 copy-done.3
  125.3 2.7 %finish_sums.1 = (f32[192,576]{1,0:T(8,128)}, f32[192,192]{1,0:T(8,128)}, f32[6,144,144]{2,1,0:T(8,128)}, f32[1,192]{1,0:T(1,128)}) custom-call(bf16[1088,128]{1,0:T(8,128)(2,1)} %bitcast.50, bf16[1088,128]{1,0:T(8,128)(2,1)} %bitcast.52, s32[1,1]{1,0:T(1,128)} %bitcast.4.core.refs_2_, f32[1,192]{1,0:T(1,128)} %bitcast.59, bf16[192,576]{1,0:T(8,128)(2,1)} %refs_4_.1), custom_call_target="tpu_custom_call" | custom-call | tf_op jit(solution)/shard_map/finish_sums/pallas_call | solution.py:638
  (39 shorter events, 2.0 us)
Async XLA Ops:
  5.8 31.1 %collective-permute-start = (bf16[2,8,216,128]{3,2,1,0:T(8,128)(2,1)}, bf16[2,8,216,128]{3,2,1,0:T(8,128)(2,1)S(1)}, u32[]{:S(2)}, u32[]{:S(2)}) collective-permute-start(bf16[2,8,216,128]{3,2,1,0:T(8,128)(2,1)} %get-tuple-element.37), channel_id=1, source_target_pairs={{0,120},{8,0},{16,8},{24,16},{32,24},{40,32},{48,40},{56,48},{64,5... | collective-permute-start | bytes 2654216 | tf_op jit(solution)/shard_map/ppermute | solution.py:668
  9.3 27.6 %collective-permute-start.1 = (bf16[2,8,144,128]{3,2,1,0:T(8,128)(2,1)}, bf16[2,8,144,128]{3,2,1,0:T(8,128)(2,1)S(1)}, u32[]{:S(2)}, u32[]{:S(2)}) collective-permute-start(bf16[2,8,144,128]{3,2,1,0:T(8,128)(2,1)} %get-tuple-element.38), channel_id=1, source_target_pairs={{0,7},{1,0},{2,1},{3,2},{4,3},{5,4},{6,5},{7,6},{8,15},{9,8},{10,9... | collective-permute-start | bytes 1769480 | tf_op jit(solution)/shard_map/ppermute | solution.py:668
  15.5 19.1 %collective-permute-start.2 = (bf16[2,8,24,192]{3,2,1,0:T(8,128)(2,1)}, bf16[2,8,24,192]{3,2,1,0:T(8,128)(2,1)S(1)}, u32[]{:S(2)}, u32[]{:S(2)}) collective-permute-start(bf16[2,8,24,192]{3,2,1,0:T(8,128)(2,1)} %get-tuple-element.39), channel_id=1, source_target_pairs={{0,127},{1,120},{2,121},{3,122},{4,123},{5,124},{6,125},{7,126},{8... | collective-permute-start | bytes 442376 | tf_op jit(solution)/shard_map/ppermute | solution.py:668
  34.6 2.3 %copy-start.7 = (bf16[2,8,24,192]{3,2,1,0:T(8,128)(2,1)}, bf16[2,8,24,192]{3,2,1,0:T(8,128)(2,1)S(1)}, u32[]{:S(2)}) copy-start(bf16[2,8,24,192]{3,2,1,0:T(8,128)(2,1)S(1)} %collective-permute-done.2.c) | copy-start | bytes 442372
  36.9 0.8 copy-start.6
  36.9 1.1 copy-start.5
  67.7 13.3 %collective-permute-start.4 = (bf16[8,216,128]{2,1,0:T(8,128)(2,1)}, bf16[8,216,128]{2,1,0:T(8,128)(2,1)S(1)}, u32[]{:S(2)}, u32[]{:S(2)}) collective-permute-start(bf16[8,216,128]{2,1,0:T(8,128)(2,1)} %get-tuple-element.50), channel_id=1, source_target_pairs={{0,8},{8,16},{16,24},{24,32},{32,40},{40,48},{48,56},{56,64},{64,7... | collective-permute-start | bytes 1327112 | tf_op jit(solution)/shard_map/ppermute | solution.py:668
  67.8 13.2 %collective-permute-start.3 = (bf16[8,144,128]{2,1,0:T(8,128)(2,1)}, bf16[8,144,128]{2,1,0:T(8,128)(2,1)S(1)}, u32[]{:S(2)}, u32[]{:S(2)}) collective-permute-start(bf16[8,144,128]{2,1,0:T(8,128)(2,1)} %get-tuple-element.49), channel_id=1, source_target_pairs={{0,1},{1,2},{2,3},{3,4},{4,5},{5,6},{6,7},{7,0},{8,9},{9,10},{10,1... | collective-permute-start | bytes 884744 | tf_op jit(solution)/shard_map/ppermute | solution.py:668
  69.8 11.1 %collective-permute-start.5 = (bf16[8,24,192]{2,1,0:T(8,128)(2,1)}, bf16[8,24,192]{2,1,0:T(8,128)(2,1)S(1)}, u32[]{:S(2)}, u32[]{:S(2)}) collective-permute-start(bf16[8,24,192]{2,1,0:T(8,128)(2,1)} %get-tuple-element.51), channel_id=1, source_target_pairs={{0,9},{1,10},{2,11},{3,12},{4,13},{5,14},{6,15},{7,8},{8,17},{9,18... | collective-permute-start | bytes 221192 | tf_op jit(solution)/shard_map/ppermute | solution.py:668
  80.9 38.9 %copy-start.4 = (bf16[8,24,192]{2,1,0:T(8,128)(2,1)}, bf16[8,24,192]{2,1,0:T(8,128)(2,1)S(1)}, u32[]{:S(2)}) copy-start(bf16[8,24,192]{2,1,0:T(8,128)(2,1)S(1)} %collective-permute-done.5.gc) | copy-start | bytes 221188
  81.0 38.8 %copy-start.2 = (bf16[8,144,128]{2,1,0:T(8,128)(2,1)}, bf16[8,144,128]{2,1,0:T(8,128)(2,1)S(1)}, u32[]{:S(2)}) copy-start(bf16[8,144,128]{2,1,0:T(8,128)(2,1)S(1)} %collective-permute-done.3.gs) | copy-start | bytes 884740
  81.0 38.8 %copy-start.1 = (bf16[8,216,128]{2,1,0:T(8,128)(2,1)}, bf16[8,216,128]{2,1,0:T(8,128)(2,1)S(1)}, u32[]{:S(2)}) copy-start(bf16[8,216,128]{2,1,0:T(8,128)(2,1)S(1)} %collective-permute-done.4.gl) | copy-start | bytes 1327108
  81.0 2.4 %collective-permute-start.6 = (bf16[1088,128]{1,0:T(8,128)(2,1)}, bf16[1088,128]{1,0:T(8,128)(2,1)S(1)}, u32[]{:S(2)}, u32[]{:S(2)}) collective-permute-start(bf16[1088,128]{1,0:T(8,128)(2,1)} %get-tuple-element.56), channel_id=1, source_target_pairs={{0,8},{8,0},{16,24},{24,16},{32,40},{40,32},{48,56},{56,48},{64,72... | collective-permute-start | bytes 835592 | tf_op jit(solution)/shard_map/ppermute | solution.py:673
  84.6 7.6 %collective-permute-start.7 = (bf16[272,128]{1,0:T(8,128)(2,1)S(1)}, bf16[272,128]{1,0:T(8,128)(2,1)S(1)}, u32[]{:S(2)}, u32[]{:S(2)}) collective-permute-start(bf16[272,128]{1,0:T(8,128)(2,1)S(1)} %get-tuple-element.67), channel_id=1, source_target_pairs={{0,16},{8,24},{16,0},{24,8},{32,48},{40,56},{48,32},{56,40},{64,80... | collective-permute-start | bytes 208904 | tf_op jit(solution)/shard_map/ppermute | solution.py:673
  84.6 9.6 %collective-permute-start.9 = (bf16[272,128]{1,0:T(8,128)(2,1)S(1)}, bf16[272,128]{1,0:T(8,128)(2,1)S(1)}, u32[]{:S(2)}, u32[]{:S(2)}) collective-permute-start(bf16[272,128]{1,0:T(8,128)(2,1)S(1)} %get-tuple-element.68), channel_id=1, source_target_pairs={{0,48},{8,56},{16,32},{24,40},{32,16},{40,24},{48,0},{56,8},{64,11... | collective-permute-start | bytes 208904 | tf_op jit(solution)/shard_map/ppermute | solution.py:673
  90.8 5.8 %collective-permute-start.8 = (bf16[272,128]{1,0:T(8,128)(2,1)S(1)}, bf16[272,128]{1,0:T(8,128)(2,1)S(1)}, u32[]{:S(2)}, u32[]{:S(2)}) collective-permute-start(bf16[272,128]{1,0:T(8,128)(2,1)S(1)} %get-tuple-element.69), channel_id=1, source_target_pairs={{0,32},{8,40},{16,48},{24,56},{32,0},{40,8},{48,16},{56,24},{64,96... | collective-permute-start | bytes 208904 | tf_op jit(solution)/shard_map/ppermute | solution.py:673
  96.6 6.3 %collective-permute-start.12 = (bf16[272,128]{1,0:T(8,128)(2,1)S(1)}, bf16[272,128]{1,0:T(8,128)(2,1)S(1)}, u32[]{:S(2)}, u32[]{:S(2)}) collective-permute-start(bf16[272,128]{1,0:T(8,128)(2,1)S(1)} %get-tuple-element.61), channel_id=1, source_target_pairs={{0,6},{1,7},{2,4},{3,5},{4,2},{5,3},{6,0},{7,1},{8,14},{9,15},{10,... | collective-permute-start | bytes 208904 | tf_op jit(solution)/shard_map/ppermute | solution.py:673
  96.9 6.1 %collective-permute-start.11 = (bf16[272,128]{1,0:T(8,128)(2,1)S(1)}, bf16[272,128]{1,0:T(8,128)(2,1)S(1)}, u32[]{:S(2)}, u32[]{:S(2)}) collective-permute-start(bf16[272,128]{1,0:T(8,128)(2,1)S(1)} %get-tuple-element.61), channel_id=1, source_target_pairs={{0,4},{1,5},{2,6},{3,7},{4,0},{5,1},{6,2},{7,3},{8,12},{9,13},{10,... | collective-permute-start | bytes 208904 | tf_op jit(solution)/shard_map/ppermute | solution.py:673
  96.9 6.9 %collective-permute-start.10 = (bf16[272,128]{1,0:T(8,128)(2,1)S(1)}, bf16[272,128]{1,0:T(8,128)(2,1)S(1)}, u32[]{:S(2)}, u32[]{:S(2)}) collective-permute-start(bf16[272,128]{1,0:T(8,128)(2,1)S(1)} %get-tuple-element.61), channel_id=1, source_target_pairs={{0,2},{1,3},{2,0},{3,1},{4,6},{5,7},{6,4},{7,5},{8,10},{9,11},{10,... | collective-permute-start | bytes 208904 | tf_op jit(solution)/shard_map/ppermute | solution.py:673
  103.9 5.6 %collective-permute-start.15 = (bf16[272,128]{1,0:T(8,128)(2,1)S(1)}, bf16[272,128]{1,0:T(8,128)(2,1)S(1)}, u32[]{:S(2)}, u32[]{:S(2)}) collective-permute-start(bf16[272,128]{1,0:T(8,128)(2,1)S(1)} %fusion.2), channel_id=1, source_target_pairs={{0,65},{1,64},{2,67},{3,66},{4,69},{5,68},{6,71},{7,70},{8,73},{9,... | collective-permute-start | bytes 208904 | tf_op jit(solution)/shard_map/ppermute | solution.py:719
  104.0 5.5 %collective-permute-start.14 = (bf16[272,128]{1,0:T(8,128)(2,1)S(1)}, bf16[272,128]{1,0:T(8,128)(2,1)S(1)}, u32[]{:S(2)}, u32[]{:S(2)}) collective-permute-start(bf16[272,128]{1,0:T(8,128)(2,1)S(1)} %fusion.2), channel_id=1, source_target_pairs={{0,64},{8,72},{16,80},{24,88},{32,96},{40,104},{48,112},{56,120},{... | collective-permute-start | bytes 208904 | tf_op jit(solution)/shard_map/ppermute | solution.py:673
  104.3 7.4 %collective-permute-start.13 = (bf16[272,128]{1,0:T(8,128)(2,1)S(1)}, bf16[272,128]{1,0:T(8,128)(2,1)S(1)}, u32[]{:S(2)}, u32[]{:S(2)}) collective-permute-start(bf16[272,128]{1,0:T(8,128)(2,1)S(1)} %fusion.2), channel_id=1, source_target_pairs={{0,1},{1,0},{2,3},{3,2},{4,5},{5,4},{6,7},{7,6},{8,9},{9,8},{10,11... | collective-permute-start | bytes 208904 | tf_op jit(solution)/shard_map/ppermute | solution.py:673
  111.8 5.6 %collective-permute-start.18 = (bf16[272,128]{1,0:T(8,128)(2,1)S(1)}, bf16[272,128]{1,0:T(8,128)(2,1)S(1)}, u32[]{:S(2)}, u32[]{:S(2)}) collective-permute-start(bf16[272,128]{1,0:T(8,128)(2,1)S(1)} %add_convert_fusion), channel_id=1, source_target_pairs={{0,48},{8,56},{16,32},{24,40},{32,16},{40,24},{48,0},{56,8},{64,11... | collective-permute-start | bytes 208904 | tf_op jit(solution)/shard_map/ppermute | solution.py:673
  113.2 5.8 %collective-permute-start.17 = (bf16[272,128]{1,0:T(8,128)(2,1)S(1)}, bf16[272,128]{1,0:T(8,128)(2,1)S(1)}, u32[]{:S(2)}, u32[]{:S(2)}) collective-permute-start(bf16[272,128]{1,0:T(8,128)(2,1)S(1)} %add_convert_fusion), channel_id=1, source_target_pairs={{0,32},{8,40},{16,48},{24,56},{32,0},{40,8},{48,16},{56,24},{64,96... | collective-permute-start | bytes 208904 | tf_op jit(solution)/shard_map/ppermute | solution.py:673
  115.3 4.3 %collective-permute-start.16 = (bf16[272,128]{1,0:T(8,128)(2,1)S(1)}, bf16[272,128]{1,0:T(8,128)(2,1)S(1)}, u32[]{:S(2)}, u32[]{:S(2)}) collective-permute-start(bf16[272,128]{1,0:T(8,128)(2,1)S(1)} %add_convert_fusion), channel_id=1, source_target_pairs={{0,16},{8,24},{16,0},{24,8},{32,48},{40,56},{48,32},{56,40},{64,80... | collective-permute-start | bytes 208904 | tf_op jit(solution)/shard_map/ppermute | solution.py:673
  119.7 4.9 %copy-start = (bf16[4,272,128]{2,1,0:T(8,128)(2,1)}, bf16[4,272,128]{2,1,0:T(8,128)(2,1)S(1)}, u32[]{:S(2)}) copy-start(bf16[4,272,128]{2,1,0:T(8,128)(2,1)S(1)} %pad_maximum_fusion.1) | copy-start | bytes 835588
  119.7 4.9 %collective-permute-start.19 = (bf16[4,272,128]{2,1,0:T(8,128)(2,1)S(1)}, bf16[4,272,128]{2,1,0:T(8,128)(2,1)S(1)}, u32[]{:S(2)}, u32[]{:S(2)}) collective-permute-start(bf16[4,272,128]{2,1,0:T(8,128)(2,1)S(1)} %pad_maximum_fusion.1), channel_id=1, source_target_pairs={{0,8},{8,0},{16,24},{24,16},{32,40},{40,32},{48,56},{56,48},{64,72... | collective-permute-start | bytes 835592 | tf_op jit(solution)/shard_map/ppermute | solution.py:673
  124.6 0.7 copy-start.3

commit v5 on v4

--- a/solution.py
+++ b/solution.py
@@ -59,6 +59,7 @@
 class Window:
     def __init__(self, fetch, put, bias_at, refs):
         self.fetch, self.put, self.bias_at, self.refs = fetch, put, bias_at, refs
+        self.also_first = self.also_last = lambda: None
 
     def front(self):
         r = self.refs
@@ -138,14 +139,14 @@
         self.put(self.dy + dx)
 
     def steps(self):
-        yield self.front
+        yield lambda: (self.front(), self.also_first())
         yield lambda: self.scores(0)
         yield lambda: (self.scores(1), self.softmax(0))
         yield lambda: (self.scores(2), self.softmax(1), self.products(0))
         yield lambda: (self.scores(3), self.softmax(2), self.products(1))
         yield lambda: (self.softmax(3), self.products(2))
         yield lambda: self.products(3)
-        yield self.back
+        yield lambda: (self.back(), self.also_last())
 
 
 STAGGER = 2
@@ -233,30 +234,30 @@
     bias_ref[1] = jnp.where(apart, F32(-1e30), flat)
 
 
-def start_windows(scratch, xs, ys, place):
-    for lv in range(2):
-        for lon in range(24):
-            keep(scratch[0], scratch[1], place(lv, lon), xs[lon // 6][lv, lon % 6])
-            keep(scratch[2], scratch[3], place(lv, lon), ys[lon // 6][lv, lon % 6])
-
-
 def inner_steps(xs, ys, consts, bias, dx_ref, gw_ref, gb_ref, scratch):
     def place(lv, lon):
         return 24 * (24 * (lon // 12) + 12 * lv + lon % 12)
 
-    start_windows(scratch, xs, ys, place)
+    def take(k):
+        for lv in range(2):
+            for lon in range(12 * k, 12 * k + 12):
+                keep(scratch[0], scratch[1], place(lv, lon), xs[lon // 6][lv, lon % 6])
+                keep(scratch[2], scratch[3], place(lv, lon), ys[lon // 6][lv, lon % 6])
+
+    def give(k):
+        for lv in range(2):
+            for lon in range(12 * k, 12 * k + 12):
+                dx_ref[lv, lon] = kept(scratch[4], scratch[5], place(lv, lon), 24)
+
+    take(0)
     refs = dict(zip(("gain", "wqkv", "wqkv_t", "wout_t"), consts), bias=bias, gb=gb_ref)
-    run_windows(
-        [
-            window_of(scratch, 576 * k + 3 + 6 * a, 24, 0, refs)
-            for k in range(2)
-            for a in range(3)
-        ],
-        gw_ref,
-    )
-    for lv in range(2):
-        for lon in range(24):
-            dx_ref[lv, lon] = kept(scratch[4], scratch[5], place(lv, lon), 24)
+    windows = [
+        window_of(scratch, 576 * k + 3 + 6 * a, 24, 0, refs) for k in range(2) for a in range(3)
+    ]
+    windows[1].also_first = lambda: take(1)
+    windows[2].also_last = lambda: give(0)
+    run_windows(windows, gw_ref)
+    give(1)
 
 
 def early_kernel(
@@ -329,6 +330,17 @@
     return wide[:rows], jnp.concatenate([high, jnp.zeros((rows, 64), F32)], axis=1)
 
 
+def dense_corner(rows):
+    right = jnp.concatenate([rows[:18, 128:], rows[18:, 128:]], axis=1)
+    return jnp.concatenate([rows[:, :128], right, jnp.zeros((2, 128), F32)], axis=0).astype(BF16)
+
+
+def undense_corner(packed):
+    wide = packed.astype(F32)
+    high = jnp.concatenate([wide[36:54, :64], wide[36:54, 64:]], axis=0)
+    return wide[:36], jnp.concatenate([high, jnp.zeros((36, 64), F32)], axis=1)
+
+
 def pack_kernel(x, y, e_ref, s_ref, c_ref, low, high):
     for n, own in enumerate((x, y)):
         for lv in range(2):
@@ -344,7 +356,16 @@
                 low[at, :] = left[:3]
                 high[at, :] = right[:3]
             s_ref[n, lv] = dense(low[base : base + 96, :], high[base : base + 96, :][:, :64])
-            c_ref[n, lv] = joined(low, high, pl.ds(base + 96, 24)).astype(BF16)
+        c_ref[n, 0] = dense_corner(
+            jnp.concatenate(
+                [
+                    joined(low, high, pl.ds(128 * (2 * n + lv) + 96 + 8 * t, 8))[:6]
+                    for lv in range(2)
+                    for t in range(3)
+                ],
+                axis=0,
+            )
+        )
 
 
 def edge_kernel(
@@ -372,6 +393,7 @@
 
     for n, own in enumerate((x, y)):
         low, high = scratch[2 * n], scratch[2 * n + 1]
+        cleft, cright = undense_corner(c[n, 0])
         for lv in range(2):
             for lon in range(6):
                 keep(low, high, place(lv, lon), own[lv, 30 + lon])
@@ -383,14 +405,14 @@
                 low[at : at + 24, :] = left[24 * lon : 24 * lon + 24]
                 high[at : at + 24, :] = right[24 * lon : 24 * lon + 24]
             left, right = undense(s[n, lv])
-            cleft, cright = split(c[n, lv].astype(F32))
             for t in range(3):
                 for m, at in enumerate(south(lv, t)):
                     rows = slice(32 * t + 12 * m, 32 * t + min(12 * m + 12, 30))
                     low[at, :] = left[rows]
                     high[at, :] = right[rows]
-                low[corner(lv, t), :] = cleft[8 * t : 8 * t + 6]
-                high[corner(lv, t), :] = cright[8 * t : 8 * t + 6]
+                rows = slice(18 * lv + 6 * t, 18 * lv + 6 * t + 6)
+                low[corner(lv, t), :] = cleft[rows]
+                high[corner(lv, t), :] = cright[rows]
     refs = dict(
         gain=gain, wqkv=wqkv, wqkv_t=wqkv_t, wout_t=wout_t, bias=bias, gb=gb_ref
     )
@@ -401,6 +423,7 @@
     )
     low, high = scratch[4], scratch[5]
     pad = jnp.zeros((2, D), F32)
+    corners = []
     for lv in range(2):
         for lon in range(6):
             oe_ref[lv, lon] = kept(low, high, place(lv, lon), 24)
@@ -411,13 +434,12 @@
         for lon in range(24):
             os_ref[lv, lon] = kept(low, high, place(lv, 12 + lon), 8)
         parts = []
-        corners = []
         for t in range(3):
             parts += [joined(low, high, at) for at in south(lv, t)] + [pad]
-            corners += [joined(low, high, corner(lv, t)), pad]
+            corners.append(joined(low, high, corner(lv, t)))
         rows = jnp.concatenate(parts, axis=0)
         bs_ref[lv] = dense(rows[:, :128], rows[:, 128:])
-        bc_ref[lv] = jnp.concatenate(corners, axis=0).astype(BF16)
+    bc_ref[0] = dense_corner(jnp.concatenate(corners, axis=0))
 
 
 def whole(shape):
@@ -510,17 +532,25 @@
     return pl.BlockSpec((2,) + rest, lambda i: (i,) + zeros)
 
 
+def both_corner():
+    return pl.BlockSpec((2, 1, 56, 128), lambda i: (0, i, 0, 0))
+
+
+def one_corner():
+    return pl.BlockSpec((1, 56, 128), lambda i: (i, 0, 0))
+
+
 def pack_halo(x, y):
     levels = x.shape[0]
     return pl.pallas_call(
         pack_kernel,
         grid=(levels // 2,),
         in_specs=[one(36, 24, D), one(36, 24, D)],
-        out_specs=[both(216, 128), both(144, 128), both(24, D)],
+        out_specs=[both(216, 128), both(144, 128), both_corner()],
         out_shape=[
             jax.ShapeDtypeStruct((2, levels, 216, 128), BF16),
             jax.ShapeDtypeStruct((2, levels, 144, 128), BF16),
-            jax.ShapeDtypeStruct((2, levels, 24, D), BF16),
+            jax.ShapeDtypeStruct((2, levels // 2, 56, 128), BF16),
         ],
         scratch_shapes=[pltpu.VMEM((512, 128), F32), pltpu.VMEM((512, 128), F32)],
         compiler_params=PARAMS,
@@ -533,7 +563,7 @@
     return pl.pallas_call(
         edge_kernel,
         grid=(levels // 2,),
-        in_specs=[one(36, 24, D), one(36, 24, D), both(216, 128), both(144, 128), both(24, D)]
+        in_specs=[one(36, 24, D), one(36, 24, D), both(216, 128), both(144, 128), both_corner()]
         + const_specs()
         + [whole(BIAS), whole(GW), whole(GB)],
         out_specs=[
@@ -541,7 +571,7 @@
             one(24, 8, D),
             one(216, 128),
             one(144, 128),
-            one(24, D),
+            one_corner(),
             whole(GW),
             whole(GB),
         ],
@@ -550,7 +580,7 @@
             jax.ShapeDtypeStruct((levels, 24, 8, D), BF16),
             jax.ShapeDtypeStruct((levels, 216, 128), BF16),
             jax.ShapeDtypeStruct((levels, 144, 128), BF16),
-            jax.ShapeDtypeStruct((levels, 24, D), BF16),
+            jax.ShapeDtypeStruct((levels // 2, 56, 128), BF16),
             jax.ShapeDtypeStruct(GW, F32),
             jax.ShapeDtypeStruct(GB, F32),
         ],
@@ -561,19 +591,21 @@
     )(x, y, e, s, c, *consts, bias, *sums)
 
 
-def assemble_kernel(inner, oe, os_, gl, gs, gc, out_ref, low, high):
+def assemble_kernel(inner, oe, os_, gl, gs, gc, *rest):
+    out_ref, low, high = rest[-3:]
     row = lax.broadcasted_iota(jnp.int32, (8, D), 0)
+    cleft, cright = undense_corner(gc[0])
     for lv in range(2):
         base = 288 * lv
         left, right = undense(gs[lv])
-        cleft, cright = split(gc[lv].astype(F32))
         for t in range(3):
             at = pl.ds(base + 48 + t, 30, stride=8)
             low[at, :] = left[32 * t : 32 * t + 30]
             high[at, :] = right[32 * t : 32 * t + 30]
             at = pl.ds(base + t, 6, stride=8)
-            low[at, :] = cleft[8 * t : 8 * t + 6]
-            high[at, :] = cright[8 * t : 8 * t + 6]
+            rows = slice(18 * lv + 6 * t, 18 * lv + 6 * t + 6)
+            low[at, :] = cleft[rows]
+            high[at, :] = cright[rows]
         left, right = undense(gl[lv])
         for lon in range(36):
             if lon < 6:
@@ -589,26 +621,39 @@
             out_ref[lv, lon] = jnp.concatenate([head, rows[8:]], axis=0).astype(BF16)
 
 
-def assemble(inner, oe, os_, got_lon, got_lat, got_both):
-    levels = inner.shape[0]
+def assemble(first, steps, grad_x, inner, oe, os_, got_lon, got_lat, got_both):
+    def at(count, *rest):
+        zeros = (0,) * len(rest)
+        return pl.BlockSpec((count,) + rest, lambda i: (i + first,) + zeros)
+
+    ins = [inner, oe, os_, got_lon, got_lat, got_both]
+    specs = [
+        at(2, 24, 24, D),
+        at(2, 6, 24, D),
+        at(2, 24, 8, D),
+        at(2, 216, 128),
+        at(2, 144, 128),
+        at(1, 56, 128),
+    ]
+    aliases = {}
+    if grad_x is not None:
+        ins.append(grad_x)
+        specs.append(pl.BlockSpec(memory_space=pl.ANY))
+        aliases = {6: 0}
     return pl.pallas_call(
         assemble_kernel,
-        grid=(levels // 2,),
-        in_specs=[
-            one(24, 24, D),
-            one(6, 24, D),
-            one(24, 8, D),
-            one(216, 128),
-            one(144, 128),
-            one(24, D),
-        ],
-        out_specs=one(36, 24, D),
-        out_shape=jax.ShapeDtypeStruct((levels, 36, 24, D), BF16),
+        grid=(steps,),
+        in_specs=specs,
+        out_specs=at(2, 36, 24, D),
+        out_shape=jax.ShapeDtypeStruct((inner.shape[0], 36, 24, D), BF16),
         scratch_shapes=[pltpu.VMEM((576, 128), F32), pltpu.VMEM((576, 128), F32)],
+        input_output_aliases=aliases,
         compiler_params=PARAMS,
-        cost_estimate=pl.CostEstimate(flops=0, bytes_accessed=6_000_000, transcendentals=0),
+        cost_estimate=pl.CostEstimate(
+            flops=0, bytes_accessed=1_500_000 * steps, transcendentals=0
+        ),
         name="assemble",
-    )(inner, oe, os_, got_lon, got_lat, got_both)
+    )(*ins)
 
 
 def finish_kernel(
@@ -681,7 +726,7 @@
     return n % 2
 
 
-def sum_over_devices(give, mine):
+def sum_over_devices(give, mine, beside):
     y = (lax.axis_index("lon") // 2) % 4
     mine = mine + flip(give, "lon", 1).astype(F32)
     quarters = mine.reshape(4, ROWS // 8, 128)
@@ -690,9 +735,11 @@
     for step in range(1, 4):
         piece = lax.dynamic_index_in_dim(qlow, y ^ step, 0, keepdims=False)
         total = total + flip(piece, "lon", 2 * step).astype(F32)
+    total, grad_x = lax.optimization_barrier((total, beside(0, None)))
     low = total.astype(BF16)
     for step in range(1, 4):
         total = total + flip(low, "lat", 2 * step).astype(F32)
+    total, grad_x = lax.optimization_barrier((total, beside(1, grad_x)))
     low = total.astype(BF16)
     total = (
         total
@@ -706,7 +753,8 @@
     line = jnp.concatenate(
         [lax.dynamic_index_in_dim(stacked, y ^ n, 0, keepdims=True) for n in range(4)], axis=0
     )
-    return line.reshape(ROWS // 2, 128), flip(line, "lon", 1).reshape(ROWS // 2, 128)
+    other = flip(line, "lon", 1)
+    return line.reshape(ROWS // 2, 128), other.reshape(ROWS // 2, 128), grad_x
 
 
 def shift_x(value):
@@ -740,8 +788,12 @@
     got_both = shift(bc, ("lon", "lat"), (1, 1))
     inner, give, mine = late_windows(x, y, consts, bias, (gw, gb), core, inner, EARLY)
     give, got_lat, got_lon, got_both = lax.optimization_barrier((give, got_lat, got_lon, got_both))
-    sums = sum_over_devices(give, mine)
-    grad_x = assemble(inner, oe, os_, got_lon, got_lat, got_both)
+    half = levels // 4
+
+    def beside(part, grad_x):
+        return assemble(half * part, half, grad_x, inner, oe, os_, got_lon, got_lat, got_both)
+
+    *sums, grad_x = sum_over_devices(give, mine, beside)
     factor = float(
         levels * lat_count * lax.axis_size("lat") * lon_count * lax.axis_size("lon")
     ) ** (-0.5)

time: 130 us -> 123 us (0.946)
  waiting for transfers between devices: 20.5 us -> 14.3 us
    ppermute x13, waiting for transfers between devices: 14.7 us -> 10.8 us  [moved(): return lax.ppermute(value, axis, [(n, to_of(n)) for n in range(count)])]
    ppermute x6, waiting for transfers between devices: 5.01 us -> 2.69 us  [shift(): return lax.ppermute(value, axes if len(axes) > 1 else axes[0], pairs)]
    ppermute x13, starting transfers between devices: 21.7 us -> 19.6 us  [moved(): return lax.ppermute(value, axis, [(n, to_of(n)) for n in range(count)])]
    pallas_call x1 -> x2, Pallas kernels: 4.8 us -> 5.45 us  [assemble(): pl.pallas_call(assemble_kernel, grid=(steps,), in_specs=specs, out_specs=...]
  transfers between devices with their start and end apart: 20 -> 20, of which waited for: 13 -> 12; matrix products, arithmetic and copies ran while one was open for 0% -> 0% of each run, Pallas kernels for 25% -> 27%
where the time goes in v5:
time: 123 us; the launch traced here: 122 us
  Pallas kernels  69.6 us (57%)
  starting transfers between devices  33.9 us (28%)
  waiting for transfers between devices  14.3 us (12%)
  local copies, waits for them, and re-layouts  1.88 us (2%)
  other arithmetic  1.34 us (1%)
    pallas_call x1, Pallas kernels, edge_windows(): pl.pallas_call(edge_kernel, grid=(levels // 2,), in_specs=[one(36, 24, D)...  29.1 us
    ppermute x13, starting transfers between devices, moved(): return lax.ppermute(value, axis, [(n, to_of(n)) for n in range(count)])  19.6 us
    pallas_call x1, Pallas kernels, early_windows(): pl.pallas_call(early_kernel, grid=(steps,), in_specs=ins + [whole((1, D))...  18.7 us
    ppermute x6, starting transfers between devices, shift(): return lax.ppermute(value, axes if len(axes) > 1 else axes[0], pairs)  13.2 us
    ppermute x13, waiting for transfers between devices, moved(): return lax.ppermute(value, axis, [(n, to_of(n)) for n in range(count)])  10.8 us
    pallas_call x1, Pallas kernels, late_windows(): pl.pallas_call(late_kernel, grid=(steps,), in_specs=ins + const_specs() +...  8.51 us
    pallas_call x2, Pallas kernels, assemble(): pl.pallas_call(assemble_kernel, grid=(steps,), in_specs=specs, out_specs=...  5.45 us
    pallas_call x1, Pallas kernels, pack_halo(): pl.pallas_call(pack_kernel, grid=(levels // 2,), in_specs=[one(36, 24, D)...  5.2 us
  transfers between devices with their start and end apart: 20, of which 12 were waited for; matrix products, arithmetic and copies ran while one was open for 0% of the time, Pallas kernels for 27%

profile of v5, /device:TPU:0, one launch (start us, length us, event | category | flops | bytes accessed | tf_op | source)
XLA Modules:
  0.0 121.8 jit_solution(8118285723652759578)
XLA Ops:
  0.6 5.2 %pack_halo.1 = (bf16[2,8,216,128]{3,2,1,0:T(8,128)(2,1)}, bf16[2,8,144,128]{3,2,1,0:T(8,128)(2,1)}, bf16[2,4,56,128]{3,2,1,0:T(8,128)(2,1)}) custom-call(bf16[8,36,24,192]{3,2,1,0:T(8,128)(2,1)} %bitcast.26, bf16[8,36,24,192]{3,2,1,0:T(8,128)(2,1)} %bitcast.36), custom_call_target="tpu_custom_call" | custom-call | tf_op jit(solution)/shard_map/pack_halo/pallas_call | solution.py:545
  5.8 3.5 %collective-permute-start = (bf16[2,8,216,128]{3,2,1,0:T(8,128)(2,1)}, bf16[2,8,216,128]{3,2,1,0:T(8,128)(2,1)S(1)}, u32[]{:S(2)}, u32[]{:S(2)}) collective-permute-start(bf16[2,8,216,128]{3,2,1,0:T(8,128)(2,1)} %get-tuple-element.41), channel_id=1, source_target_pairs={{0,120},{8,0},{16,8},{24,16},{32,24},{40,32},{48,40},{56,48},{64,5... | collective-permute-start | bytes 2654216 | tf_op jit(solution)/shard_map/ppermute | solution.py:713
  9.3 6.2 %collective-permute-start.1 = (bf16[2,8,144,128]{3,2,1,0:T(8,128)(2,1)}, bf16[2,8,144,128]{3,2,1,0:T(8,128)(2,1)S(1)}, u32[]{:S(2)}, u32[]{:S(2)}) collective-permute-start(bf16[2,8,144,128]{3,2,1,0:T(8,128)(2,1)} %get-tuple-element.42), channel_id=1, source_target_pairs={{0,7},{1,0},{2,1},{3,2},{4,3},{5,4},{6,5},{7,6},{8,15},{9,8},{10,9... | collective-permute-start | bytes 1769480 | tf_op jit(solution)/shard_map/ppermute | solution.py:713
  15.8 18.7 %early_windows.1 = (bf16[8,24,24,192]{3,2,1,0:T(8,128)(2,1)}, f32[4,192,192]{2,1,0:T(8,128)}, f32[144,896]{1,0:T(8,128)}, f32[2,144,896]{2,1,0:T(8,128)}, bf16[1...) custom-call(bf16[8,36,24,192]{3,2,1,0:T(8,128)(2,1)} %bitcast.27, ...), custom_call_target="tpu_custom_call" | custom-call | flops 3822059520 | bytes 2985984 | tf_op jit(solution)/shard_map/early_windows/pallas_call | solution.py:479
  35.2 0.8 copy-done.6
  36.3 29.1 %edge_windows.1 = (bf16[8,6,24,192]{3,2,1,0:T(8,128)(2,1)}, bf16[8,24,8,192]{3,2,1,0:T(8,128)(2,1)}, bf16[8,216,128]{2,1,0:T(8,128)(2,1)}, bf16[8,144,128]{2,1,0...) custom-call(bf16[8,36,24,192]{3,2,1,0:T(8,128)(2,1)} %bitcast.31, ...), custom_call_target="tpu_custom_call" | custom-call | flops 5096079360 | bytes 3981312 | tf_op jit(solution)/shard_map/edge_windows/pallas_call | solution.py:563
  65.6 2.9 %collective-permute-start.3 = (bf16[8,144,128]{2,1,0:T(8,128)(2,1)}, bf16[8,144,128]{2,1,0:T(8,128)(2,1)S(1)}, u32[]{:S(2)}, u32[]{:S(2)}) collective-permute-start(bf16[8,144,128]{2,1,0:T(8,128)(2,1)} %get-tuple-element.51), channel_id=1, source_target_pairs={{0,1},{1,2},{2,3},{3,4},{4,5},{5,6},{6,7},{7,0},{8,9},{9,10},{10,1... | collective-permute-start | bytes 884744 | tf_op jit(solution)/shard_map/ppermute | solution.py:713
  68.5 8.5 %late_windows.1 = (bf16[8,24,24,192]{3,2,1,0:T(8,128)(2,1)}, bf16[1088,128]{1,0:T(8,128)(2,1)}, f32[1088,128]{1,0:T(8,128)}) custom-call(bf16[8,36,24,192]{3,2,1,0:T(8,128)(2,1)} %bitcast.32, bf16[8,36,24,192]{3,2,1,0:T(8,128)(2,1)} %bitcast.33, bf16[8,36,24,192]{3,2,1,0:T(8,128)(2,1)} %bitcast.34, ...), custom_call_target="tpu_custom_call", output_to_operand_aliasing={{0}: (16, {})} | custom-call | flops 1274019840 | bytes 995328 | tf_op jit(solution)/shard_map/late_windows/pallas_call | solution.py:504
  77.0 1.1 collective-permute-done.5.gc
  78.1 1.0 collective-permute-done.3.gs
  79.7 1.4 %collective-permute-done.6 = bf16[1088,128]{1,0:T(8,128)(2,1)S(1)} collective-permute-done((bf16[1088,128]{1,0:T(8,128)(2,1)}, bf16[1088,128]{1,0:T(8,128)(2,1)S(1)}, u32[]{:S(2)}, u32[]{:S(2)}) %collective-permute-start.6) | collective-permute-done | bytes 278560 | tf_op jit(solution)/shard_map/ppermute | solution.py:718
  81.1 1.1 convert_add_fusion
  82.8 5.1 %collective-permute-start.9 = (bf16[272,128]{1,0:T(8,128)(2,1)S(1)}, bf16[272,128]{1,0:T(8,128)(2,1)S(1)}, u32[]{:S(2)}, u32[]{:S(2)}) collective-permute-start(bf16[272,128]{1,0:T(8,128)(2,1)S(1)} %get-tuple-element.74), channel_id=1, source_target_pairs={{0,48},{8,56},{16,32},{24,40},{32,16},{40,24},{48,0},{56,8},{64,11... | collective-permute-start | bytes 208904 | tf_op jit(solution)/shard_map/ppermute | solution.py:718
  87.8 1.4 %collective-permute-start.8 = (bf16[272,128]{1,0:T(8,128)(2,1)S(1)}, bf16[272,128]{1,0:T(8,128)(2,1)S(1)}, u32[]{:S(2)}, u32[]{:S(2)}) collective-permute-start(bf16[272,128]{1,0:T(8,128)(2,1)S(1)} %get-tuple-element.75), channel_id=1, source_target_pairs={{0,32},{8,40},{16,48},{24,56},{32,0},{40,8},{48,16},{56,24},{64,96... | collective-permute-start | bytes 208904 | tf_op jit(solution)/shard_map/ppermute | solution.py:718
  89.2 2.7 %assemble.2.rest_0_ = bf16[8,36,24,192]{3,2,1,0:T(8,128)(2,1)} custom-call(bf16[8,24,24,192]{3,2,1,0:T(8,128)(2,1)} %get-tuple-element.55.inner, bf16[8,6,24,192]{3,2,1,0:T(8,128)(2,1)} %get-tuple-element.56.oe, bf16[8,24,8,192]{3,2,1,0:T(8,128)(2,1)} %get-tuple-element.57.os_, bf16[8,216,128]{2,1,0:T(8,128)(2,1)} %copy-done, ...), custom_call_target="tpu_custom_call" | custom-call | bytes 3000000 | tf_op jit(solution)/shard_map/assemble/pallas_call | solution.py:643
  92.0 1.7 %collective-permute-done.8 = bf16[272,128]{1,0:T(8,128)(2,1)S(1)} collective-permute-done((bf16[272,128]{1,0:T(8,128)(2,1)S(1)}, bf16[272,128]{1,0:T(8,128)(2,1)S(1)}, u32[]{:S(2)}, u32[]{:S(2)}) %collective-permute-start.8) | collective-permute-done | bytes 69664 | tf_op jit(solution)/shard_map/ppermute | solution.py:718
  93.7 1.1 collective-permute-start.12
  94.8 3.1 %collective-permute-start.10 = (bf16[272,128]{1,0:T(8,128)(2,1)S(1)}, bf16[272,128]{1,0:T(8,128)(2,1)S(1)}, u32[]{:S(2)}, u32[]{:S(2)}) collective-permute-start(bf16[272,128]{1,0:T(8,128)(2,1)S(1)} %convert_element_type.48), channel_id=1, source_target_pairs={{0,2},{1,3},{2,0},{3,1},{4,6},{5,7},{6,4},{7,5},{8,10},{9,11},{10,... | collective-permute-start | bytes 208904 | tf_op jit(solution)/shard_map/ppermute | solution.py:718
  97.9 2.7 %assemble.3 = bf16[8,36,24,192]{3,2,1,0:T(8,128)(2,1)} custom-call(bf16[8,24,24,192]{3,2,1,0:T(8,128)(2,1)} %get-tuple-element.55.inner, bf16[8,6,24,192]{3,2,1,0:T(8,128)(2,1)} %get-tuple-element.56.oe, bf16[8,24,8,192]{3,2,1,0:T(8,128)(2,1)} %get-tuple-element.57.os_, bf16[8,216,128]{2,1,0:T(8,128)(2,1)} %copy-done, ...), custom_call_target="tpu_custom_call", output_to_operand_aliasing={{}: (6, {})} | custom-call | bytes 3000000 | tf_op jit(solution)/shard_map/assemble/pallas_call | solution.py:643
  101.0 1.2 collective-permute-start.15
  102.1 0.6 collective-permute-start.14
  102.7 3.0 %collective-permute-start.13 = (bf16[272,128]{1,0:T(8,128)(2,1)S(1)}, bf16[272,128]{1,0:T(8,128)(2,1)S(1)}, u32[]{:S(2)}, u32[]{:S(2)}) collective-permute-start(bf16[272,128]{1,0:T(8,128)(2,1)S(1)} %convert_element_type.52), channel_id=1, source_target_pairs={{0,1},{1,0},{2,3},{3,2},{4,5},{5,4},{6,7},{7,6},{8,9},{9,8},{10,11... | collective-permute-start | bytes 208904 | tf_op jit(solution)/shard_map/ppermute | solution.py:718
  105.8 0.8 collective-permute-done.15
  106.6 2.2 %collective-permute-done.13 = bf16[272,128]{1,0:T(8,128)(2,1)S(1)} collective-permute-done((bf16[272,128]{1,0:T(8,128)(2,1)S(1)}, bf16[272,128]{1,0:T(8,128)(2,1)S(1)}, u32[]{:S(2)}, u32[]{:S(2)}) %collective-permute-start.13) | collective-permute-done | bytes 69664 | tf_op jit(solution)/shard_map/ppermute | solution.py:718
  108.8 1.4 %collective-permute-start.18 = (bf16[272,128]{1,0:T(8,128)(2,1)S(1)}, bf16[272,128]{1,0:T(8,128)(2,1)S(1)}, u32[]{:S(2)}, u32[]{:S(2)}) collective-permute-start(bf16[272,128]{1,0:T(8,128)(2,1)S(1)} %add_convert_fusion), channel_id=1, source_target_pairs={{0,48},{8,56},{16,32},{24,40},{32,16},{40,24},{48,0},{56,8},{64,11... | collective-permute-start | bytes 208904 | tf_op jit(solution)/shard_map/ppermute | solution.py:718
  110.2 2.1 %collective-permute-start.17 = (bf16[272,128]{1,0:T(8,128)(2,1)S(1)}, bf16[272,128]{1,0:T(8,128)(2,1)S(1)}, u32[]{:S(2)}, u32[]{:S(2)}) collective-permute-start(bf16[272,128]{1,0:T(8,128)(2,1)S(1)} %add_convert_fusion), channel_id=1, source_target_pairs={{0,32},{8,40},{16,48},{24,56},{32,0},{40,8},{48,16},{56,24},{64,96... | collective-permute-start | bytes 208904 | tf_op jit(solution)/shard_map/ppermute | solution.py:718
  112.3 0.7 collective-permute-start.16
  113.0 1.4 %collective-permute-done.18 = bf16[272,128]{1,0:T(8,128)(2,1)S(1)} collective-permute-done((bf16[272,128]{1,0:T(8,128)(2,1)S(1)}, bf16[272,128]{1,0:T(8,128)(2,1)S(1)}, u32[]{:S(2)}, u32[]{:S(2)}) %collective-permute-start.18) | collective-permute-done | bytes 69664 | tf_op jit(solution)/shard_map/ppermute | solution.py:718
  114.4 1.6 %collective-permute-done.17 = bf16[272,128]{1,0:T(8,128)(2,1)S(1)} collective-permute-done((bf16[272,128]{1,0:T(8,128)(2,1)S(1)}, bf16[272,128]{1,0:T(8,128)(2,1)S(1)}, u32[]{:S(2)}, u32[]{:S(2)}) %collective-permute-start.17) | collective-permute-done | bytes 69664 | tf_op jit(solution)/shard_map/ppermute | solution.py:718
  116.8 1.5 %collective-permute-done.19 = bf16[4,272,128]{2,1,0:T(8,128)(2,1)S(1)} collective-permute-done((bf16[4,272,128]{2,1,0:T(8,128)(2,1)S(1)}, bf16[4,272,128]{2,1,0:T(8,128)(2,1)S(1)}, u32[]{:S(2)}, u32[]{:S(2)}) %collective-permute-start.19) | collective-permute-done | bytes 278560 | tf_op jit(solution)/shard_map/ppermute | solution.py:718
  118.4 0.7 copy-done.3
  119.1 2.7 %finish_sums.1 = (f32[192,576]{1,0:T(8,128)}, f32[192,192]{1,0:T(8,128)}, f32[6,144,144]{2,1,0:T(8,128)}, f32[1,192]{1,0:T(1,128)}) custom-call(bf16[1088,128]{1,0:T(8,128)(2,1)} %bitcast.49, bf16[1088,128]{1,0:T(8,128)(2,1)} %bitcast.51, s32[1,1]{1,0:T(1,128)} %bitcast.4.core.refs_2_, f32[1,192]{1,0:T(1,128)} %bitcast.58, bf16[192,576]{1,0:T(8,128)(2,1)} %refs_4_.1), custom_call_target="tpu_custom_call" | custom-call | tf_op jit(solution)/shard_map/finish_sums/pallas_call | solution.py:683
  (42 shorter events, 3.9 us)
Async XLA Ops:
  5.8 29.3 %collective-permute-start = (bf16[2,8,216,128]{3,2,1,0:T(8,128)(2,1)}, bf16[2,8,216,128]{3,2,1,0:T(8,128)(2,1)S(1)}, u32[]{:S(2)}, u32[]{:S(2)}) collective-permute-start(bf16[2,8,216,128]{3,2,1,0:T(8,128)(2,1)} %get-tuple-element.41), channel_id=1, source_target_pairs={{0,120},{8,0},{16,8},{24,16},{32,24},{40,32},{48,40},{56,48},{64,5... | collective-permute-start | bytes 2654216 | tf_op jit(solution)/shard_map/ppermute | solution.py:713
  9.3 25.9 %collective-permute-start.1 = (bf16[2,8,144,128]{3,2,1,0:T(8,128)(2,1)}, bf16[2,8,144,128]{3,2,1,0:T(8,128)(2,1)S(1)}, u32[]{:S(2)}, u32[]{:S(2)}) collective-permute-start(bf16[2,8,144,128]{3,2,1,0:T(8,128)(2,1)} %get-tuple-element.42), channel_id=1, source_target_pairs={{0,7},{1,0},{2,1},{3,2},{4,3},{5,4},{6,5},{7,6},{8,15},{9,8},{10,9... | collective-permute-start | bytes 1769480 | tf_op jit(solution)/shard_map/ppermute | solution.py:713
  15.5 19.1 %collective-permute-start.2 = (bf16[2,4,56,128]{3,2,1,0:T(8,128)(2,1)}, bf16[2,4,56,128]{3,2,1,0:T(8,128)(2,1)S(1)}, u32[]{:S(2)}, u32[]{:S(2)}) collective-permute-start(bf16[2,4,56,128]{3,2,1,0:T(8,128)(2,1)} %get-tuple-element.43), channel_id=1, source_target_pairs={{0,127},{1,120},{2,121},{3,122},{4,123},{5,124},{6,125},{7,126},{8... | collective-permute-start | bytes 344072 | tf_op jit(solution)/shard_map/ppermute | solution.py:713
  34.6 0.6 copy-start.7
  35.2 0.8 copy-start.6
  35.2 1.1 copy-start.5
  65.3 13.8 %collective-permute-start.4 = (bf16[8,216,128]{2,1,0:T(8,128)(2,1)}, bf16[8,216,128]{2,1,0:T(8,128)(2,1)S(1)}, u32[]{:S(2)}, u32[]{:S(2)}) collective-permute-start(bf16[8,216,128]{2,1,0:T(8,128)(2,1)} %get-tuple-element.52), channel_id=1, source_target_pairs={{0,8},{8,16},{16,24},{24,32},{32,40},{40,48},{48,56},{56,64},{64,7... | collective-permute-start | bytes 1327112 | tf_op jit(solution)/shard_map/ppermute | solution.py:713
  65.6 13.5 %collective-permute-start.3 = (bf16[8,144,128]{2,1,0:T(8,128)(2,1)}, bf16[8,144,128]{2,1,0:T(8,128)(2,1)S(1)}, u32[]{:S(2)}, u32[]{:S(2)}) collective-permute-start(bf16[8,144,128]{2,1,0:T(8,128)(2,1)} %get-tuple-element.51), channel_id=1, source_target_pairs={{0,1},{1,2},{2,3},{3,4},{4,5},{5,6},{6,7},{7,0},{8,9},{9,10},{10,1... | collective-permute-start | bytes 884744 | tf_op jit(solution)/shard_map/ppermute | solution.py:713
  68.5 9.6 %collective-permute-start.5 = (bf16[4,56,128]{2,1,0:T(8,128)(2,1)}, bf16[4,56,128]{2,1,0:T(8,128)(2,1)S(1)}, u32[]{:S(2)}, u32[]{:S(2)}) collective-permute-start(bf16[4,56,128]{2,1,0:T(8,128)(2,1)} %get-tuple-element.53), channel_id=1, source_target_pairs={{0,9},{1,10},{2,11},{3,12},{4,13},{5,14},{6,15},{7,8},{8,17},{9,18... | collective-permute-start | bytes 172040 | tf_op jit(solution)/shard_map/ppermute | solution.py:713
  78.1 11.1 %copy-start.4 = (bf16[4,56,128]{2,1,0:T(8,128)(2,1)}, bf16[4,56,128]{2,1,0:T(8,128)(2,1)S(1)}, u32[]{:S(2)}) copy-start(bf16[4,56,128]{2,1,0:T(8,128)(2,1)S(1)} %collective-permute-done.5.gc) | copy-start | bytes 172036
  79.1 10.1 %copy-start.1 = (bf16[8,144,128]{2,1,0:T(8,128)(2,1)}, bf16[8,144,128]{2,1,0:T(8,128)(2,1)S(1)}, u32[]{:S(2)}) copy-start(bf16[8,144,128]{2,1,0:T(8,128)(2,1)S(1)} %collective-permute-done.3.gs) | copy-start | bytes 884740
  79.1 10.1 %copy-start = (bf16[8,216,128]{2,1,0:T(8,128)(2,1)}, bf16[8,216,128]{2,1,0:T(8,128)(2,1)S(1)}, u32[]{:S(2)}) copy-start(bf16[8,216,128]{2,1,0:T(8,128)(2,1)S(1)} %collective-permute-done.4.gl) | copy-start | bytes 1327108
  79.1 1.9 %collective-permute-start.6 = (bf16[1088,128]{1,0:T(8,128)(2,1)}, bf16[1088,128]{1,0:T(8,128)(2,1)S(1)}, u32[]{:S(2)}, u32[]{:S(2)}) collective-permute-start(bf16[1088,128]{1,0:T(8,128)(2,1)} %get-tuple-element.54), channel_id=1, source_target_pairs={{0,8},{8,0},{16,24},{24,16},{32,40},{40,32},{48,56},{56,48},{64,72... | collective-permute-start | bytes 835592 | tf_op jit(solution)/shard_map/ppermute | solution.py:718
  82.2 9.7 %collective-permute-start.7 = (bf16[272,128]{1,0:T(8,128)(2,1)S(1)}, bf16[272,128]{1,0:T(8,128)(2,1)S(1)}, u32[]{:S(2)}, u32[]{:S(2)}) collective-permute-start(bf16[272,128]{1,0:T(8,128)(2,1)S(1)} %get-tuple-element.73), channel_id=1, source_target_pairs={{0,16},{8,24},{16,0},{24,8},{32,48},{40,56},{48,32},{56,40},{64,80... | collective-permute-start | bytes 208904 | tf_op jit(solution)/shard_map/ppermute | solution.py:718
  82.8 9.2 %collective-permute-start.9 = (bf16[272,128]{1,0:T(8,128)(2,1)S(1)}, bf16[272,128]{1,0:T(8,128)(2,1)S(1)}, u32[]{:S(2)}, u32[]{:S(2)}) collective-permute-start(bf16[272,128]{1,0:T(8,128)(2,1)S(1)} %get-tuple-element.74), channel_id=1, source_target_pairs={{0,48},{8,56},{16,32},{24,40},{32,16},{40,24},{48,0},{56,8},{64,11... | collective-permute-start | bytes 208904 | tf_op jit(solution)/shard_map/ppermute | solution.py:718
  87.8 5.8 %collective-permute-start.8 = (bf16[272,128]{1,0:T(8,128)(2,1)S(1)}, bf16[272,128]{1,0:T(8,128)(2,1)S(1)}, u32[]{:S(2)}, u32[]{:S(2)}) collective-permute-start(bf16[272,128]{1,0:T(8,128)(2,1)S(1)} %get-tuple-element.75), channel_id=1, source_target_pairs={{0,32},{8,40},{16,48},{24,56},{32,0},{40,8},{48,16},{56,24},{64,96... | collective-permute-start | bytes 208904 | tf_op jit(solution)/shard_map/ppermute | solution.py:718
  93.7 6.9 %collective-permute-start.12 = (bf16[272,128]{1,0:T(8,128)(2,1)S(1)}, bf16[272,128]{1,0:T(8,128)(2,1)S(1)}, u32[]{:S(2)}, u32[]{:S(2)}) collective-permute-start(bf16[272,128]{1,0:T(8,128)(2,1)S(1)} %convert_element_type.48), channel_id=1, source_target_pairs={{0,6},{1,7},{2,4},{3,5},{4,2},{5,3},{6,0},{7,1},{8,14},{9,15},{10,... | collective-permute-start | bytes 208904 | tf_op jit(solution)/shard_map/ppermute | solution.py:718
  94.8 5.8 %collective-permute-start.11 = (bf16[272,128]{1,0:T(8,128)(2,1)S(1)}, bf16[272,128]{1,0:T(8,128)(2,1)S(1)}, u32[]{:S(2)}, u32[]{:S(2)}) collective-permute-start(bf16[272,128]{1,0:T(8,128)(2,1)S(1)} %convert_element_type.48), channel_id=1, source_target_pairs={{0,4},{1,5},{2,6},{3,7},{4,0},{5,1},{6,2},{7,3},{8,12},{9,13},{10,... | collective-permute-start | bytes 208904 | tf_op jit(solution)/shard_map/ppermute | solution.py:718
  94.8 6.1 %collective-permute-start.10 = (bf16[272,128]{1,0:T(8,128)(2,1)S(1)}, bf16[272,128]{1,0:T(8,128)(2,1)S(1)}, u32[]{:S(2)}, u32[]{:S(2)}) collective-permute-start(bf16[272,128]{1,0:T(8,128)(2,1)S(1)} %convert_element_type.48), channel_id=1, source_target_pairs={{0,2},{1,3},{2,0},{3,1},{4,6},{5,7},{6,4},{7,5},{8,10},{9,11},{10,... | collective-permute-start | bytes 208904 | tf_op jit(solution)/shard_map/ppermute | solution.py:718
  101.0 5.6 %collective-permute-start.15 = (bf16[272,128]{1,0:T(8,128)(2,1)S(1)}, bf16[272,128]{1,0:T(8,128)(2,1)S(1)}, u32[]{:S(2)}, u32[]{:S(2)}) collective-permute-start(bf16[272,128]{1,0:T(8,128)(2,1)S(1)} %convert_element_type.52), channel_id=1, source_target_pairs={{0,65},{1,64},{2,67},{3,66},{4,69},{5,68},{6,71},{7,70},{8,73},{9,... | collective-permute-start | bytes 208904 | tf_op jit(solution)/shard_map/ppermute | solution.py:767
  102.1 4.4 %collective-permute-start.14 = (bf16[272,128]{1,0:T(8,128)(2,1)S(1)}, bf16[272,128]{1,0:T(8,128)(2,1)S(1)}, u32[]{:S(2)}, u32[]{:S(2)}) collective-permute-start(bf16[272,128]{1,0:T(8,128)(2,1)S(1)} %convert_element_type.52), channel_id=1, source_target_pairs={{0,64},{8,72},{16,80},{24,88},{32,96},{40,104},{48,112},{56,120},{... | collective-permute-start | bytes 208904 | tf_op jit(solution)/shard_map/ppermute | solution.py:718
  102.7 6.1 %collective-permute-start.13 = (bf16[272,128]{1,0:T(8,128)(2,1)S(1)}, bf16[272,128]{1,0:T(8,128)(2,1)S(1)}, u32[]{:S(2)}, u32[]{:S(2)}) collective-permute-start(bf16[272,128]{1,0:T(8,128)(2,1)S(1)} %convert_element_type.52), channel_id=1, source_target_pairs={{0,1},{1,0},{2,3},{3,2},{4,5},{5,4},{6,7},{7,6},{8,9},{9,8},{10,11... | collective-permute-start | bytes 208904 | tf_op jit(solution)/shard_map/ppermute | solution.py:718
  108.8 5.6 %collective-permute-start.18 = (bf16[272,128]{1,0:T(8,128)(2,1)S(1)}, bf16[272,128]{1,0:T(8,128)(2,1)S(1)}, u32[]{:S(2)}, u32[]{:S(2)}) collective-permute-start(bf16[272,128]{1,0:T(8,128)(2,1)S(1)} %add_convert_fusion), channel_id=1, source_target_pairs={{0,48},{8,56},{16,32},{24,40},{32,16},{40,24},{48,0},{56,8},{64,11... | collective-permute-start | bytes 208904 | tf_op jit(solution)/shard_map/ppermute | solution.py:718
  110.2 5.8 %collective-permute-start.17 = (bf16[272,128]{1,0:T(8,128)(2,1)S(1)}, bf16[272,128]{1,0:T(8,128)(2,1)S(1)}, u32[]{:S(2)}, u32[]{:S(2)}) collective-permute-start(bf16[272,128]{1,0:T(8,128)(2,1)S(1)} %add_convert_fusion), channel_id=1, source_target_pairs={{0,32},{8,40},{16,48},{24,56},{32,0},{40,8},{48,16},{56,24},{64,96... | collective-permute-start | bytes 208904 | tf_op jit(solution)/shard_map/ppermute | solution.py:718
  112.3 4.3 %collective-permute-start.16 = (bf16[272,128]{1,0:T(8,128)(2,1)S(1)}, bf16[272,128]{1,0:T(8,128)(2,1)S(1)}, u32[]{:S(2)}, u32[]{:S(2)}) collective-permute-start(bf16[272,128]{1,0:T(8,128)(2,1)S(1)} %add_convert_fusion), channel_id=1, source_target_pairs={{0,16},{8,24},{16,0},{24,8},{32,48},{40,56},{48,32},{56,40},{64,80... | collective-permute-start | bytes 208904 | tf_op jit(solution)/shard_map/ppermute | solution.py:718
  116.7 1.7 %copy-start.2 = (bf16[4,272,128]{2,1,0:T(8,128)(2,1)}, bf16[4,272,128]{2,1,0:T(8,128)(2,1)S(1)}, u32[]{:S(2)}) copy-start(bf16[4,272,128]{2,1,0:T(8,128)(2,1)S(1)} %pad_maximum_fusion.1) | copy-start | bytes 835588
  116.8 1.6 %collective-permute-start.19 = (bf16[4,272,128]{2,1,0:T(8,128)(2,1)S(1)}, bf16[4,272,128]{2,1,0:T(8,128)(2,1)S(1)}, u32[]{:S(2)}, u32[]{:S(2)}) collective-permute-start(bf16[4,272,128]{2,1,0:T(8,128)(2,1)S(1)} %pad_maximum_fusion.1), channel_id=1, source_target_pairs={{0,8},{8,0},{16,24},{24,16},{32,40},{40,32},{48,56},{56,48},{64,72... | collective-permute-start | bytes 835592 | tf_op jit(solution)/shard_map/ppermute | solution.py:718
  118.4 0.7 copy-start.3

commit v6 on v5

--- a/solution.py
+++ b/solution.py
@@ -150,7 +150,6 @@
 
 
 STAGGER = 2
-EARLY = 3
 
 
 def run_windows(windows, gw_ref):
@@ -260,7 +259,7 @@
     give(1)
 
 
-def early_kernel(
+def inner_kernel(
     x0, x1, x2, x3, y0, y1, y2, y3, gain, weight, out_weight, pair, last, dx_ref, gw_ref, gb_ref, bias_ref, wqkv, wqkv_t, wout_t, *scratch
 ):
     @pl.when(pl.program_id(0) == 0)
@@ -280,17 +279,7 @@
     inner_steps((x0, x1, x2, x3), (y0, y1, y2, y3), consts, bias_ref, dx_ref, gw_ref, gb_ref, scratch)
 
 
-def late_kernel(
-    x0, x1, x2, x3, y0, y1, y2, y3, gain, wqkv, wqkv_t, wout_t, bias, gw_in, gb_in, core, _, dx_ref, give_ref, mine_ref, gw_ref, gb_ref, sum_ref, *scratch
-):
-    @pl.when(pl.program_id(0) == 0)
-    def _():
-        gw_ref[...] = gw_in[...]
-        gb_ref[...] = gb_in[...]
-
-    consts = (gain, wqkv, wqkv_t, wout_t)
-    inner_steps((x0, x1, x2, x3), (y0, y1, y2, y3), consts, bias, dx_ref, gw_ref, gb_ref, scratch)
-
+def write_halves(core, give_ref, mine_ref, gw_ref, gb_ref, sum_ref):
     @pl.when(pl.program_id(0) == pl.num_programs(0) - 1)
     def _():
         whole = jnp.concatenate([gw_ref[n] for n in range(4)], axis=1)
@@ -342,34 +331,29 @@
 
 
 def pack_kernel(x, y, e_ref, s_ref, c_ref, low, high):
+    pad = jnp.zeros((2, D), F32)
     for n, own in enumerate((x, y)):
+        corners = []
         for lv in range(2):
-            base = 128 * (2 * n + lv)
+            base = 288 * (2 * n + lv)
             east = jnp.concatenate([own[lv, lon].astype(F32) for lon in range(6)], axis=0)
             e_ref[n, lv] = dense(east[:, :128], east[:, 128:])
             for lon in range(36):
-                if lon < 6:
-                    at = pl.ds(base + 96 + lon, 3, stride=8)
-                else:
-                    at = pl.ds(base + lon - 6, 3, stride=32)
-                left, right = split(own[lv, lon].astype(F32)[:8])
-                low[at, :] = left[:3]
-                high[at, :] = right[:3]
-            s_ref[n, lv] = dense(low[base : base + 96, :], high[base : base + 96, :][:, :64])
-        c_ref[n, 0] = dense_corner(
-            jnp.concatenate(
-                [
-                    joined(low, high, pl.ds(128 * (2 * n + lv) + 96 + 8 * t, 8))[:6]
-                    for lv in range(2)
-                    for t in range(3)
-                ],
-                axis=0,
-            )
-        )
-
-
-def edge_kernel(
-    x, y, e, s, c, gain, wqkv, wqkv_t, wout_t, bias, gw_in, gb_in, oe_ref, os_ref, be_ref, bs_ref, bc_ref, gw_ref, gb_ref, *scratch
+                rows = own[lv, lon].astype(F32)[:8]
+                at = slice(base + 8 * lon, base + 8 * lon + 8)
+                low[at, :] = rows[:, :128]
+                high[at, :64] = rows[:, 128:]
+            parts = []
+            for t in range(3):
+                parts += [joined(low, high, pl.ds(base + 48 + t, 30, stride=8)), pad]
+                corners.append(joined(low, high, pl.ds(base + t, 6, stride=8)))
+            rows = jnp.concatenate(parts, axis=0)
+            s_ref[n, lv] = dense(rows[:, :128], rows[:, 128:])
+        c_ref[n, 0] = dense_corner(jnp.concatenate(corners, axis=0))
+
+
+def south_kernel(
+    x, y, e, s, c, gain, wqkv, wqkv_t, wout_t, bias, gw_in, gb_in, os_ref, tail_ref, bs_ref, bc_ref, gw_ref, gb_ref, *scratch
 ):
     @pl.when(pl.program_id(0) == 0)
     def _():
@@ -377,69 +361,108 @@
         gb_ref[...] = gb_in[...]
 
     def place(lv, lon):
-        if lon < 12:
-            return 32 * (12 * lv + lon)
-        return 768 + 16 * (24 * ((lon - 12) // 12) + 12 * lv + lon % 12)
+        return 1152 * (lv // 2) + 16 * (24 * (lon // 12) + 12 * (lv % 2) + lon % 12)
 
     def south(lv, t):
         return [
-            pl.ds(place(lv, 12) + 8 + t, 12, stride=16),
-            pl.ds(place(lv, 24) + 8 + t, 12, stride=16),
-            pl.ds(place(lv, 0) + 24 + t, 6, stride=32),
+            pl.ds(place(lv, 12 * m) + 8 + t, 12 if m < 2 else 6, stride=16) for m in range(3)
         ]
 
     def corner(lv, t):
-        return pl.ds(place(lv, 6) + 24 + t, 6, stride=32)
+        return pl.ds(place(lv, 30) + 8 + t, 6, stride=16)
 
     for n, own in enumerate((x, y)):
         low, high = scratch[2 * n], scratch[2 * n + 1]
-        cleft, cright = undense_corner(c[n, 0])
-        for lv in range(2):
-            for lon in range(6):
-                keep(low, high, place(lv, lon), own[lv, 30 + lon])
-            for lon in range(24):
-                keep(low, high, place(lv, 12 + lon), own[lv, 6 + lon].astype(F32)[16:])
+        for lv in range(4):
+            if lv % 2 == 0:
+                cleft, cright = undense_corner(c[n, lv // 2])
+            for lon in range(30):
+                keep(low, high, place(lv, lon), own[lv, 6 + lon].astype(F32)[16:])
             left, right = undense(e[n, lv])
             for lon in range(6):
-                at = place(lv, 6 + lon)
-                low[at : at + 24, :] = left[24 * lon : 24 * lon + 24]
-                high[at : at + 24, :] = right[24 * lon : 24 * lon + 24]
+                at = place(lv, 30 + lon)
+                low[at : at + 8, :] = left[24 * lon + 16 : 24 * lon + 24]
+                high[at : at + 8, :] = right[24 * lon + 16 : 24 * lon + 24]
             left, right = undense(s[n, lv])
             for t in range(3):
                 for m, at in enumerate(south(lv, t)):
                     rows = slice(32 * t + 12 * m, 32 * t + min(12 * m + 12, 30))
                     low[at, :] = left[rows]
                     high[at, :] = right[rows]
-                rows = slice(18 * lv + 6 * t, 18 * lv + 6 * t + 6)
+                rows = slice(18 * (lv % 2) + 6 * t, 18 * (lv % 2) + 6 * t + 6)
                 low[corner(lv, t), :] = cleft[rows]
                 high[corner(lv, t), :] = cright[rows]
-    refs = dict(
-        gain=gain, wqkv=wqkv, wqkv_t=wqkv_t, wout_t=wout_t, bias=bias, gb=gb_ref
-    )
+    refs = dict(gain=gain, wqkv=wqkv, wqkv_t=wqkv_t, wout_t=wout_t, bias=bias, gb=gb_ref)
     run_windows(
-        [window_of(scratch, 3 + 6 * a, 32, int(a == 3), refs) for a in range(4)]
-        + [window_of(scratch, 768 + 384 * k + 5, 16, 1, refs) for k in range(2)],
+        [
+            window_of(scratch, 1152 * p + 384 * k + 5, 16, 1, refs)
+            for p in range(2)
+            for k in range(3)
+        ],
         gw_ref,
     )
     low, high = scratch[4], scratch[5]
     pad = jnp.zeros((2, D), F32)
     corners = []
-    for lv in range(2):
+    for lv in range(4):
+        for lon in range(30):
+            os_ref[lv, lon] = kept(low, high, place(lv, lon), 8)
         for lon in range(6):
-            oe_ref[lv, lon] = kept(low, high, place(lv, lon), 24)
-        east = jnp.concatenate(
-            [joined(low, high, pl.ds(place(lv, 6 + lon), 24)) for lon in range(6)], axis=0
-        )
-        be_ref[lv] = dense(east[:, :128], east[:, 128:])
-        for lon in range(24):
-            os_ref[lv, lon] = kept(low, high, place(lv, 12 + lon), 8)
+            tail_ref[lv, lon] = kept(low, high, place(lv, 30 + lon), 8)
         parts = []
         for t in range(3):
             parts += [joined(low, high, at) for at in south(lv, t)] + [pad]
             corners.append(joined(low, high, corner(lv, t)))
         rows = jnp.concatenate(parts, axis=0)
         bs_ref[lv] = dense(rows[:, :128], rows[:, 128:])
-    bc_ref[0] = dense_corner(jnp.concatenate(corners, axis=0))
+    for p in range(2):
+        bc_ref[p] = dense_corner(jnp.concatenate(corners[6 * p : 6 * p + 6], axis=0))
+
+
+def east_kernel(
+    x, y, e, tail, gain, wqkv, wqkv_t, wout_t, bias, gw_in, gb_in, core, oe_ref, be_ref, give_ref, mine_ref, gw_ref, gb_ref, sum_ref, *scratch
+):
+    @pl.when(pl.program_id(0) == 0)
+    def _():
+        gw_ref[...] = gw_in[...]
+        gb_ref[...] = gb_in[...]
+
+    def place(lv, lon):
+        return 576 * (lv // 2) + 24 * (12 * (lv % 2) + lon)
+
+    for n, own in enumerate((x, y)):
+        low, high = scratch[2 * n], scratch[2 * n + 1]
+        for lv in range(4):
+            left, right = undense(e[n, lv])
+            for lon in range(6):
+                keep(low, high, place(lv, lon), own[lv, lon])
+                at = place(lv, 6 + lon)
+                low[at : at + 24, :] = left[24 * lon : 24 * lon + 24]
+                high[at : at + 24, :] = right[24 * lon : 24 * lon + 24]
+    refs = dict(gain=gain, wqkv=wqkv, wqkv_t=wqkv_t, wout_t=wout_t, bias=bias, gb=gb_ref)
+    run_windows(
+        [
+            window_of(scratch, 576 * p + 3 + 6 * a, 24, 0, refs)
+            for p in range(2)
+            for a in range(3)
+        ],
+        gw_ref,
+    )
+    low, high = scratch[4], scratch[5]
+    row = lax.broadcasted_iota(jnp.int32, (8, D), 0)
+    for lv in range(4):
+        east = []
+        for lon in range(6):
+            oe_ref[lv, lon] = kept(low, high, place(lv, lon), 24)
+            at = place(lv, 6 + lon)
+            last = joined(low, high, pl.ds(at + 16, 8))
+            east += [
+                joined(low, high, pl.ds(at, 16)),
+                jnp.where(row >= 5, tail[lv, lon].astype(F32), last),
+            ]
+        east = jnp.concatenate(east, axis=0)
+        be_ref[lv] = dense(east[:, :128], east[:, 128:])
+    write_halves(core, give_ref, mine_ref, gw_ref, gb_ref, sum_ref)
 
 
 def whole(shape):
@@ -466,18 +489,19 @@
     return [pltpu.VMEM((rows, 128), F32) for _ in range(6)]
 
 
-def inner_specs(first):
+def inner_specs():
     def cols(n):
-        return pl.BlockSpec((2, 6, 24, D), lambda i: (i + first, n, 0, 0))
+        return pl.BlockSpec((2, 6, 24, D), lambda i: (i, n, 0, 0))
 
     four = [cols(n) for n in range(1, 5)]
-    return four + four, pl.BlockSpec((2, 24, 24, D), lambda i: (i + first, 0, 0, 0))
-
-
-def early_windows(x, y, weights, pair_bias, last, steps):
-    ins, out = inner_specs(0)
+    return four + four, pl.BlockSpec((2, 24, 24, D), lambda i: (i, 0, 0, 0))
+
+
+def inner_windows(x, y, weights, pair_bias, last):
+    steps = x.shape[0] // 2
+    ins, out = inner_specs()
     return pl.pallas_call(
-        early_kernel,
+        inner_kernel,
         grid=(steps,),
         in_specs=ins
         + [whole((1, D)), whole((D, 3 * D)), whole((D, D)), whole((HEADS, W, W)), whole((1, 1))],
@@ -494,32 +518,8 @@
         scratch_shapes=halves(1152),
         compiler_params=PARAMS,
         cost_estimate=cost(6 * steps),
-        name="early_windows",
+        name="inner_windows",
     )(x, x, x, x, y, y, y, y, *weights, pair_bias, last)
-
-
-def late_windows(x, y, consts, bias, sums, core, inner, first):
-    steps = x.shape[0] // 2 - first
-    ins, out = inner_specs(first)
-    return pl.pallas_call(
-        late_kernel,
-        grid=(steps,),
-        in_specs=ins
-        + const_specs()
-        + [whole(BIAS), whole(GW), whole(GB), whole((1, 1)), pl.BlockSpec(memory_space=pl.ANY)],
-        out_specs=[out, whole((ROWS // 2, 128)), whole((ROWS // 2, 128))],
-        out_shape=[
-            jax.ShapeDtypeStruct(inner.shape, BF16),
-            jax.ShapeDtypeStruct((ROWS // 2, 128), BF16),
-            jax.ShapeDtypeStruct((ROWS // 2, 128), F32),
-        ],
-        scratch_shapes=[pltpu.VMEM(GW, F32), pltpu.VMEM(GB, F32), pltpu.VMEM((ROWS, 128), F32)]
-        + halves(1152),
-        input_output_aliases={16: 0},
-        compiler_params=PARAMS,
-        cost_estimate=cost(6 * steps),
-        name="late_windows",
-    )(x, x, x, x, y, y, y, y, *consts, bias, *sums, core, inner)
 
 
 def both(*rest):
@@ -552,43 +552,89 @@
             jax.ShapeDtypeStruct((2, levels, 144, 128), BF16),
             jax.ShapeDtypeStruct((2, levels // 2, 56, 128), BF16),
         ],
-        scratch_shapes=[pltpu.VMEM((512, 128), F32), pltpu.VMEM((512, 128), F32)],
+        scratch_shapes=[pltpu.VMEM((1152, 128), F32), pltpu.VMEM((1152, 128), F32)],
         compiler_params=PARAMS,
         name="pack_halo",
     )(x, y)
 
 
-def edge_windows(x, y, e, s, c, consts, bias, sums):
+def four(*rest, at=0):
+    zeros = (0,) * (len(rest) - 1)
+    return pl.BlockSpec((4,) + rest, lambda i: (i, at) + zeros)
+
+
+def both_four(count, *rest):
+    return pl.BlockSpec((2, count) + rest, lambda i: (0, i, 0, 0))
+
+
+def south_windows(x, y, e, s, c, consts, bias, sums):
     levels = x.shape[0]
     return pl.pallas_call(
-        edge_kernel,
-        grid=(levels // 2,),
-        in_specs=[one(36, 24, D), one(36, 24, D), both(216, 128), both(144, 128), both_corner()]
+        south_kernel,
+        grid=(levels // 4,),
+        in_specs=[
+            four(36, 24, D),
+            four(36, 24, D),
+            both_four(4, 216, 128),
+            both_four(4, 144, 128),
+            both_four(2, 56, 128),
+        ]
         + const_specs()
         + [whole(BIAS), whole(GW), whole(GB)],
         out_specs=[
-            one(6, 24, D),
-            one(24, 8, D),
-            one(216, 128),
-            one(144, 128),
-            one_corner(),
+            four(30, 8, D),
+            four(6, 8, D),
+            four(144, 128),
+            pl.BlockSpec((2, 56, 128), lambda i: (i, 0, 0)),
             whole(GW),
             whole(GB),
         ],
         out_shape=[
-            jax.ShapeDtypeStruct((levels, 6, 24, D), BF16),
-            jax.ShapeDtypeStruct((levels, 24, 8, D), BF16),
-            jax.ShapeDtypeStruct((levels, 216, 128), BF16),
+            jax.ShapeDtypeStruct((levels, 30, 8, D), BF16),
+            jax.ShapeDtypeStruct((levels, 6, 8, D), BF16),
             jax.ShapeDtypeStruct((levels, 144, 128), BF16),
             jax.ShapeDtypeStruct((levels // 2, 56, 128), BF16),
             jax.ShapeDtypeStruct(GW, F32),
             jax.ShapeDtypeStruct(GB, F32),
         ],
-        scratch_shapes=halves(1536),
+        scratch_shapes=halves(2304),
         compiler_params=PARAMS,
-        cost_estimate=cost(24),
-        name="edge_windows",
+        cost_estimate=cost(12),
+        name="south_windows",
     )(x, y, e, s, c, *consts, bias, *sums)
+
+
+def east_windows(x, y, e, tail, consts, bias, sums, core):
+    levels = x.shape[0]
+    return pl.pallas_call(
+        east_kernel,
+        grid=(levels // 4,),
+        in_specs=[
+            four(6, 24, D, at=5),
+            four(6, 24, D, at=5),
+            both_four(4, 216, 128),
+            four(6, 8, D),
+        ]
+        + const_specs()
+        + [whole(BIAS), whole(GW), whole(GB), whole((1, 1))],
+        out_specs=[
+            four(6, 24, D),
+            four(216, 128),
+            whole((ROWS // 2, 128)),
+            whole((ROWS // 2, 128)),
+        ],
+        out_shape=[
+            jax.ShapeDtypeStruct((levels, 6, 24, D), BF16),
+            jax.ShapeDtypeStruct((levels, 216, 128), BF16),
+            jax.ShapeDtypeStruct((ROWS // 2, 128), BF16),
+            jax.ShapeDtypeStruct((ROWS // 2, 128), F32),
+        ],
+        scratch_shapes=[pltpu.VMEM(GW, F32), pltpu.VMEM(GB, F32), pltpu.VMEM((ROWS, 128), F32)]
+        + halves(1152),
+        compiler_params=PARAMS,
+        cost_estimate=cost(12),
+        name="east_windows",
+    )(x, y, e, tail, *consts, bias, *sums, core)
 
 
 def assemble_kernel(inner, oe, os_, gl, gs, gc, *rest):
@@ -611,12 +657,10 @@
             if lon < 6:
                 at = slice(24 * lon, 24 * lon + 24)
                 rows = jnp.concatenate([left[at], right[at, :64]], axis=1)
-            elif lon < 30:
-                rows = inner[lv, lon - 6].astype(F32)
+            else:
+                rows = (inner[lv, lon - 6] if lon < 30 else oe[lv, lon - 30]).astype(F32)
                 tail = os_[lv, lon - 6].astype(F32)
                 rows = jnp.concatenate([rows[:16], jnp.where(row >= 5, tail, rows[16:])], axis=0)
-            else:
-                rows = oe[lv, lon - 30].astype(F32)
             head = jnp.where(row < 3, joined(low, high, pl.ds(base + 8 * lon, 8)), rows[:8])
             out_ref[lv, lon] = jnp.concatenate([head, rows[8:]], axis=0).astype(BF16)
 
@@ -630,7 +674,7 @@
     specs = [
         at(2, 24, 24, D),
         at(2, 6, 24, D),
-        at(2, 24, 8, D),
+        at(2, 30, 8, D),
         at(2, 216, 128),
         at(2, 144, 128),
         at(1, 56, 128),
@@ -726,7 +770,7 @@
     return n % 2
 
 
-def sum_over_devices(give, mine, beside):
+def sum_over_devices(give, mine, back, beside):
     y = (lax.axis_index("lon") // 2) % 4
     mine = mine + flip(give, "lon", 1).astype(F32)
     quarters = mine.reshape(4, ROWS // 8, 128)
@@ -735,11 +779,11 @@
     for step in range(1, 4):
         piece = lax.dynamic_index_in_dim(qlow, y ^ step, 0, keepdims=False)
         total = total + flip(piece, "lon", 2 * step).astype(F32)
-    total, grad_x = lax.optimization_barrier((total, beside(0, None)))
     low = total.astype(BF16)
     for step in range(1, 4):
         total = total + flip(low, "lat", 2 * step).astype(F32)
-    total, grad_x = lax.optimization_barrier((total, beside(1, grad_x)))
+    total, got_lon = lax.optimization_barrier((total, back[0]))
+    back = (got_lon, *back[1:])
     low = total.astype(BF16)
     total = (
         total
@@ -747,12 +791,14 @@
         + flip(low, "lon", 8).astype(F32)
         + shift_x(low).astype(F32)
     )
+    total, grad_x = lax.optimization_barrier((total, beside(0, None, back)))
     low = total.astype(BF16)
     others = [low] + [flip(low, "lon", 2 * step) for step in range(1, 4)]
     stacked = jnp.stack(others)
     line = jnp.concatenate(
         [lax.dynamic_index_in_dim(stacked, y ^ n, 0, keepdims=True) for n in range(4)], axis=0
     )
+    line, grad_x = lax.optimization_barrier((line, beside(1, grad_x, back)))
     other = flip(line, "lon", 1)
     return line.reshape(ROWS // 2, 128), other.reshape(ROWS // 2, 128), grad_x
 
@@ -778,22 +824,23 @@
     gain = ln_gain.reshape(1, D)
     core = (lax.axis_index("lon") % 2).astype(jnp.int32).reshape(1, 1)
     last = (lax.axis_index("lat") == lax.axis_size("lat") - 1).astype(jnp.int32).reshape(1, 1)
-    inner, gw, gb, bias, *laid = early_windows(
-        x, y, (gain, qkv_weight, out_weight), pair_bias, last, EARLY
+    inner, gw, gb, bias, *laid = inner_windows(
+        x, y, (gain, qkv_weight, out_weight), pair_bias, last
     )
     consts = [gain] + laid
-    oe, os_, be, bs, bc, gw, gb = edge_windows(x, y, e, s, c, consts, bias, (gw, gb))
+    os_, tail, bs, bc, gw, gb = south_windows(x, y, e, s, c, consts, bias, (gw, gb))
     got_lat = shift(bs, ("lat",), (1,))
+    got_both = shift(bc, ("lon", "lat"), (1, 1))
+    oe, be, give, mine = east_windows(x, y, e, tail, consts, bias, (gw, gb), core)
     got_lon = shift(be, ("lon",), (1,))
-    got_both = shift(bc, ("lon", "lat"), (1, 1))
-    inner, give, mine = late_windows(x, y, consts, bias, (gw, gb), core, inner, EARLY)
-    give, got_lat, got_lon, got_both = lax.optimization_barrier((give, got_lat, got_lon, got_both))
+    give, got_lat, got_both = lax.optimization_barrier((give, got_lat, got_both))
+    back = (got_lon, got_lat, got_both)
     half = levels // 4
 
-    def beside(part, grad_x):
-        return assemble(half * part, half, grad_x, inner, oe, os_, got_lon, got_lat, got_both)
-
-    *sums, grad_x = sum_over_devices(give, mine, beside)
+    def beside(part, grad_x, got):
+        return assemble(half * part, half, grad_x, inner, oe, os_, *got)
+
+    *sums, grad_x = sum_over_devices(give, mine, back, beside)
     factor = float(
         levels * lat_count * lax.axis_size("lat") * lon_count * lax.axis_size("lon")
     ) ** (-0.5)

time: 123 us -> 118 us (0.959)
  starting transfers between devices: 33.9 us -> 30.7 us
  Pallas kernels: 69.6 us -> 67.8 us
    ppermute x13, starting transfers between devices: 19.6 us -> 14.8 us  [moved(): return lax.ppermute(value, axis, [(n, to_of(n)) for n in range(count)])]
    ppermute x13, waiting for transfers between devices: 10.8 us -> 14.3 us  [moved(): return lax.ppermute(value, axis, [(n, to_of(n)) for n in range(count)])]
    ppermute x6, waiting for transfers between devices: 2.69 us -> 0.02 us  [shift(): return lax.ppermute(value, axes if len(axes) > 1 else axes[0], pairs)]
    pallas_call x3, Pallas kernels: 56.3 us -> 54.6 us  [the longest x1 23.8 us: inner_windows(): pl.pallas_call(inner_kernel, grid=(steps,), in_specs=ins + [whole((1, D))...]
    ppermute x1, starting transfers between devices: 1.16 us -> 2.64 us  [shift_x(): return lax.ppermute(value, ('lon', 'lat'), pairs)]
  transfers between devices with their start and end apart: 20 -> 20, of which waited for: 12 -> 10; matrix products, arithmetic and copies ran while one was open for 0% -> 0% of each run, Pallas kernels for 27% -> 37%
where the time goes in v6:
time: 118 us; the launch traced here: 117 us
  Pallas kernels  67.8 us (57%)
  starting transfers between devices  30.7 us (26%)
  waiting for transfers between devices  14.3 us (12%)
  local copies, waits for them, and re-layouts  1.89 us (2%)
  other arithmetic  1.38 us (1%)
    pallas_call x1, Pallas kernels, inner_windows(): pl.pallas_call(inner_kernel, grid=(steps,), in_specs=ins + [whole((1, D))...  23.8 us
    pallas_call x1, Pallas kernels, south_windows(): pl.pallas_call(south_kernel, grid=(levels // 4,), in_specs=[four(36, 24,...  16.5 us
    ppermute x13, starting transfers between devices, moved(): return lax.ppermute(value, axis, [(n, to_of(n)) for n in range(count)])  14.8 us
    ppermute x13, waiting for transfers between devices, moved(): return lax.ppermute(value, axis, [(n, to_of(n)) for n in range(count)])  14.3 us
    pallas_call x1, Pallas kernels, east_windows(): pl.pallas_call(east_kernel, grid=(levels // 4,), in_specs=[four(6, 24, D,...  14.3 us
    ppermute x6, starting transfers between devices, shift(): return lax.ppermute(value, axes if len(axes) > 1 else axes[0], pairs)  13.3 us
    pallas_call x2, Pallas kernels, assemble(): pl.pallas_call(assemble_kernel, grid=(steps,), in_specs=specs, out_specs=...  5.53 us
    pallas_call x1, Pallas kernels, pack_halo(): pl.pallas_call(pack_kernel, grid=(levels // 2,), in_specs=[one(36, 24, D)...  4.96 us
  transfers between devices with their start and end apart: 20, of which 10 were waited for; matrix products, arithmetic and copies ran while one was open for 0% of the time, Pallas kernels for 37%

profile of v6, /device:TPU:0, one launch (start us, length us, event | category | flops | bytes accessed | tf_op | source)
XLA Modules:
  0.0 117.0 jit_solution(1687862514850599791)
XLA Ops:
  0.6 5.0 %pack_halo.1 = (bf16[2,8,216,128]{3,2,1,0:T(8,128)(2,1)}, bf16[2,8,144,128]{3,2,1,0:T(8,128)(2,1)}, bf16[2,4,56,128]{3,2,1,0:T(8,128)(2,1)}) custom-call(bf16[8,36,24,192]{3,2,1,0:T(8,128)(2,1)} %bitcast.30, bf16[8,36,24,192]{3,2,1,0:T(8,128)(2,1)} %bitcast.37), custom_call_target="tpu_custom_call" | custom-call | tf_op jit(solution)/shard_map/pack_halo/pallas_call | solution.py:545
  5.6 3.5 %collective-permute-start = (bf16[2,8,216,128]{3,2,1,0:T(8,128)(2,1)}, bf16[2,8,216,128]{3,2,1,0:T(8,128)(2,1)S(1)}, u32[]{:S(2)}, u32[]{:S(2)}) collective-permute-start(bf16[2,8,216,128]{3,2,1,0:T(8,128)(2,1)} %get-tuple-element.38), channel_id=1, source_target_pairs={{0,120},{8,0},{16,8},{24,16},{32,24},{40,32},{48,40},{56,48},{64,5... | collective-permute-start | bytes 2654216 | tf_op jit(solution)/shard_map/ppermute | solution.py:757
  9.1 6.2 %collective-permute-start.1 = (bf16[2,8,144,128]{3,2,1,0:T(8,128)(2,1)}, bf16[2,8,144,128]{3,2,1,0:T(8,128)(2,1)S(1)}, u32[]{:S(2)}, u32[]{:S(2)}) collective-permute-start(bf16[2,8,144,128]{3,2,1,0:T(8,128)(2,1)} %get-tuple-element.39), channel_id=1, source_target_pairs={{0,7},{1,0},{2,1},{3,2},{4,3},{5,4},{6,5},{7,6},{8,15},{9,8},{10,9... | collective-permute-start | bytes 1769480 | tf_op jit(solution)/shard_map/ppermute | solution.py:757
  15.3 0.3 collective-permute-start.2
  15.6 23.8 %inner_windows.1 = (bf16[8,24,24,192]{3,2,1,0:T(8,128)(2,1)}, f32[4,192,192]{2,1,0:T(8,128)}, f32[144,896]{1,0:T(8,128)}, f32[2,144,896]{2,1,0:T(8,128)}, bf16[1...) custom-call(bf16[8,36,24,192]{3,2,1,0:T(8,128)(2,1)} %bitcast.31, ...), custom_call_target="tpu_custom_call" | custom-call | flops 5096079360 | bytes 3981312 | tf_op jit(solution)/shard_map/inner_windows/pallas_call | solution.py:503
  39.5 0.6 copy-done.7
  40.6 16.5 %south_windows.1 = (bf16[8,30,8,192]{3,2,1,0:T(8,128)(2,1)}, bf16[8,6,8,192]{3,2,1,0:T(8,128)(2,1)}, bf16[8,144,128]{2,1,0:T(8,128)(2,1)}, bf16[4,56,128]{2,1,0:...) custom-call(bf16[8,36,24,192]{3,2,1,0:T(8,128)(2,1)} %bitcast.35, bf16[8,36,24,192]{3,2,1,0:T(8,128)(2,1)} %bitcast.42, ...), custom_call_target="tpu_custom_call" | custom-call | flops 2548039680 | bytes 1990656 | tf_op jit(solution)/shard_map/south_windows/pallas_call | solution.py:572
  57.1 1.8 %collective-permute-start.3 = (bf16[8,144,128]{2,1,0:T(8,128)(2,1)}, bf16[8,144,128]{2,1,0:T(8,128)(2,1)S(1)}, u32[]{:S(2)}, u32[]{:S(2)}) collective-permute-start(bf16[8,144,128]{2,1,0:T(8,128)(2,1)} %get-tuple-element.52), channel_id=1, source_target_pairs={{0,1},{1,2},{2,3},{3,4},{4,5},{5,6},{6,7},{7,0},{8,9},{9,10},{10,1... | collective-permute-start | bytes 884744 | tf_op jit(solution)/shard_map/ppermute | solution.py:757
  58.8 1.5 %collective-permute-start.4 = (bf16[4,56,128]{2,1,0:T(8,128)(2,1)}, bf16[4,56,128]{2,1,0:T(8,128)(2,1)S(1)}, u32[]{:S(2)}, u32[]{:S(2)}) collective-permute-start(bf16[4,56,128]{2,1,0:T(8,128)(2,1)} %get-tuple-element.53), channel_id=1, source_target_pairs={{0,9},{1,10},{2,11},{3,12},{4,13},{5,14},{6,15},{7,8},{8,17},{9,18... | collective-permute-start | bytes 172040 | tf_op jit(solution)/shard_map/ppermute | solution.py:757
  60.3 14.3 %east_windows.1 = (bf16[8,6,24,192]{3,2,1,0:T(8,128)(2,1)}, bf16[8,216,128]{2,1,0:T(8,128)(2,1)}, bf16[1088,128]{1,0:T(8,128)(2,1)}, f32[1088,128]{1,0:T(8,128)}) custom-call(bf16[8,36,24,192]{3,2,1,0:T(8,128)(2,1)} %bitcast.36, bf16[8,36,24,192]{3,2,1,0:T(8,128)(2,1)} %bitcast.43, bf16[2,8,216,128]{3,2,1,0:T(8,128)(2,1)} %copy-done, ...), custom_call_target="tpu_custom_call" | custom-call | flops 2548039680 | bytes 1990656 | tf_op jit(solution)/shard_map/east_windows/pallas_call | solution.py:609
  74.8 1.7 %collective-permute-done.5 = bf16[1088,128]{1,0:T(8,128)(2,1)S(1)} collective-permute-done((bf16[1088,128]{1,0:T(8,128)(2,1)}, bf16[1088,128]{1,0:T(8,128)(2,1)S(1)}, u32[]{:S(2)}, u32[]{:S(2)}) %collective-permute-start.5) | collective-permute-done | bytes 278560 | tf_op jit(solution)/shard_map/ppermute | solution.py:762
  76.5 1.1 convert_add_fusion
  77.8 1.7 %collective-permute-start.8 = (bf16[272,128]{1,0:T(8,128)(2,1)S(1)}, bf16[272,128]{1,0:T(8,128)(2,1)S(1)}, u32[]{:S(2)}, u32[]{:S(2)}) collective-permute-start(bf16[272,128]{1,0:T(8,128)(2,1)S(1)} %get-tuple-element.76), channel_id=1, source_target_pairs={{0,48},{8,56},{16,32},{24,40},{32,16},{40,24},{48,0},{56,8},{64,11... | collective-permute-start | bytes 208904 | tf_op jit(solution)/shard_map/ppermute | solution.py:762
  79.5 2.4 %collective-permute-start.7 = (bf16[272,128]{1,0:T(8,128)(2,1)S(1)}, bf16[272,128]{1,0:T(8,128)(2,1)S(1)}, u32[]{:S(2)}, u32[]{:S(2)}) collective-permute-start(bf16[272,128]{1,0:T(8,128)(2,1)S(1)} %get-tuple-element.77), channel_id=1, source_target_pairs={{0,32},{8,40},{16,48},{24,56},{32,0},{40,8},{48,16},{56,24},{64,96... | collective-permute-start | bytes 208904 | tf_op jit(solution)/shard_map/ppermute | solution.py:762
  82.1 1.3 %collective-permute-done.8 = bf16[272,128]{1,0:T(8,128)(2,1)S(1)} collective-permute-done((bf16[272,128]{1,0:T(8,128)(2,1)S(1)}, bf16[272,128]{1,0:T(8,128)(2,1)S(1)}, u32[]{:S(2)}, u32[]{:S(2)}) %collective-permute-start.8) | collective-permute-done | bytes 69664 | tf_op jit(solution)/shard_map/ppermute | solution.py:762
  83.4 1.9 %collective-permute-done.7 = bf16[272,128]{1,0:T(8,128)(2,1)S(1)} collective-permute-done((bf16[272,128]{1,0:T(8,128)(2,1)S(1)}, bf16[272,128]{1,0:T(8,128)(2,1)S(1)}, u32[]{:S(2)}, u32[]{:S(2)}) %collective-permute-start.7) | collective-permute-done | bytes 69664 | tf_op jit(solution)/shard_map/ppermute | solution.py:762
  85.3 3.1 %collective-permute-start.11 = (bf16[272,128]{1,0:T(8,128)(2,1)S(1)}, bf16[272,128]{1,0:T(8,128)(2,1)S(1)}, u32[]{:S(2)}, u32[]{:S(2)}) collective-permute-start(bf16[272,128]{1,0:T(8,128)(2,1)S(1)} %fusion.2), channel_id=1, source_target_pairs={{0,6},{1,7},{2,4},{3,5},{4,2},{5,3},{6,0},{7,1},{8,14},{9,15},{10,... | collective-permute-start | bytes 208904 | tf_op jit(solution)/shard_map/ppermute | solution.py:762
  88.4 1.1 collective-permute-start.9
  89.5 1.4 %collective-permute-done.11 = bf16[272,128]{1,0:T(8,128)(2,1)S(1)} collective-permute-done((bf16[272,128]{1,0:T(8,128)(2,1)S(1)}, bf16[272,128]{1,0:T(8,128)(2,1)S(1)}, u32[]{:S(2)}, u32[]{:S(2)}) %collective-permute-start.11) | collective-permute-done | bytes 69664 | tf_op jit(solution)/shard_map/ppermute | solution.py:762
  90.9 3.3 %collective-permute-done.10 = bf16[272,128]{1,0:T(8,128)(2,1)S(1)} collective-permute-done((bf16[272,128]{1,0:T(8,128)(2,1)S(1)}, bf16[272,128]{1,0:T(8,128)(2,1)S(1)}, u32[]{:S(2)}, u32[]{:S(2)}) %collective-permute-start.10) | collective-permute-done | bytes 69664 | tf_op jit(solution)/shard_map/ppermute | solution.py:762
  94.4 2.6 %collective-permute-start.15 = (bf16[272,128]{1,0:T(8,128)(2,1)S(1)}, bf16[272,128]{1,0:T(8,128)(2,1)S(1)}, u32[]{:S(2)}, u32[]{:S(2)}) collective-permute-start(bf16[272,128]{1,0:T(8,128)(2,1)S(1)} %convert_element_type.52), channel_id=1, source_target_pairs={{0,65},{1,64},{2,67},{3,66},{4,69},{5,68},{6,71},{7,70},{8,73},{9,... | collective-permute-start | bytes 208904 | tf_op jit(solution)/shard_map/ppermute | solution.py:813
  97.2 1.9 %collective-permute-start.13 = (bf16[272,128]{1,0:T(8,128)(2,1)S(1)}, bf16[272,128]{1,0:T(8,128)(2,1)S(1)}, u32[]{:S(2)}, u32[]{:S(2)}) collective-permute-start(bf16[272,128]{1,0:T(8,128)(2,1)S(1)} %convert_element_type.52), channel_id=1, source_target_pairs={{0,1},{1,0},{2,3},{3,2},{4,5},{5,4},{6,7},{7,6},{8,9},{9,8},{10,11... | collective-permute-start | bytes 208904 | tf_op jit(solution)/shard_map/ppermute | solution.py:762
  99.2 2.8 %assemble.2.rest_0_ = bf16[8,36,24,192]{3,2,1,0:T(8,128)(2,1)} custom-call(bf16[8,24,24,192]{3,2,1,0:T(8,128)(2,1)} %get-tuple-element.57.inner, bf16[8,6,24,192]{3,2,1,0:T(8,128)(2,1)} %get-tuple-element.58.oe, bf16[8,30,8,192]{3,2,1,0:T(8,128)(2,1)} %get-tuple-element.59.os_, bf16[8,216,128]{2,1,0:T(8,128)(2,1)} %copy-done.1, ...), custom_call_target="tpu_custom_call" | custom-call | bytes 3000000 | tf_op jit(solution)/shard_map/assemble/pallas_call | solution.py:687
  102.0 1.1 collective-permute-done.13
  103.1 3.2 %collective-permute-start.17 = (bf16[272,128]{1,0:T(8,128)(2,1)S(1)}, bf16[272,128]{1,0:T(8,128)(2,1)S(1)}, u32[]{:S(2)}, u32[]{:S(2)}) collective-permute-start(bf16[272,128]{1,0:T(8,128)(2,1)S(1)} %convert_add_fusion.1), channel_id=1, source_target_pairs={{0,32},{8,40},{16,48},{24,56},{32,0},{40,8},{48,16},{56,24},{64,96... | collective-permute-start | bytes 208904 | tf_op jit(solution)/shard_map/ppermute | solution.py:762
  106.3 1.0 collective-permute-start.18
  107.3 2.8 %assemble.3 = bf16[8,36,24,192]{3,2,1,0:T(8,128)(2,1)} custom-call(bf16[8,24,24,192]{3,2,1,0:T(8,128)(2,1)} %get-tuple-element.57.inner, bf16[8,6,24,192]{3,2,1,0:T(8,128)(2,1)} %get-tuple-element.58.oe, bf16[8,30,8,192]{3,2,1,0:T(8,128)(2,1)} %get-tuple-element.59.os_, bf16[8,216,128]{2,1,0:T(8,128)(2,1)} %copy-done.1, ...), custom_call_target="tpu_custom_call", output_to_operand_aliasing={{}: (6, {})} | custom-call | bytes 3000000 | tf_op jit(solution)/shard_map/assemble/pallas_call | solution.py:687
  110.0 0.6 collective-permute-done.16
  110.6 1.2 %collective-permute-done.18 = bf16[272,128]{1,0:T(8,128)(2,1)S(1)} collective-permute-done((bf16[272,128]{1,0:T(8,128)(2,1)S(1)}, bf16[272,128]{1,0:T(8,128)(2,1)S(1)}, u32[]{:S(2)}, u32[]{:S(2)}) %collective-permute-start.18) | collective-permute-done | bytes 69664 | tf_op jit(solution)/shard_map/ppermute | solution.py:762
  112.0 1.5 %collective-permute-done.19 = bf16[4,272,128]{2,1,0:T(8,128)(2,1)S(1)} collective-permute-done((bf16[4,272,128]{2,1,0:T(8,128)(2,1)S(1)}, bf16[4,272,128]{2,1,0:T(8,128)(2,1)S(1)}, u32[]{:S(2)}, u32[]{:S(2)}) %collective-permute-start.19) | collective-permute-done | bytes 278560 | tf_op jit(solution)/shard_map/ppermute | solution.py:762
  113.6 0.7 copy-done.5
  114.3 2.7 %finish_sums.1 = (f32[192,576]{1,0:T(8,128)}, f32[192,192]{1,0:T(8,128)}, f32[6,144,144]{2,1,0:T(8,128)}, f32[1,192]{1,0:T(1,128)}) custom-call(bf16[1088,128]{1,0:T(8,128)(2,1)} %bitcast.48, bf16[1088,128]{1,0:T(8,128)(2,1)} %bitcast.50, s32[1,1]{1,0:T(1,128)} %bitcast.4.core.refs_2_, f32[1,192]{1,0:T(1,128)} %bitcast.57, bf16[192,576]{1,0:T(8,128)(2,1)} %refs_4_.1), custom_call_target="tpu_custom_call" | custom-call | tf_op jit(solution)/shard_map/finish_sums/pallas_call | solution.py:727
  (41 shorter events, 1.6 us)
Async XLA Ops:
  5.6 33.9 %collective-permute-start = (bf16[2,8,216,128]{3,2,1,0:T(8,128)(2,1)}, bf16[2,8,216,128]{3,2,1,0:T(8,128)(2,1)S(1)}, u32[]{:S(2)}, u32[]{:S(2)}) collective-permute-start(bf16[2,8,216,128]{3,2,1,0:T(8,128)(2,1)} %get-tuple-element.38), channel_id=1, source_target_pairs={{0,120},{8,0},{16,8},{24,16},{32,24},{40,32},{48,40},{56,48},{64,5... | collective-permute-start | bytes 2654216 | tf_op jit(solution)/shard_map/ppermute | solution.py:757
  9.1 30.4 %collective-permute-start.1 = (bf16[2,8,144,128]{3,2,1,0:T(8,128)(2,1)}, bf16[2,8,144,128]{3,2,1,0:T(8,128)(2,1)S(1)}, u32[]{:S(2)}, u32[]{:S(2)}) collective-permute-start(bf16[2,8,144,128]{3,2,1,0:T(8,128)(2,1)} %get-tuple-element.39), channel_id=1, source_target_pairs={{0,7},{1,0},{2,1},{3,2},{4,3},{5,4},{6,5},{7,6},{8,15},{9,8},{10,9... | collective-permute-start | bytes 1769480 | tf_op jit(solution)/shard_map/ppermute | solution.py:757
  15.3 24.2 %collective-permute-start.2 = (bf16[2,4,56,128]{3,2,1,0:T(8,128)(2,1)}, bf16[2,4,56,128]{3,2,1,0:T(8,128)(2,1)S(1)}, u32[]{:S(2)}, u32[]{:S(2)}) collective-permute-start(bf16[2,4,56,128]{3,2,1,0:T(8,128)(2,1)} %get-tuple-element.40), channel_id=1, source_target_pairs={{0,127},{1,120},{2,121},{3,122},{4,123},{5,124},{6,125},{7,126},{8... | collective-permute-start | bytes 344072 | tf_op jit(solution)/shard_map/ppermute | solution.py:757
  39.4 0.6 copy-start.7
  39.5 0.9 copy-start.4
  39.5 1.1 copy-start
  57.1 17.6 %collective-permute-start.3 = (bf16[8,144,128]{2,1,0:T(8,128)(2,1)}, bf16[8,144,128]{2,1,0:T(8,128)(2,1)S(1)}, u32[]{:S(2)}, u32[]{:S(2)}) collective-permute-start(bf16[8,144,128]{2,1,0:T(8,128)(2,1)} %get-tuple-element.52), channel_id=1, source_target_pairs={{0,1},{1,2},{2,3},{3,4},{4,5},{5,6},{6,7},{7,0},{8,9},{9,10},{10,1... | collective-permute-start | bytes 884744 | tf_op jit(solution)/shard_map/ppermute | solution.py:757
  58.8 15.8 %collective-permute-start.4 = (bf16[4,56,128]{2,1,0:T(8,128)(2,1)}, bf16[4,56,128]{2,1,0:T(8,128)(2,1)S(1)}, u32[]{:S(2)}, u32[]{:S(2)}) collective-permute-start(bf16[4,56,128]{2,1,0:T(8,128)(2,1)} %get-tuple-element.53), channel_id=1, source_target_pairs={{0,9},{1,10},{2,11},{3,12},{4,13},{5,14},{6,15},{7,8},{8,17},{9,18... | collective-permute-start | bytes 172040 | tf_op jit(solution)/shard_map/ppermute | solution.py:757
  74.6 24.5 %copy-start.6 = (bf16[4,56,128]{2,1,0:T(8,128)(2,1)}, bf16[4,56,128]{2,1,0:T(8,128)(2,1)S(1)}, u32[]{:S(2)}) copy-start(bf16[4,56,128]{2,1,0:T(8,128)(2,1)S(1)} %collective-permute-done.4.gc) | copy-start | bytes 172036
  74.6 24.5 %copy-start.2 = (bf16[8,144,128]{2,1,0:T(8,128)(2,1)}, bf16[8,144,128]{2,1,0:T(8,128)(2,1)S(1)}, u32[]{:S(2)}) copy-start(bf16[8,144,128]{2,1,0:T(8,128)(2,1)S(1)} %collective-permute-done.3.gs) | copy-start | bytes 884740
  74.6 1.8 %collective-permute-start.5 = (bf16[1088,128]{1,0:T(8,128)(2,1)}, bf16[1088,128]{1,0:T(8,128)(2,1)S(1)}, u32[]{:S(2)}, u32[]{:S(2)}) collective-permute-start(bf16[1088,128]{1,0:T(8,128)(2,1)} %get-tuple-element.54), channel_id=1, source_target_pairs={{0,8},{8,0},{16,24},{24,16},{32,40},{40,32},{48,56},{56,48},{64,72... | collective-permute-start | bytes 835592 | tf_op jit(solution)/shard_map/ppermute | solution.py:762
  77.7 4.4 %collective-permute-start.6 = (bf16[272,128]{1,0:T(8,128)(2,1)S(1)}, bf16[272,128]{1,0:T(8,128)(2,1)S(1)}, u32[]{:S(2)}, u32[]{:S(2)}) collective-permute-start(bf16[272,128]{1,0:T(8,128)(2,1)S(1)} %get-tuple-element.75), channel_id=1, source_target_pairs={{0,16},{8,24},{16,0},{24,8},{32,48},{40,56},{48,32},{56,40},{64,80... | collective-permute-start | bytes 208904 | tf_op jit(solution)/shard_map/ppermute | solution.py:762
  77.8 5.6 %collective-permute-start.8 = (bf16[272,128]{1,0:T(8,128)(2,1)S(1)}, bf16[272,128]{1,0:T(8,128)(2,1)S(1)}, u32[]{:S(2)}, u32[]{:S(2)}) collective-permute-start(bf16[272,128]{1,0:T(8,128)(2,1)S(1)} %get-tuple-element.76), channel_id=1, source_target_pairs={{0,48},{8,56},{16,32},{24,40},{32,16},{40,24},{48,0},{56,8},{64,11... | collective-permute-start | bytes 208904 | tf_op jit(solution)/shard_map/ppermute | solution.py:762
  79.5 5.8 %collective-permute-start.7 = (bf16[272,128]{1,0:T(8,128)(2,1)S(1)}, bf16[272,128]{1,0:T(8,128)(2,1)S(1)}, u32[]{:S(2)}, u32[]{:S(2)}) collective-permute-start(bf16[272,128]{1,0:T(8,128)(2,1)S(1)} %get-tuple-element.77), channel_id=1, source_target_pairs={{0,32},{8,40},{16,48},{24,56},{32,0},{40,8},{48,16},{56,24},{64,96... | collective-permute-start | bytes 208904 | tf_op jit(solution)/shard_map/ppermute | solution.py:762
  81.9 12.5 %collective-permute-start.12 = (bf16[8,216,128]{2,1,0:T(8,128)(2,1)}, bf16[8,216,128]{2,1,0:T(8,128)(2,1)S(1)}, u32[]{:S(2)}, u32[]{:S(2)}) collective-permute-start(bf16[8,216,128]{2,1,0:T(8,128)(2,1)} %get-tuple-element.55), channel_id=1, source_target_pairs={{0,8},{8,16},{16,24},{24,32},{32,40},{40,48},{48,56},{56,64},{64,7... | collective-permute-start | bytes 1327112 | tf_op jit(solution)/shard_map/ppermute | solution.py:757
  85.3 5.6 %collective-permute-start.11 = (bf16[272,128]{1,0:T(8,128)(2,1)S(1)}, bf16[272,128]{1,0:T(8,128)(2,1)S(1)}, u32[]{:S(2)}, u32[]{:S(2)}) collective-permute-start(bf16[272,128]{1,0:T(8,128)(2,1)S(1)} %fusion.2), channel_id=1, source_target_pairs={{0,6},{1,7},{2,4},{3,5},{4,2},{5,3},{6,0},{7,1},{8,14},{9,15},{10,... | collective-permute-start | bytes 208904 | tf_op jit(solution)/shard_map/ppermute | solution.py:762
  88.4 5.8 %collective-permute-start.10 = (bf16[272,128]{1,0:T(8,128)(2,1)S(1)}, bf16[272,128]{1,0:T(8,128)(2,1)S(1)}, u32[]{:S(2)}, u32[]{:S(2)}) collective-permute-start(bf16[272,128]{1,0:T(8,128)(2,1)S(1)} %fusion.2), channel_id=1, source_target_pairs={{0,4},{1,5},{2,6},{3,7},{4,0},{5,1},{6,2},{7,3},{8,12},{9,13},{10,... | collective-permute-start | bytes 208904 | tf_op jit(solution)/shard_map/ppermute | solution.py:762
  88.4 5.8 %collective-permute-start.9 = (bf16[272,128]{1,0:T(8,128)(2,1)S(1)}, bf16[272,128]{1,0:T(8,128)(2,1)S(1)}, u32[]{:S(2)}, u32[]{:S(2)}) collective-permute-start(bf16[272,128]{1,0:T(8,128)(2,1)S(1)} %fusion.2), channel_id=1, source_target_pairs={{0,2},{1,3},{2,0},{3,1},{4,6},{5,7},{6,4},{7,5},{8,10},{9,11},{10,... | collective-permute-start | bytes 208904 | tf_op jit(solution)/shard_map/ppermute | solution.py:762
  94.3 4.8 %copy-start.1 = (bf16[8,216,128]{2,1,0:T(8,128)(2,1)}, bf16[8,216,128]{2,1,0:T(8,128)(2,1)S(1)}, u32[]{:S(2)}) copy-start(bf16[8,216,128]{2,1,0:T(8,128)(2,1)S(1)} %collective-permute-done.12.gl) | copy-start | bytes 1327108
  94.4 7.6 %collective-permute-start.15 = (bf16[272,128]{1,0:T(8,128)(2,1)S(1)}, bf16[272,128]{1,0:T(8,128)(2,1)S(1)}, u32[]{:S(2)}, u32[]{:S(2)}) collective-permute-start(bf16[272,128]{1,0:T(8,128)(2,1)S(1)} %convert_element_type.52), channel_id=1, source_target_pairs={{0,65},{1,64},{2,67},{3,66},{4,69},{5,68},{6,71},{7,70},{8,73},{9,... | collective-permute-start | bytes 208904 | tf_op jit(solution)/shard_map/ppermute | solution.py:813
  97.0 4.9 %collective-permute-start.14 = (bf16[272,128]{1,0:T(8,128)(2,1)S(1)}, bf16[272,128]{1,0:T(8,128)(2,1)S(1)}, u32[]{:S(2)}, u32[]{:S(2)}) collective-permute-start(bf16[272,128]{1,0:T(8,128)(2,1)S(1)} %convert_element_type.52), channel_id=1, source_target_pairs={{0,64},{8,72},{16,80},{24,88},{32,96},{40,104},{48,112},{56,120},{... | collective-permute-start | bytes 208904 | tf_op jit(solution)/shard_map/ppermute | solution.py:762
  97.2 5.8 %collective-permute-start.13 = (bf16[272,128]{1,0:T(8,128)(2,1)S(1)}, bf16[272,128]{1,0:T(8,128)(2,1)S(1)}, u32[]{:S(2)}, u32[]{:S(2)}) collective-permute-start(bf16[272,128]{1,0:T(8,128)(2,1)S(1)} %convert_element_type.52), channel_id=1, source_target_pairs={{0,1},{1,0},{2,3},{3,2},{4,5},{5,4},{6,7},{7,6},{8,9},{9,8},{10,11... | collective-permute-start | bytes 208904 | tf_op jit(solution)/shard_map/ppermute | solution.py:762
  103.1 6.9 %collective-permute-start.17 = (bf16[272,128]{1,0:T(8,128)(2,1)S(1)}, bf16[272,128]{1,0:T(8,128)(2,1)S(1)}, u32[]{:S(2)}, u32[]{:S(2)}) collective-permute-start(bf16[272,128]{1,0:T(8,128)(2,1)S(1)} %convert_add_fusion.1), channel_id=1, source_target_pairs={{0,32},{8,40},{16,48},{24,56},{32,0},{40,8},{48,16},{56,24},{64,96... | collective-permute-start | bytes 208904 | tf_op jit(solution)/shard_map/ppermute | solution.py:762
  106.3 4.3 %collective-permute-start.16 = (bf16[272,128]{1,0:T(8,128)(2,1)S(1)}, bf16[272,128]{1,0:T(8,128)(2,1)S(1)}, u32[]{:S(2)}, u32[]{:S(2)}) collective-permute-start(bf16[272,128]{1,0:T(8,128)(2,1)S(1)} %convert_add_fusion.1), channel_id=1, source_target_pairs={{0,16},{8,24},{16,0},{24,8},{32,48},{40,56},{48,32},{56,40},{64,80... | collective-permute-start | bytes 208904 | tf_op jit(solution)/shard_map/ppermute | solution.py:762
  106.3 5.5 %collective-permute-start.18 = (bf16[272,128]{1,0:T(8,128)(2,1)S(1)}, bf16[272,128]{1,0:T(8,128)(2,1)S(1)}, u32[]{:S(2)}, u32[]{:S(2)}) collective-permute-start(bf16[272,128]{1,0:T(8,128)(2,1)S(1)} %convert_add_fusion.1), channel_id=1, source_target_pairs={{0,48},{8,56},{16,32},{24,40},{32,16},{40,24},{48,0},{56,8},{64,11... | collective-permute-start | bytes 208904 | tf_op jit(solution)/shard_map/ppermute | solution.py:762
  111.9 1.7 %copy-start.3 = (bf16[4,272,128]{2,1,0:T(8,128)(2,1)}, bf16[4,272,128]{2,1,0:T(8,128)(2,1)S(1)}, u32[]{:S(2)}) copy-start(bf16[4,272,128]{2,1,0:T(8,128)(2,1)S(1)} %pad_maximum_fusion.1) | copy-start | bytes 835588
  111.9 1.6 %collective-permute-start.19 = (bf16[4,272,128]{2,1,0:T(8,128)(2,1)S(1)}, bf16[4,272,128]{2,1,0:T(8,128)(2,1)S(1)}, u32[]{:S(2)}, u32[]{:S(2)}) collective-permute-start(bf16[4,272,128]{2,1,0:T(8,128)(2,1)S(1)} %pad_maximum_fusion.1), channel_id=1, source_target_pairs={{0,8},{8,0},{16,24},{24,16},{32,40},{40,32},{48,56},{56,48},{64,72... | collective-permute-start | bytes 835592 | tf_op jit(solution)/shard_map/ppermute | solution.py:762
  113.6 0.7 copy-start.5

commit v7 on v6

--- a/solution.py
+++ b/solution.py
@@ -235,28 +235,33 @@
 
 def inner_steps(xs, ys, consts, bias, dx_ref, gw_ref, gb_ref, scratch):
     def place(lv, lon):
-        return 24 * (24 * (lon // 12) + 12 * lv + lon % 12)
-
-    def take(k):
-        for lv in range(2):
-            for lon in range(12 * k, 12 * k + 12):
-                keep(scratch[0], scratch[1], place(lv, lon), xs[lon // 6][lv, lon % 6])
-                keep(scratch[2], scratch[3], place(lv, lon), ys[lon // 6][lv, lon % 6])
-
-    def give(k):
-        for lv in range(2):
-            for lon in range(12 * k, 12 * k + 12):
-                dx_ref[lv, lon] = kept(scratch[4], scratch[5], place(lv, lon), 24)
-
-    take(0)
+        return 1152 * (lv // 2) + 24 * (24 * (lon // 12) + 12 * (lv % 2) + lon % 12)
+
+    def columns(group):
+        p, k = group // 2, group % 2
+        return [(2 * p + lv, 12 * k + lon) for lv in range(2) for lon in range(12)]
+
+    def take(group):
+        for lv, lon in columns(group):
+            keep(scratch[0], scratch[1], place(lv, lon), xs[lon // 6][lv, lon % 6])
+            keep(scratch[2], scratch[3], place(lv, lon), ys[lon // 6][lv, lon % 6])
+
+    def give(group):
+        for lv, lon in columns(group):
+            dx_ref[lv, lon] = kept(scratch[4], scratch[5], place(lv, lon), 24)
+
     refs = dict(zip(("gain", "wqkv", "wqkv_t", "wout_t"), consts), bias=bias, gb=gb_ref)
     windows = [
-        window_of(scratch, 576 * k + 3 + 6 * a, 24, 0, refs) for k in range(2) for a in range(3)
+        window_of(scratch, 576 * group + 3 + 6 * a, 24, 0, refs)
+        for group in range(4)
+        for a in range(3)
     ]
-    windows[1].also_first = lambda: take(1)
-    windows[2].also_last = lambda: give(0)
+    take(0)
+    for group in range(3):
+        windows[3 * group + 1].also_first = lambda g=group + 1: take(g)
+        windows[3 * group + 2].also_last = lambda g=group: give(g)
     run_windows(windows, gw_ref)
-    give(1)
+    give(3)
 
 
 def inner_kernel(
@@ -330,13 +335,13 @@
     return wide[:36], jnp.concatenate([high, jnp.zeros((36, 64), F32)], axis=1)
 
 
-def pack_kernel(x, y, e_ref, s_ref, c_ref, low, high):
+def pack_kernel(x, y, xe, ye, e_ref, s_ref, c_ref, low, high):
     pad = jnp.zeros((2, D), F32)
-    for n, own in enumerate((x, y)):
+    for n, (own, edge) in enumerate(((x, xe), (y, ye))):
         corners = []
         for lv in range(2):
             base = 288 * (2 * n + lv)
-            east = jnp.concatenate([own[lv, lon].astype(F32) for lon in range(6)], axis=0)
+            east = jnp.concatenate([edge[lv, lon].astype(F32) for lon in range(6)], axis=0)
             e_ref[n, lv] = dense(east[:, :128], east[:, 128:])
             for lon in range(36):
                 rows = own[lv, lon].astype(F32)[:8]
@@ -371,52 +376,55 @@
     def corner(lv, t):
         return pl.ds(place(lv, 30) + 8 + t, 6, stride=16)
 
-    for n, own in enumerate((x, y)):
-        low, high = scratch[2 * n], scratch[2 * n + 1]
-        for lv in range(4):
-            if lv % 2 == 0:
-                cleft, cright = undense_corner(c[n, lv // 2])
+    def take(p):
+        for n, own in enumerate((x, y)):
+            low, high = scratch[2 * n], scratch[2 * n + 1]
+            for lv in (2 * p, 2 * p + 1):
+                if lv % 2 == 0:
+                    cleft, cright = undense_corner(c[n, lv // 2])
+                for lon in range(30):
+                    keep(low, high, place(lv, lon), own[lv, 6 + lon].astype(F32)[16:])
+                left, right = undense(e[n, lv])
+                for lon in range(6):
+                    at = place(lv, 30 + lon)
+                    low[at : at + 8, :] = left[24 * lon + 16 : 24 * lon + 24]
+                    high[at : at + 8, :] = right[24 * lon + 16 : 24 * lon + 24]
+                left, right = undense(s[n, lv])
+                for t in range(3):
+                    for m, at in enumerate(south(lv, t)):
+                        rows = slice(32 * t + 12 * m, 32 * t + min(12 * m + 12, 30))
+                        low[at, :] = left[rows]
+                        high[at, :] = right[rows]
+                    rows = slice(18 * (lv % 2) + 6 * t, 18 * (lv % 2) + 6 * t + 6)
+                    low[corner(lv, t), :] = cleft[rows]
+                    high[corner(lv, t), :] = cright[rows]
+
+    def give(p):
+        low, high = scratch[4], scratch[5]
+        pad = jnp.zeros((2, D), F32)
+        corners = []
+        for lv in (2 * p, 2 * p + 1):
             for lon in range(30):
-                keep(low, high, place(lv, lon), own[lv, 6 + lon].astype(F32)[16:])
-            left, right = undense(e[n, lv])
+                os_ref[lv, lon] = kept(low, high, place(lv, lon), 8)
             for lon in range(6):
-                at = place(lv, 30 + lon)
-                low[at : at + 8, :] = left[24 * lon + 16 : 24 * lon + 24]
-                high[at : at + 8, :] = right[24 * lon + 16 : 24 * lon + 24]
-            left, right = undense(s[n, lv])
+                tail_ref[lv, lon] = kept(low, high, place(lv, 30 + lon), 8)
+            parts = []
             for t in range(3):
-                for m, at in enumerate(south(lv, t)):
-                    rows = slice(32 * t + 12 * m, 32 * t + min(12 * m + 12, 30))
-                    low[at, :] = left[rows]
-                    high[at, :] = right[rows]
-                rows = slice(18 * (lv % 2) + 6 * t, 18 * (lv % 2) + 6 * t + 6)
-                low[corner(lv, t), :] = cleft[rows]
-                high[corner(lv, t), :] = cright[rows]
+                parts += [joined(low, high, at) for at in south(lv, t)] + [pad]
+                corners.append(joined(low, high, corner(lv, t)))
+            rows = jnp.concatenate(parts, axis=0)
+            bs_ref[lv] = dense(rows[:, :128], rows[:, 128:])
+        bc_ref[p] = dense_corner(jnp.concatenate(corners, axis=0))
+
+    take(0)
     refs = dict(gain=gain, wqkv=wqkv, wqkv_t=wqkv_t, wout_t=wout_t, bias=bias, gb=gb_ref)
-    run_windows(
-        [
-            window_of(scratch, 1152 * p + 384 * k + 5, 16, 1, refs)
-            for p in range(2)
-            for k in range(3)
-        ],
-        gw_ref,
-    )
-    low, high = scratch[4], scratch[5]
-    pad = jnp.zeros((2, D), F32)
-    corners = []
-    for lv in range(4):
-        for lon in range(30):
-            os_ref[lv, lon] = kept(low, high, place(lv, lon), 8)
-        for lon in range(6):
-            tail_ref[lv, lon] = kept(low, high, place(lv, 30 + lon), 8)
-        parts = []
-        for t in range(3):
-            parts += [joined(low, high, at) for at in south(lv, t)] + [pad]
-            corners.append(joined(low, high, corner(lv, t)))
-        rows = jnp.concatenate(parts, axis=0)
-        bs_ref[lv] = dense(rows[:, :128], rows[:, 128:])
-    for p in range(2):
-        bc_ref[p] = dense_corner(jnp.concatenate(corners[6 * p : 6 * p + 6], axis=0))
+    windows = [
+        window_of(scratch, 1152 * p + 384 * k + 5, 16, 1, refs) for p in range(2) for k in range(3)
+    ]
+    windows[1].also_first = lambda: take(1)
+    windows[2].also_last = lambda: give(0)
+    run_windows(windows, gw_ref)
+    give(1)
 
 
 def east_kernel(
@@ -491,14 +499,14 @@
 
 def inner_specs():
     def cols(n):
-        return pl.BlockSpec((2, 6, 24, D), lambda i: (i, n, 0, 0))
-
-    four = [cols(n) for n in range(1, 5)]
-    return four + four, pl.BlockSpec((2, 24, 24, D), lambda i: (i, 0, 0, 0))
+        return pl.BlockSpec((4, 6, 24, D), lambda i: (i, n, 0, 0))
+
+    parts = [cols(n) for n in range(1, 5)]
+    return parts + parts, pl.BlockSpec((4, 24, 24, D), lambda i: (i, 0, 0, 0))
 
 
 def inner_windows(x, y, weights, pair_bias, last):
-    steps = x.shape[0] // 2
+    steps = x.shape[0] // 4
     ins, out = inner_specs()
     return pl.pallas_call(
         inner_kernel,
@@ -515,9 +523,9 @@
             jax.ShapeDtypeStruct((3 * D, D), BF16),
             jax.ShapeDtypeStruct((D, D), BF16),
         ],
-        scratch_shapes=halves(1152),
+        scratch_shapes=halves(2304),
         compiler_params=PARAMS,
-        cost_estimate=cost(6 * steps),
+        cost_estimate=cost(12 * steps),
         name="inner_windows",
     )(x, x, x, x, y, y, y, y, *weights, pair_bias, last)
 
@@ -545,7 +553,7 @@
     return pl.pallas_call(
         pack_kernel,
         grid=(levels // 2,),
-        in_specs=[one(36, 24, D), one(36, 24, D)],
+        in_specs=[one(36, 16, D), one(36, 16, D), one(6, 24, D), one(6, 24, D)],
         out_specs=[both(216, 128), both(144, 128), both_corner()],
         out_shape=[
             jax.ShapeDtypeStruct((2, levels, 216, 128), BF16),
@@ -555,7 +563,7 @@
         scratch_shapes=[pltpu.VMEM((1152, 128), F32), pltpu.VMEM((1152, 128), F32)],
         compiler_params=PARAMS,
         name="pack_halo",
-    )(x, y)
+    )(x, y, x, y)
 
 
 def four(*rest, at=0):

time: 118 us -> 118 us (level)
  no operation moved by 1% of the time
where the time goes in v7:
time: 118 us; the launch traced here: 116 us
  Pallas kernels  67.1 us (57%)
  starting transfers between devices  30.6 us (26%)
  waiting for transfers between devices  14.3 us (12%)
  local copies, waits for them, and re-layouts  1.89 us (2%)
  other arithmetic  1.38 us (1%)
    pallas_call x1, Pallas kernels, inner_windows(): pl.pallas_call(inner_kernel, grid=(steps,), in_specs=ins + [whole((1, D))...  23 us
    pallas_call x1, Pallas kernels, south_windows(): pl.pallas_call(south_kernel, grid=(levels // 4,), in_specs=[four(36, 24,...  16.7 us
    ppermute x13, starting transfers between devices, moved(): return lax.ppermute(value, axis, [(n, to_of(n)) for n in range(count)])  14.9 us
    pallas_call x1, Pallas kernels, east_windows(): pl.pallas_call(east_kernel, grid=(levels // 4,), in_specs=[four(6, 24, D,...  14.5 us
    ppermute x13, waiting for transfers between devices, moved(): return lax.ppermute(value, axis, [(n, to_of(n)) for n in range(count)])  14.3 us
    ppermute x6, starting transfers between devices, shift(): return lax.ppermute(value, axes if len(axes) > 1 else axes[0], pairs)  13.1 us
    pallas_call x2, Pallas kernels, assemble(): pl.pallas_call(assemble_kernel, grid=(steps,), in_specs=specs, out_specs=...  5.53 us
    pallas_call x1, Pallas kernels, pack_halo(): pl.pallas_call(pack_kernel, grid=(levels // 2,), in_specs=[one(36, 16, D)...  4.69 us
  transfers between devices with their start and end apart: 20, of which 10 were waited for; matrix products, arithmetic and copies ran while one was open for 0% of the time, Pallas kernels for 37%

profile of v7, /device:TPU:0, one launch (start us, length us, event | category | flops | bytes accessed | tf_op | source)
XLA Modules:
  0.0 116.1 jit_solution(10249703169550576358)
XLA Ops:
  0.6 4.7 %pack_halo.1 = (bf16[2,8,216,128]{3,2,1,0:T(8,128)(2,1)}, bf16[2,8,144,128]{3,2,1,0:T(8,128)(2,1)}, bf16[2,4,56,128]{3,2,1,0:T(8,128)(2,1)}) custom-call(bf16[8,36,24,192]{3,2,1,0:T(8,128)(2,1)} %bitcast.30, bf16[8,36,24,192]{3,2,1,0:T(8,128)(2,1)} %bitcast.38, bf16[8,36,24,192]{3,2,1,0:T(8,128)(2,1)} %bitcast.31, bf16[8,36,24,192]{3,2,1,0:T(8,128)(2,1)} %bitcast.39), custom_call_target="tpu_custom_call" | custom-call | tf_op jit(solution)/shard_map/pack_halo/pallas_call | solution.py:553
  5.3 3.5 %collective-permute-start = (bf16[2,8,216,128]{3,2,1,0:T(8,128)(2,1)}, bf16[2,8,216,128]{3,2,1,0:T(8,128)(2,1)S(1)}, u32[]{:S(2)}, u32[]{:S(2)}) collective-permute-start(bf16[2,8,216,128]{3,2,1,0:T(8,128)(2,1)} %get-tuple-element.38), channel_id=1, source_target_pairs={{0,120},{8,0},{16,8},{24,16},{32,24},{40,32},{48,40},{56,48},{64,5... | collective-permute-start | bytes 2654216 | tf_op jit(solution)/shard_map/ppermute | solution.py:765
  8.8 6.2 %collective-permute-start.1 = (bf16[2,8,144,128]{3,2,1,0:T(8,128)(2,1)}, bf16[2,8,144,128]{3,2,1,0:T(8,128)(2,1)S(1)}, u32[]{:S(2)}, u32[]{:S(2)}) collective-permute-start(bf16[2,8,144,128]{3,2,1,0:T(8,128)(2,1)} %get-tuple-element.39), channel_id=1, source_target_pairs={{0,7},{1,0},{2,1},{3,2},{4,3},{5,4},{6,5},{7,6},{8,15},{9,8},{10,9... | collective-permute-start | bytes 1769480 | tf_op jit(solution)/shard_map/ppermute | solution.py:765
  15.0 0.3 collective-permute-start.2
  15.3 23.0 %inner_windows.1 = (bf16[8,24,24,192]{3,2,1,0:T(8,128)(2,1)}, f32[4,192,192]{2,1,0:T(8,128)}, f32[144,896]{1,0:T(8,128)}, f32[2,144,896]{2,1,0:T(8,128)}, bf16[1...) custom-call(bf16[8,36,24,192]{3,2,1,0:T(8,128)(2,1)} %bitcast.32, ...), custom_call_target="tpu_custom_call" | custom-call | flops 5096079360 | bytes 3981312 | tf_op jit(solution)/shard_map/inner_windows/pallas_call | solution.py:511
  38.4 0.6 copy-done.7
  39.5 16.7 %south_windows.1 = (bf16[8,30,8,192]{3,2,1,0:T(8,128)(2,1)}, bf16[8,6,8,192]{3,2,1,0:T(8,128)(2,1)}, bf16[8,144,128]{2,1,0:T(8,128)(2,1)}, bf16[4,56,128]{2,1,0:...) custom-call(bf16[8,36,24,192]{3,2,1,0:T(8,128)(2,1)} %bitcast.36, bf16[8,36,24,192]{3,2,1,0:T(8,128)(2,1)} %bitcast.44, ...), custom_call_target="tpu_custom_call" | custom-call | flops 2548039680 | bytes 1990656 | tf_op jit(solution)/shard_map/south_windows/pallas_call | solution.py:580
  56.2 1.6 %collective-permute-start.3 = (bf16[8,144,128]{2,1,0:T(8,128)(2,1)}, bf16[8,144,128]{2,1,0:T(8,128)(2,1)S(1)}, u32[]{:S(2)}, u32[]{:S(2)}) collective-permute-start(bf16[8,144,128]{2,1,0:T(8,128)(2,1)} %get-tuple-element.52), channel_id=1, source_target_pairs={{0,1},{1,2},{2,3},{3,4},{4,5},{5,6},{6,7},{7,0},{8,9},{9,10},{10,1... | collective-permute-start | bytes 884744 | tf_op jit(solution)/shard_map/ppermute | solution.py:765
  57.8 1.5 %collective-permute-start.4 = (bf16[4,56,128]{2,1,0:T(8,128)(2,1)}, bf16[4,56,128]{2,1,0:T(8,128)(2,1)S(1)}, u32[]{:S(2)}, u32[]{:S(2)}) collective-permute-start(bf16[4,56,128]{2,1,0:T(8,128)(2,1)} %get-tuple-element.53), channel_id=1, source_target_pairs={{0,9},{1,10},{2,11},{3,12},{4,13},{5,14},{6,15},{7,8},{8,17},{9,18... | collective-permute-start | bytes 172040 | tf_op jit(solution)/shard_map/ppermute | solution.py:765
  59.2 14.5 %east_windows.1 = (bf16[8,6,24,192]{3,2,1,0:T(8,128)(2,1)}, bf16[8,216,128]{2,1,0:T(8,128)(2,1)}, bf16[1088,128]{1,0:T(8,128)(2,1)}, f32[1088,128]{1,0:T(8,128)}) custom-call(bf16[8,36,24,192]{3,2,1,0:T(8,128)(2,1)} %bitcast.37, bf16[8,36,24,192]{3,2,1,0:T(8,128)(2,1)} %bitcast.45, bf16[2,8,216,128]{3,2,1,0:T(8,128)(2,1)} %copy-done, ...), custom_call_target="tpu_custom_call" | custom-call | flops 2548039680 | bytes 1990656 | tf_op jit(solution)/shard_map/east_windows/pallas_call | solution.py:617
  73.9 1.7 %collective-permute-done.5 = bf16[1088,128]{1,0:T(8,128)(2,1)S(1)} collective-permute-done((bf16[1088,128]{1,0:T(8,128)(2,1)}, bf16[1088,128]{1,0:T(8,128)(2,1)S(1)}, u32[]{:S(2)}, u32[]{:S(2)}) %collective-permute-start.5) | collective-permute-done | bytes 278560 | tf_op jit(solution)/shard_map/ppermute | solution.py:770
  75.6 1.1 convert_add_fusion
  76.9 1.7 %collective-permute-start.8 = (bf16[272,128]{1,0:T(8,128)(2,1)S(1)}, bf16[272,128]{1,0:T(8,128)(2,1)S(1)}, u32[]{:S(2)}, u32[]{:S(2)}) collective-permute-start(bf16[272,128]{1,0:T(8,128)(2,1)S(1)} %get-tuple-element.76), channel_id=1, source_target_pairs={{0,48},{8,56},{16,32},{24,40},{32,16},{40,24},{48,0},{56,8},{64,11... | collective-permute-start | bytes 208904 | tf_op jit(solution)/shard_map/ppermute | solution.py:770
  78.6 2.4 %collective-permute-start.7 = (bf16[272,128]{1,0:T(8,128)(2,1)S(1)}, bf16[272,128]{1,0:T(8,128)(2,1)S(1)}, u32[]{:S(2)}, u32[]{:S(2)}) collective-permute-start(bf16[272,128]{1,0:T(8,128)(2,1)S(1)} %get-tuple-element.77), channel_id=1, source_target_pairs={{0,32},{8,40},{16,48},{24,56},{32,0},{40,8},{48,16},{56,24},{64,96... | collective-permute-start | bytes 208904 | tf_op jit(solution)/shard_map/ppermute | solution.py:770
  81.2 1.3 %collective-permute-done.8 = bf16[272,128]{1,0:T(8,128)(2,1)S(1)} collective-permute-done((bf16[272,128]{1,0:T(8,128)(2,1)S(1)}, bf16[272,128]{1,0:T(8,128)(2,1)S(1)}, u32[]{:S(2)}, u32[]{:S(2)}) %collective-permute-start.8) | collective-permute-done | bytes 69664 | tf_op jit(solution)/shard_map/ppermute | solution.py:770
  82.5 1.9 %collective-permute-done.7 = bf16[272,128]{1,0:T(8,128)(2,1)S(1)} collective-permute-done((bf16[272,128]{1,0:T(8,128)(2,1)S(1)}, bf16[272,128]{1,0:T(8,128)(2,1)S(1)}, u32[]{:S(2)}, u32[]{:S(2)}) %collective-permute-start.7) | collective-permute-done | bytes 69664 | tf_op jit(solution)/shard_map/ppermute | solution.py:770
  84.5 3.1 %collective-permute-start.11 = (bf16[272,128]{1,0:T(8,128)(2,1)S(1)}, bf16[272,128]{1,0:T(8,128)(2,1)S(1)}, u32[]{:S(2)}, u32[]{:S(2)}) collective-permute-start(bf16[272,128]{1,0:T(8,128)(2,1)S(1)} %fusion.2), channel_id=1, source_target_pairs={{0,6},{1,7},{2,4},{3,5},{4,2},{5,3},{6,0},{7,1},{8,14},{9,15},{10,... | collective-permute-start | bytes 208904 | tf_op jit(solution)/shard_map/ppermute | solution.py:770
  87.6 1.1 collective-permute-start.9
  88.7 1.4 %collective-permute-done.11 = bf16[272,128]{1,0:T(8,128)(2,1)S(1)} collective-permute-done((bf16[272,128]{1,0:T(8,128)(2,1)S(1)}, bf16[272,128]{1,0:T(8,128)(2,1)S(1)}, u32[]{:S(2)}, u32[]{:S(2)}) %collective-permute-start.11) | collective-permute-done | bytes 69664 | tf_op jit(solution)/shard_map/ppermute | solution.py:770
  90.1 3.3 %collective-permute-done.10 = bf16[272,128]{1,0:T(8,128)(2,1)S(1)} collective-permute-done((bf16[272,128]{1,0:T(8,128)(2,1)S(1)}, bf16[272,128]{1,0:T(8,128)(2,1)S(1)}, u32[]{:S(2)}, u32[]{:S(2)}) %collective-permute-start.10) | collective-permute-done | bytes 69664 | tf_op jit(solution)/shard_map/ppermute | solution.py:770
  93.5 2.6 %collective-permute-start.15 = (bf16[272,128]{1,0:T(8,128)(2,1)S(1)}, bf16[272,128]{1,0:T(8,128)(2,1)S(1)}, u32[]{:S(2)}, u32[]{:S(2)}) collective-permute-start(bf16[272,128]{1,0:T(8,128)(2,1)S(1)} %convert_element_type.52), channel_id=1, source_target_pairs={{0,65},{1,64},{2,67},{3,66},{4,69},{5,68},{6,71},{7,70},{8,73},{9,... | collective-permute-start | bytes 208904 | tf_op jit(solution)/shard_map/ppermute | solution.py:821
  96.4 1.9 %collective-permute-start.13 = (bf16[272,128]{1,0:T(8,128)(2,1)S(1)}, bf16[272,128]{1,0:T(8,128)(2,1)S(1)}, u32[]{:S(2)}, u32[]{:S(2)}) collective-permute-start(bf16[272,128]{1,0:T(8,128)(2,1)S(1)} %convert_element_type.52), channel_id=1, source_target_pairs={{0,1},{1,0},{2,3},{3,2},{4,5},{5,4},{6,7},{7,6},{8,9},{9,8},{10,11... | collective-permute-start | bytes 208904 | tf_op jit(solution)/shard_map/ppermute | solution.py:770
  98.3 2.8 %assemble.2.rest_0_ = bf16[8,36,24,192]{3,2,1,0:T(8,128)(2,1)} custom-call(bf16[8,24,24,192]{3,2,1,0:T(8,128)(2,1)} %get-tuple-element.57.inner, bf16[8,6,24,192]{3,2,1,0:T(8,128)(2,1)} %get-tuple-element.58.oe, bf16[8,30,8,192]{3,2,1,0:T(8,128)(2,1)} %get-tuple-element.59.os_, bf16[8,216,128]{2,1,0:T(8,128)(2,1)} %copy-done.1, ...), custom_call_target="tpu_custom_call" | custom-call | bytes 3000000 | tf_op jit(solution)/shard_map/assemble/pallas_call | solution.py:695
  101.1 1.1 collective-permute-done.13
  102.2 3.2 %collective-permute-start.17 = (bf16[272,128]{1,0:T(8,128)(2,1)S(1)}, bf16[272,128]{1,0:T(8,128)(2,1)S(1)}, u32[]{:S(2)}, u32[]{:S(2)}) collective-permute-start(bf16[272,128]{1,0:T(8,128)(2,1)S(1)} %convert_add_fusion.1), channel_id=1, source_target_pairs={{0,32},{8,40},{16,48},{24,56},{32,0},{40,8},{48,16},{56,24},{64,96... | collective-permute-start | bytes 208904 | tf_op jit(solution)/shard_map/ppermute | solution.py:770
  105.4 1.0 collective-permute-start.18
  106.4 2.8 %assemble.3 = bf16[8,36,24,192]{3,2,1,0:T(8,128)(2,1)} custom-call(bf16[8,24,24,192]{3,2,1,0:T(8,128)(2,1)} %get-tuple-element.57.inner, bf16[8,6,24,192]{3,2,1,0:T(8,128)(2,1)} %get-tuple-element.58.oe, bf16[8,30,8,192]{3,2,1,0:T(8,128)(2,1)} %get-tuple-element.59.os_, bf16[8,216,128]{2,1,0:T(8,128)(2,1)} %copy-done.1, ...), custom_call_target="tpu_custom_call", output_to_operand_aliasing={{}: (6, {})} | custom-call | bytes 3000000 | tf_op jit(solution)/shard_map/assemble/pallas_call | solution.py:695
  109.2 0.6 collective-permute-done.16
  109.7 1.2 %collective-permute-done.18 = bf16[272,128]{1,0:T(8,128)(2,1)S(1)} collective-permute-done((bf16[272,128]{1,0:T(8,128)(2,1)S(1)}, bf16[272,128]{1,0:T(8,128)(2,1)S(1)}, u32[]{:S(2)}, u32[]{:S(2)}) %collective-permute-start.18) | collective-permute-done | bytes 69664 | tf_op jit(solution)/shard_map/ppermute | solution.py:770
  111.2 1.5 %collective-permute-done.19 = bf16[4,272,128]{2,1,0:T(8,128)(2,1)S(1)} collective-permute-done((bf16[4,272,128]{2,1,0:T(8,128)(2,1)S(1)}, bf16[4,272,128]{2,1,0:T(8,128)(2,1)S(1)}, u32[]{:S(2)}, u32[]{:S(2)}) %collective-permute-start.19) | collective-permute-done | bytes 278560 | tf_op jit(solution)/shard_map/ppermute | solution.py:770
  112.7 0.7 copy-done.5
  113.4 2.7 %finish_sums.1 = (f32[192,576]{1,0:T(8,128)}, f32[192,192]{1,0:T(8,128)}, f32[6,144,144]{2,1,0:T(8,128)}, f32[1,192]{1,0:T(1,128)}) custom-call(bf16[1088,128]{1,0:T(8,128)(2,1)} %bitcast.50, bf16[1088,128]{1,0:T(8,128)(2,1)} %bitcast.52, s32[1,1]{1,0:T(1,128)} %bitcast.4.core.refs_2_, f32[1,192]{1,0:T(1,128)} %bitcast.59, bf16[192,576]{1,0:T(8,128)(2,1)} %refs_4_.1), custom_call_target="tpu_custom_call" | custom-call | tf_op jit(solution)/shard_map/finish_sums/pallas_call | solution.py:735
  (41 shorter events, 1.6 us)
Async XLA Ops:
  5.3 33.1 %collective-permute-start = (bf16[2,8,216,128]{3,2,1,0:T(8,128)(2,1)}, bf16[2,8,216,128]{3,2,1,0:T(8,128)(2,1)S(1)}, u32[]{:S(2)}, u32[]{:S(2)}) collective-permute-start(bf16[2,8,216,128]{3,2,1,0:T(8,128)(2,1)} %get-tuple-element.38), channel_id=1, source_target_pairs={{0,120},{8,0},{16,8},{24,16},{32,24},{40,32},{48,40},{56,48},{64,5... | collective-permute-start | bytes 2654216 | tf_op jit(solution)/shard_map/ppermute | solution.py:765
  8.8 29.6 %collective-permute-start.1 = (bf16[2,8,144,128]{3,2,1,0:T(8,128)(2,1)}, bf16[2,8,144,128]{3,2,1,0:T(8,128)(2,1)S(1)}, u32[]{:S(2)}, u32[]{:S(2)}) collective-permute-start(bf16[2,8,144,128]{3,2,1,0:T(8,128)(2,1)} %get-tuple-element.39), channel_id=1, source_target_pairs={{0,7},{1,0},{2,1},{3,2},{4,3},{5,4},{6,5},{7,6},{8,15},{9,8},{10,9... | collective-permute-start | bytes 1769480 | tf_op jit(solution)/shard_map/ppermute | solution.py:765
  15.0 23.4 %collective-permute-start.2 = (bf16[2,4,56,128]{3,2,1,0:T(8,128)(2,1)}, bf16[2,4,56,128]{3,2,1,0:T(8,128)(2,1)S(1)}, u32[]{:S(2)}, u32[]{:S(2)}) collective-permute-start(bf16[2,4,56,128]{3,2,1,0:T(8,128)(2,1)} %get-tuple-element.40), channel_id=1, source_target_pairs={{0,127},{1,120},{2,121},{3,122},{4,123},{5,124},{6,125},{7,126},{8... | collective-permute-start | bytes 344072 | tf_op jit(solution)/shard_map/ppermute | solution.py:765
  38.4 0.6 copy-start.7
  38.4 0.9 copy-start.4
  38.4 1.1 copy-start
  56.2 17.6 %collective-permute-start.3 = (bf16[8,144,128]{2,1,0:T(8,128)(2,1)}, bf16[8,144,128]{2,1,0:T(8,128)(2,1)S(1)}, u32[]{:S(2)}, u32[]{:S(2)}) collective-permute-start(bf16[8,144,128]{2,1,0:T(8,128)(2,1)} %get-tuple-element.52), channel_id=1, source_target_pairs={{0,1},{1,2},{2,3},{3,4},{4,5},{5,6},{6,7},{7,0},{8,9},{9,10},{10,1... | collective-permute-start | bytes 884744 | tf_op jit(solution)/shard_map/ppermute | solution.py:765
  57.8 16.0 %collective-permute-start.4 = (bf16[4,56,128]{2,1,0:T(8,128)(2,1)}, bf16[4,56,128]{2,1,0:T(8,128)(2,1)S(1)}, u32[]{:S(2)}, u32[]{:S(2)}) collective-permute-start(bf16[4,56,128]{2,1,0:T(8,128)(2,1)} %get-tuple-element.53), channel_id=1, source_target_pairs={{0,9},{1,10},{2,11},{3,12},{4,13},{5,14},{6,15},{7,8},{8,17},{9,18... | collective-permute-start | bytes 172040 | tf_op jit(solution)/shard_map/ppermute | solution.py:765
  73.8 24.6 %copy-start.6 = (bf16[4,56,128]{2,1,0:T(8,128)(2,1)}, bf16[4,56,128]{2,1,0:T(8,128)(2,1)S(1)}, u32[]{:S(2)}) copy-start(bf16[4,56,128]{2,1,0:T(8,128)(2,1)S(1)} %collective-permute-done.4.gc) | copy-start | bytes 172036
  73.8 24.5 %copy-start.2 = (bf16[8,144,128]{2,1,0:T(8,128)(2,1)}, bf16[8,144,128]{2,1,0:T(8,128)(2,1)S(1)}, u32[]{:S(2)}) copy-start(bf16[8,144,128]{2,1,0:T(8,128)(2,1)S(1)} %collective-permute-done.3.gs) | copy-start | bytes 884740
  73.8 1.8 %collective-permute-start.5 = (bf16[1088,128]{1,0:T(8,128)(2,1)}, bf16[1088,128]{1,0:T(8,128)(2,1)S(1)}, u32[]{:S(2)}, u32[]{:S(2)}) collective-permute-start(bf16[1088,128]{1,0:T(8,128)(2,1)} %get-tuple-element.54), channel_id=1, source_target_pairs={{0,8},{8,0},{16,24},{24,16},{32,40},{40,32},{48,56},{56,48},{64,72... | collective-permute-start | bytes 835592 | tf_op jit(solution)/shard_map/ppermute | solution.py:770
  76.8 4.4 %collective-permute-start.6 = (bf16[272,128]{1,0:T(8,128)(2,1)S(1)}, bf16[272,128]{1,0:T(8,128)(2,1)S(1)}, u32[]{:S(2)}, u32[]{:S(2)}) collective-permute-start(bf16[272,128]{1,0:T(8,128)(2,1)S(1)} %get-tuple-element.75), channel_id=1, source_target_pairs={{0,16},{8,24},{16,0},{24,8},{32,48},{40,56},{48,32},{56,40},{64,80... | collective-permute-start | bytes 208904 | tf_op jit(solution)/shard_map/ppermute | solution.py:770
  76.9 5.6 %collective-permute-start.8 = (bf16[272,128]{1,0:T(8,128)(2,1)S(1)}, bf16[272,128]{1,0:T(8,128)(2,1)S(1)}, u32[]{:S(2)}, u32[]{:S(2)}) collective-permute-start(bf16[272,128]{1,0:T(8,128)(2,1)S(1)} %get-tuple-element.76), channel_id=1, source_target_pairs={{0,48},{8,56},{16,32},{24,40},{32,16},{40,24},{48,0},{56,8},{64,11... | collective-permute-start | bytes 208904 | tf_op jit(solution)/shard_map/ppermute | solution.py:770
  78.6 5.8 %collective-permute-start.7 = (bf16[272,128]{1,0:T(8,128)(2,1)S(1)}, bf16[272,128]{1,0:T(8,128)(2,1)S(1)}, u32[]{:S(2)}, u32[]{:S(2)}) collective-permute-start(bf16[272,128]{1,0:T(8,128)(2,1)S(1)} %get-tuple-element.77), channel_id=1, source_target_pairs={{0,32},{8,40},{16,48},{24,56},{32,0},{40,8},{48,16},{56,24},{64,96... | collective-permute-start | bytes 208904 | tf_op jit(solution)/shard_map/ppermute | solution.py:770
  81.0 12.5 %collective-permute-start.12 = (bf16[8,216,128]{2,1,0:T(8,128)(2,1)}, bf16[8,216,128]{2,1,0:T(8,128)(2,1)S(1)}, u32[]{:S(2)}, u32[]{:S(2)}) collective-permute-start(bf16[8,216,128]{2,1,0:T(8,128)(2,1)} %get-tuple-element.55), channel_id=1, source_target_pairs={{0,8},{8,16},{16,24},{24,32},{32,40},{40,48},{48,56},{56,64},{64,7... | collective-permute-start | bytes 1327112 | tf_op jit(solution)/shard_map/ppermute | solution.py:765
  84.5 5.6 %collective-permute-start.11 = (bf16[272,128]{1,0:T(8,128)(2,1)S(1)}, bf16[272,128]{1,0:T(8,128)(2,1)S(1)}, u32[]{:S(2)}, u32[]{:S(2)}) collective-permute-start(bf16[272,128]{1,0:T(8,128)(2,1)S(1)} %fusion.2), channel_id=1, source_target_pairs={{0,6},{1,7},{2,4},{3,5},{4,2},{5,3},{6,0},{7,1},{8,14},{9,15},{10,... | collective-permute-start | bytes 208904 | tf_op jit(solution)/shard_map/ppermute | solution.py:770
  87.6 5.8 %collective-permute-start.10 = (bf16[272,128]{1,0:T(8,128)(2,1)S(1)}, bf16[272,128]{1,0:T(8,128)(2,1)S(1)}, u32[]{:S(2)}, u32[]{:S(2)}) collective-permute-start(bf16[272,128]{1,0:T(8,128)(2,1)S(1)} %fusion.2), channel_id=1, source_target_pairs={{0,4},{1,5},{2,6},{3,7},{4,0},{5,1},{6,2},{7,3},{8,12},{9,13},{10,... | collective-permute-start | bytes 208904 | tf_op jit(solution)/shard_map/ppermute | solution.py:770
  87.6 5.8 %collective-permute-start.9 = (bf16[272,128]{1,0:T(8,128)(2,1)S(1)}, bf16[272,128]{1,0:T(8,128)(2,1)S(1)}, u32[]{:S(2)}, u32[]{:S(2)}) collective-permute-start(bf16[272,128]{1,0:T(8,128)(2,1)S(1)} %fusion.2), channel_id=1, source_target_pairs={{0,2},{1,3},{2,0},{3,1},{4,6},{5,7},{6,4},{7,5},{8,10},{9,11},{10,... | collective-permute-start | bytes 208904 | tf_op jit(solution)/shard_map/ppermute | solution.py:770
  93.5 4.8 %copy-start.1 = (bf16[8,216,128]{2,1,0:T(8,128)(2,1)}, bf16[8,216,128]{2,1,0:T(8,128)(2,1)S(1)}, u32[]{:S(2)}) copy-start(bf16[8,216,128]{2,1,0:T(8,128)(2,1)S(1)} %collective-permute-done.12.gl) | copy-start | bytes 1327108
  93.5 7.6 %collective-permute-start.15 = (bf16[272,128]{1,0:T(8,128)(2,1)S(1)}, bf16[272,128]{1,0:T(8,128)(2,1)S(1)}, u32[]{:S(2)}, u32[]{:S(2)}) collective-permute-start(bf16[272,128]{1,0:T(8,128)(2,1)S(1)} %convert_element_type.52), channel_id=1, source_target_pairs={{0,65},{1,64},{2,67},{3,66},{4,69},{5,68},{6,71},{7,70},{8,73},{9,... | collective-permute-start | bytes 208904 | tf_op jit(solution)/shard_map/ppermute | solution.py:821
  96.2 4.9 %collective-permute-start.14 = (bf16[272,128]{1,0:T(8,128)(2,1)S(1)}, bf16[272,128]{1,0:T(8,128)(2,1)S(1)}, u32[]{:S(2)}, u32[]{:S(2)}) collective-permute-start(bf16[272,128]{1,0:T(8,128)(2,1)S(1)} %convert_element_type.52), channel_id=1, source_target_pairs={{0,64},{8,72},{16,80},{24,88},{32,96},{40,104},{48,112},{56,120},{... | collective-permute-start | bytes 208904 | tf_op jit(solution)/shard_map/ppermute | solution.py:770
  96.4 5.8 %collective-permute-start.13 = (bf16[272,128]{1,0:T(8,128)(2,1)S(1)}, bf16[272,128]{1,0:T(8,128)(2,1)S(1)}, u32[]{:S(2)}, u32[]{:S(2)}) collective-permute-start(bf16[272,128]{1,0:T(8,128)(2,1)S(1)} %convert_element_type.52), channel_id=1, source_target_pairs={{0,1},{1,0},{2,3},{3,2},{4,5},{5,4},{6,7},{7,6},{8,9},{9,8},{10,11... | collective-permute-start | bytes 208904 | tf_op jit(solution)/shard_map/ppermute | solution.py:770
  102.2 6.9 %collective-permute-start.17 = (bf16[272,128]{1,0:T(8,128)(2,1)S(1)}, bf16[272,128]{1,0:T(8,128)(2,1)S(1)}, u32[]{:S(2)}, u32[]{:S(2)}) collective-permute-start(bf16[272,128]{1,0:T(8,128)(2,1)S(1)} %convert_add_fusion.1), channel_id=1, source_target_pairs={{0,32},{8,40},{16,48},{24,56},{32,0},{40,8},{48,16},{56,24},{64,96... | collective-permute-start | bytes 208904 | tf_op jit(solution)/shard_map/ppermute | solution.py:770
  105.4 4.3 %collective-permute-start.16 = (bf16[272,128]{1,0:T(8,128)(2,1)S(1)}, bf16[272,128]{1,0:T(8,128)(2,1)S(1)}, u32[]{:S(2)}, u32[]{:S(2)}) collective-permute-start(bf16[272,128]{1,0:T(8,128)(2,1)S(1)} %convert_add_fusion.1), channel_id=1, source_target_pairs={{0,16},{8,24},{16,0},{24,8},{32,48},{40,56},{48,32},{56,40},{64,80... | collective-permute-start | bytes 208904 | tf_op jit(solution)/shard_map/ppermute | solution.py:770
  105.4 5.5 %collective-permute-start.18 = (bf16[272,128]{1,0:T(8,128)(2,1)S(1)}, bf16[272,128]{1,0:T(8,128)(2,1)S(1)}, u32[]{:S(2)}, u32[]{:S(2)}) collective-permute-start(bf16[272,128]{1,0:T(8,128)(2,1)S(1)} %convert_add_fusion.1), channel_id=1, source_target_pairs={{0,48},{8,56},{16,32},{24,40},{32,16},{40,24},{48,0},{56,8},{64,11... | collective-permute-start | bytes 208904 | tf_op jit(solution)/shard_map/ppermute | solution.py:770
  111.1 1.7 %copy-start.3 = (bf16[4,272,128]{2,1,0:T(8,128)(2,1)}, bf16[4,272,128]{2,1,0:T(8,128)(2,1)S(1)}, u32[]{:S(2)}) copy-start(bf16[4,272,128]{2,1,0:T(8,128)(2,1)S(1)} %pad_maximum_fusion.1) | copy-start | bytes 835588
  111.1 1.6 %collective-permute-start.19 = (bf16[4,272,128]{2,1,0:T(8,128)(2,1)S(1)}, bf16[4,272,128]{2,1,0:T(8,128)(2,1)S(1)}, u32[]{:S(2)}, u32[]{:S(2)}) collective-permute-start(bf16[4,272,128]{2,1,0:T(8,128)(2,1)S(1)} %pad_maximum_fusion.1), channel_id=1, source_target_pairs={{0,8},{8,0},{16,24},{24,16},{32,40},{40,32},{48,56},{56,48},{64,72... | collective-permute-start | bytes 835592 | tf_op jit(solution)/shard_map/ppermute | solution.py:770
  112.7 0.7 copy-start.5
